TPU v7x, 32 devices: a whole 2x2x4 slice. The times are simulated.
32 devices in a mesh: dp: 8 (over y, x, core), tensor: 4 (over z).
Axes of the slice: x: 2, y: 2, z: 4, core: 2. Of those that a mesh axis runs over, the one named last changes fastest.
Arguments:
- tokens_in: bfloat16 [8192, 1024], P(('dp', 'tensor')), may hold values from -6 to 6
- out_grad: bfloat16 [8192, 1024], P(('dp', 'tensor')), may hold values from -6 to 6
- attn_gain: bfloat16 [1024], P('dp'), may hold values from 0.5 to 1.5
- w_query: bfloat16 [1024, 1024], P('dp', 'tensor'), may hold values from -0.1875 to 0.1875
- w_key: bfloat16 [1024, 1024], P('dp', 'tensor'), may hold values from -0.1875 to 0.1875
- w_value: bfloat16 [1024, 1024], P('dp', 'tensor'), may hold values from -0.1875 to 0.1875
- w_output: bfloat16 [1024, 1024], P('tensor', 'dp'), may hold values from -0.75 to 0.75
- rel_table: float32 [16, 32], P('tensor'), may hold values from -4 to 4
- moe_gain: bfloat16 [1024], P('dp'), may hold values from 0.5 to 1.5
- w_router: bfloat16 [1024, 4], P('dp'), may hold values from -0.125 to 0.125
- w_gate: bfloat16 [4, 1024, 2816], P(None, 'dp', 'tensor'), may hold values from -0.1875 to 0.1875
- w_up: bfloat16 [4, 1024, 2816], P(None, 'dp', 'tensor'), may hold values from -0.1875 to 0.1875
- down_weight: bfloat16 [4, 2816, 1024], P(None, 'tensor', 'dp'), may hold values from -0.3125 to 0.3125
- expert_ids: int32 [8192, 2], P('dp'), may hold values from 0 to 3, as said below
- piece_starts: int32 [8, 2], P('dp'), may hold values from 0 to 768, as said below
Outputs:
- out_rows: bfloat16 [8192, 1024], P(('dp', 'tensor'))
- in_grad: float32 [8192, 1024], P(('dp', 'tensor'))
- grad_attn_gain: float32 [1024], P(('dp', 'tensor'))
- grad_w_query: float32 [1024, 1024], P('dp', 'tensor')
- grad_w_key: float32 [1024, 1024], P('dp', 'tensor')
- grad_w_value: float32 [1024, 1024], P('dp', 'tensor')
- grad_w_output: float32 [1024, 1024], P('tensor', 'dp')
- grad_rel_table: float32 [16, 32], P('tensor')
- grad_moe_gain: float32 [1024], P(('dp', 'tensor'))
- grad_w_router: float32 [1024, 4], P(('dp', 'tensor'))
- gate_weight_gradient: float32 [4, 1024, 2816], P(None, 'dp', 'tensor')
- grad_w_up: float32 [4, 1024, 2816], P(None, 'dp', 'tensor')
- grad_w_down: float32 [4, 2816, 1024], P(None, 'tensor', 'dp')
Inputs may be any that keep to these rules, and one draw needn't show every extreme that they name: `expert_ids`: the two experts of a token differ. Within the tokens of each index of dp, one expert, which one drawn from the seed, is among the two choices of exactly 768 tokens. `piece_starts`: in each sequence the k-th of the 2 pieces lies wholly inside the k-th of 2 equal parts of the sequence; positions count from the sequence's start. Some sequence's first piece starts at position 0 and some sequence's last piece ends at the sequence's end.
All inputs are finite; a program needn't handle non-finite values.
Results may differ from a plain program's by a relative error of at most 0.02.
Values may be sent and summed in bfloat16 or wider, within the bound.
No kernel may reach another device: no remote copies, remote signals or barrier semaphores. Data moves between devices by JAX's collectives and lax.ppermute only.
A program may use at most 256 MiB of HBM per device.

v0:
```python
import jax
import jax.numpy as jnp
from jax import lax
from jax.sharding import PartitionSpec as P

EXPERTS = 4
SEQ_LEN = 1024
PIECE = 256
PIECES = 2
CAP = 640


EPSILON = 1e-06
PRECISE = lax.Precision.HIGHEST
LIMITS = (12, 16, 23, 32, 46, 64, 91)
MASKED = -1e30


def bucket_of(offsets):
    distance = jnp.abs(offsets)
    far_bucket = jnp.full_like(distance, 8)
    for bound_value in LIMITS:
        far_bucket = far_bucket + (distance >= bound_value).astype(jnp.int32)
    near_bucket = jnp.where(distance < 8, distance, far_bucket)
    return near_bucket + jnp.where(offsets > 0, 16, 0).astype(jnp.int32)


def piece_labels(starts_in, row_total):
    token_positions = jnp.arange(row_total, dtype=jnp.int32)
    seq_ids = token_positions // SEQ_LEN
    inner_pos = token_positions % SEQ_LEN
    own_starts = jnp.take(starts_in, seq_ids, axis=0)
    inside = (inner_pos[:, None] >= own_starts) & (inner_pos[:, None] < own_starts + PIECE)
    numbers = seq_ids[:, None] * PIECES + jnp.arange(PIECES, dtype=jnp.int32)[None, :]
    labels = jnp.max(jnp.where(inside, numbers, -1), axis=1)
    return (seq_ids, labels)


def block_mask(seq_ids, labels, first_row, block_rows):
    query_pos = first_row + jnp.arange(block_rows, dtype=jnp.int32)
    key_pos = jnp.arange(seq_ids.shape[0], dtype=jnp.int32)
    query_seq = lax.dynamic_slice_in_dim(seq_ids, first_row, block_rows)
    query_label = lax.dynamic_slice_in_dim(labels, first_row, block_rows)
    same_seq = query_seq[:, None] == seq_ids[None, :]
    causal = key_pos[None, :] <= query_pos[:, None]
    joint = (query_label[:, None] == labels[None, :]) & (query_label[:, None] >= 0)
    return same_seq & (causal | joint)


def route_slots(ids_in):
    row_total = ids_in.shape[0]
    expert_range = jnp.arange(EXPERTS, dtype=jnp.int32)
    first_hot = (ids_in[:, 0:1] == expert_range[None, :]).astype(jnp.int32)
    second_hot = (ids_in[:, 1:2] == expert_range[None, :]).astype(jnp.int32)
    first_run = jnp.cumsum(first_hot, axis=0)
    second_run = jnp.cumsum(second_hot, axis=0) + first_run[-1][None, :]
    first_place = jnp.sum(first_run * first_hot, axis=1) - 1
    second_place = jnp.sum(second_run * second_hot, axis=1) - 1
    dump_slot = EXPERTS * CAP
    first_slot = jnp.where(first_place < CAP, ids_in[:, 0] * CAP + first_place, dump_slot)
    second_slot = jnp.where(second_place < CAP, ids_in[:, 1] * CAP + second_place, dump_slot)
    row_ids = jnp.arange(row_total, dtype=jnp.int32)
    slot_owner = (
        jnp.full((dump_slot + 1,), row_total, jnp.int32)
        .at[first_slot]
        .set(row_ids)
        .at[second_slot]
        .set(row_ids)
    )
    return (first_slot, second_slot, slot_owner[:dump_slot])


def rms_scale(values, gain_vec):
    return (
        values * lax.rsqrt(jnp.mean(values * values, axis=-1, keepdims=True) + EPSILON) * gain_vec
    )


def geglu_unit(gate_pre, up_pre):
    return jax.nn.gelu(gate_pre, approximate=True) * up_pre


def softmax_rows(logits):
    row_max = jnp.max(logits, axis=-1, keepdims=True)
    exponent = jnp.exp(logits - row_max)
    return exponent / jnp.sum(exponent, axis=-1, keepdims=True)


def skew_rows(window, row_count, key_count):
    head_count = window.shape[0]
    width_full = row_count + key_count
    padded = jnp.concatenate([window, jnp.zeros((head_count, 1), window.dtype)], 1)
    spread = jnp.broadcast_to(padded[:, None, :], (head_count, row_count, width_full)).reshape(
        head_count, row_count * width_full
    )
    cut = spread[:, row_count - 1 : row_count - 1 + row_count * (width_full - 1)]
    return cut.reshape(head_count, row_count, width_full - 1)[:, :, :key_count]


def unskew_rows(matrix, row_count, key_count):
    head_count = matrix.shape[0]
    width_full = row_count + key_count
    widened = jnp.concatenate(
        [matrix, jnp.zeros((head_count, row_count, width_full - 1 - key_count), matrix.dtype)], 2
    )
    flat = widened.reshape(head_count, row_count * (width_full - 1))
    flat = jnp.concatenate(
        [
            jnp.zeros((head_count, row_count - 1), matrix.dtype),
            flat,
            jnp.zeros((head_count, 1), matrix.dtype),
        ],
        1,
    )
    return jnp.sum(flat.reshape(head_count, row_count, width_full), axis=1)[:, : width_full - 1]


def on_device(
    tokens_in,
    out_grad,
    attn_gain,
    w_query,
    w_key,
    w_value,
    w_output,
    rel_table,
    moe_gain,
    w_router,
    w_gate,
    w_up,
    down_weight,
    expert_ids,
    piece_starts,
):

    def fetch_dense():
        return (
            lax.all_gather(attn_gain, "dp", axis=0, tiled=True),
            lax.all_gather(moe_gain, "dp", axis=0, tiled=True),
            lax.all_gather(w_router, "dp", axis=0, tiled=True),
            lax.all_gather(w_query, "dp", axis=0, tiled=True),
            lax.all_gather(w_key, "dp", axis=0, tiled=True),
            lax.all_gather(w_value, "dp", axis=0, tiled=True),
            lax.all_gather(w_output, "dp", axis=1, tiled=True),
        )

    def fetch_experts():
        return (
            lax.all_gather(w_gate, "dp", axis=1, tiled=True),
            lax.all_gather(w_up, "dp", axis=1, tiled=True),
            lax.all_gather(down_weight, "dp", axis=2, tiled=True),
        )

    tok_rows = tokens_in.shape[0]
    model_width = tokens_in.shape[1]
    group_rows = expert_ids.shape[0]
    head_count = rel_table.shape[0]
    bucket_count = rel_table.shape[1]
    tensor_size = lax.axis_size("tensor")
    dp_size = lax.axis_size("dp")
    tensor_index = lax.axis_index("tensor")
    own_first = tensor_index * tok_rows
    block_rows = min(512, group_rows)
    block_total = group_rows // block_rows
    block_ids = jnp.arange(block_total, dtype=jnp.int32)
    dump_slot = EXPERTS * CAP
    seq_ids, labels = piece_labels(piece_starts, group_rows)
    bucket_range = jnp.arange(bucket_count, dtype=jnp.int32)
    all_offsets = jnp.arange(2 * group_rows - 1, dtype=jnp.int32) - (group_rows - 1)
    offset_onehot = (bucket_of(all_offsets)[:, None] == bucket_range[None, :]).astype(jnp.float32)
    bias_line = jnp.dot(rel_table, offset_onehot.T, precision=PRECISE)
    window_len = block_rows + group_rows - 1

    def own_part(values):
        return lax.dynamic_slice_in_dim(values, own_first, tok_rows, 0)

    rows_in, grad_all = (
        lax.all_gather(tokens_in, "tensor", axis=0, tiled=True),
        lax.all_gather(out_grad, "tensor", axis=0, tiled=True),
    )
    resid_full = rows_in.astype(jnp.float32)
    gain_one, gain_two, router_w, query_w, key_w, value_w, output_w = fetch_dense()
    normed_one = rms_scale(resid_full, gain_one.astype(jnp.float32)).astype(jnp.bfloat16)
    queries = (
        jnp.dot(normed_one, query_w, preferred_element_type=jnp.float32)
        .astype(jnp.bfloat16)
        .reshape(group_rows, head_count, -1)
    )
    keys_all = (
        jnp.dot(normed_one, key_w, preferred_element_type=jnp.float32)
        .astype(jnp.bfloat16)
        .reshape(group_rows, head_count, -1)
    )
    values_all = (
        jnp.dot(normed_one, value_w, preferred_element_type=jnp.float32)
        .astype(jnp.bfloat16)
        .reshape(group_rows, head_count, -1)
    )

    def window_start(first_row):
        return group_rows - first_row - block_rows

    def block_scores(block_index):
        first_row = block_index * block_rows
        visible = block_mask(seq_ids, labels, first_row, block_rows)
        window = lax.dynamic_slice_in_dim(bias_line, window_start(first_row), window_len, 1)
        query_rows = lax.dynamic_slice_in_dim(queries, first_row, block_rows, 0)
        raw_scores = (
            jnp.einsum("qhd,khd->hqk", query_rows, keys_all, preferred_element_type=jnp.float32)
            * 0.125
        )
        raw_scores = raw_scores + skew_rows(window, block_rows, group_rows)
        return (jnp.where(visible[None], raw_scores, MASKED), first_row, query_rows)

    def forward_block(block_index):
        scores, first_row, query_rows = block_scores(block_index)
        row_max = jnp.max(scores, axis=2, keepdims=True)
        exponent = jnp.exp(scores - row_max)
        row_sum = jnp.sum(exponent, axis=2, keepdims=True)
        chances = (exponent / row_sum).astype(jnp.bfloat16)
        mixed_rows = jnp.einsum(
            "hqk,khd->qhd", chances, values_all, preferred_element_type=jnp.float32
        )
        return (mixed_rows, row_max + jnp.log(row_sum))

    blended_blocks, log_sums = lax.map(forward_block, block_ids)
    attended = blended_blocks.reshape(group_rows, -1).astype(jnp.bfloat16)
    attn_part = jnp.dot(attended, output_w, preferred_element_type=jnp.float32)
    resid_mid = resid_full + lax.psum(attn_part.astype(jnp.bfloat16), "tensor").astype(jnp.float32)
    gain_two_wide = gain_two.astype(jnp.float32)
    normed_two = rms_scale(resid_mid, gain_two_wide).astype(jnp.bfloat16)
    route_probs = softmax_rows(jnp.dot(normed_two, router_w, preferred_element_type=jnp.float32))
    gate_vals = jnp.take_along_axis(route_probs, expert_ids, axis=1)
    first_slot, second_slot, slot_owner = route_slots(expert_ids)
    zero_full = jnp.zeros((1, model_width), jnp.float32)
    dispatch = (slot_owner[:, None] == jnp.arange(group_rows, dtype=jnp.int32)[None, :]).astype(
        jnp.bfloat16
    )
    routed = (
        jnp.dot(dispatch, normed_two, preferred_element_type=jnp.float32)
        .astype(jnp.bfloat16)
        .reshape(EXPERTS, CAP, model_width)
    )
    gate_w, up_w, down_w = fetch_experts()
    gate_pre = jnp.einsum("ecd,edf->ecf", routed, gate_w, preferred_element_type=jnp.float32)
    up_pre = jnp.einsum("ecd,edf->ecf", routed, up_w, preferred_element_type=jnp.float32)
    hidden = geglu_unit(gate_pre, up_pre).astype(jnp.bfloat16)
    expert_out = jnp.einsum(
        "ecf,efd->ecd", hidden, down_w, preferred_element_type=jnp.float32
    ).reshape(dump_slot, model_width)
    out_pad = jnp.concatenate([expert_out, zero_full], 0)
    resid_out = own_part(resid_mid) + lax.psum_scatter(
        (gate_vals[:, 0:1] * out_pad[first_slot] + gate_vals[:, 1:2] * out_pad[second_slot]).astype(
            jnp.bfloat16
        ),
        "tensor",
        scatter_dimension=0,
        tiled=True,
    ).astype(jnp.float32)
    out_rows = resid_out.astype(jnp.bfloat16)
    slot_gates = (
        jnp.zeros((dump_slot + 1,), jnp.float32)
        .at[first_slot]
        .set(gate_vals[:, 0])
        .at[second_slot]
        .set(gate_vals[:, 1])[:dump_slot]
    )
    slot_grad = (
        slot_gates[:, None] * jnp.dot(dispatch, grad_all, preferred_element_type=jnp.float32)
    ).astype(jnp.bfloat16)
    grad_wide = grad_all.astype(jnp.float32)
    gate_grad_a = jnp.sum(grad_wide * out_pad[first_slot], axis=1)
    gate_grad_b = jnp.sum(grad_wide * out_pad[second_slot], axis=1)
    expert_range = jnp.arange(EXPERTS, dtype=jnp.int32)
    prob_grad = (expert_ids[:, 0:1] == expert_range[None, :]) * gate_grad_a[:, None] + (
        expert_ids[:, 1:2] == expert_range[None, :]
    ) * gate_grad_b[:, None]
    logit_grad = route_probs * (prob_grad - jnp.sum(route_probs * prob_grad, axis=1, keepdims=True))
    gate_w, up_w, down_w = fetch_experts()
    slot_block = slot_grad.reshape(EXPERTS, CAP, model_width)
    hidden_grad = jnp.einsum("ecd,efd->ecf", slot_block, down_w, preferred_element_type=jnp.float32)
    unused_value, geglu_pull = jax.vjp(geglu_unit, gate_pre, up_pre)
    gate_gradient, up_grad = geglu_pull(hidden_grad)
    gate_gradient = gate_gradient.astype(jnp.bfloat16)
    up_grad = up_grad.astype(jnp.bfloat16)
    grad_down = jnp.einsum("ecf,ecd->efd", hidden, slot_block, preferred_element_type=jnp.float32)
    grad_gate = jnp.einsum(
        "ecd,ecf->edf", routed, gate_gradient, preferred_element_type=jnp.float32
    )
    grad_up = jnp.einsum("ecd,ecf->edf", routed, up_grad, preferred_element_type=jnp.float32)
    routed_grad = jnp.einsum(
        "ecf,edf->ecd", gate_gradient, gate_w, preferred_element_type=jnp.float32
    ) + jnp.einsum("ecf,edf->ecd", up_grad, up_w, preferred_element_type=jnp.float32)
    routed_flat = routed_grad.reshape(dump_slot, model_width)
    grad_gate_out, grad_up_out, grad_down_out = (
        lax.psum_scatter(grad_gate, "dp", scatter_dimension=1, tiled=True),
        lax.psum_scatter(grad_up, "dp", scatter_dimension=1, tiled=True),
        lax.psum_scatter(grad_down, "dp", scatter_dimension=2, tiled=True),
    )
    routed_pad = jnp.concatenate([routed_flat, zero_full], 0)
    router_wide = router_w.astype(jnp.float32)
    norm_two_part = (
        routed_pad[first_slot]
        + routed_pad[second_slot]
        + jnp.dot(logit_grad, router_wide.T, precision=PRECISE)
    )
    router_part = jnp.dot(normed_two.astype(jnp.float32).T, logit_grad, precision=PRECISE)
    local_two = lax.psum(norm_two_part.astype(jnp.bfloat16), "tensor").astype(jnp.float32)

    def norm_two_of(values):
        return rms_scale(values, gain_two_wide)

    unused_value, second_pull = jax.vjp(norm_two_of, resid_mid)
    mid_part = second_pull(local_two)[0]
    own_mid = own_part(resid_mid)
    own_scale = lax.rsqrt(jnp.mean(own_mid * own_mid, axis=-1, keepdims=True) + EPSILON)
    gain_two_part = jnp.sum(own_part(local_two) * own_mid * own_scale, axis=0)
    resid_grad = grad_wide + mid_part
    attn_grad = resid_grad.astype(jnp.bfloat16)
    gain_one, gain_two, router_w, query_w, key_w, value_w, output_w = fetch_dense()
    output_gradient = jnp.einsum(
        "gh,gd->hd", attended, attn_grad, preferred_element_type=jnp.float32
    )
    mixed_grad = (
        jnp.einsum("gd,hd->gh", attn_grad, output_w, preferred_element_type=jnp.float32)
        .astype(jnp.bfloat16)
        .reshape(group_rows, head_count, -1)
    )
    window_ids = jnp.arange(window_len, dtype=jnp.int32)

    def backward_block(carried, block_index):
        key_acc, value_acc, table_acc = carried
        scores, first_row, query_rows = block_scores(block_index)
        chances = jnp.exp(scores - log_sums[block_index])
        grad_rows = lax.dynamic_slice_in_dim(mixed_grad, first_row, block_rows, 0)
        chance_grad = jnp.einsum(
            "qhd,khd->hqk", grad_rows, values_all, preferred_element_type=jnp.float32
        )
        inner_sum = jnp.sum(chances * chance_grad, axis=2, keepdims=True)
        score_gradient = (chances * (chance_grad - inner_sum)).astype(jnp.bfloat16)
        query_grad = (
            jnp.einsum("hqk,khd->qhd", score_gradient, keys_all, preferred_element_type=jnp.float32)
            * 0.125
        )
        key_acc = (
            key_acc
            + jnp.einsum(
                "hqk,qhd->khd", score_gradient, query_rows, preferred_element_type=jnp.float32
            )
            * 0.125
        )
        value_acc = value_acc + jnp.einsum(
            "hqk,qhd->khd",
            chances.astype(jnp.bfloat16),
            grad_rows,
            preferred_element_type=jnp.float32,
        )
        diagonal_sums = unskew_rows(score_gradient.astype(jnp.float32), block_rows, group_rows)
        window_offsets = window_ids + window_start(first_row) - (group_rows - 1)
        window_onehot = (bucket_of(window_offsets)[:, None] == bucket_range[None, :]).astype(
            jnp.float32
        )
        table_acc = table_acc + jnp.dot(diagonal_sums, window_onehot, precision=PRECISE)
        return ((key_acc, value_acc, table_acc), query_grad)

    start_acc = (
        jnp.zeros(keys_all.shape, jnp.float32),
        jnp.zeros(values_all.shape, jnp.float32),
        jnp.zeros(rel_table.shape, jnp.float32),
    )
    (key_acc, value_acc, table_acc), query_blocks = lax.scan(backward_block, start_acc, block_ids)
    query_grad = query_blocks.reshape(group_rows, -1).astype(jnp.bfloat16)
    key_grad = key_acc.reshape(group_rows, -1).astype(jnp.bfloat16)
    value_grad = value_acc.reshape(group_rows, -1).astype(jnp.bfloat16)
    grad_query = jnp.einsum("gd,gh->dh", normed_one, query_grad, preferred_element_type=jnp.float32)
    grad_key = jnp.einsum("gd,gh->dh", normed_one, key_grad, preferred_element_type=jnp.float32)
    grad_value = jnp.einsum("gd,gh->dh", normed_one, value_grad, preferred_element_type=jnp.float32)
    summed_rows = jnp.einsum("gh,dh->gd", query_grad, query_w, preferred_element_type=jnp.float32)
    summed_rows = summed_rows + jnp.einsum(
        "gh,dh->gd", key_grad, key_w, preferred_element_type=jnp.float32
    )
    norm_one_grad = lax.psum_scatter(
        (
            summed_rows
            + jnp.einsum("gh,dh->gd", value_grad, value_w, preferred_element_type=jnp.float32)
        ).astype(jnp.bfloat16),
        "tensor",
        scatter_dimension=0,
        tiled=True,
    ).astype(jnp.float32)
    unused_value, first_pull = jax.vjp(
        rms_scale, tokens_in.astype(jnp.float32), gain_one.astype(jnp.float32)
    )
    in_part, gain_one_part = first_pull(norm_one_grad)
    in_grad = own_part(resid_grad) + in_part
    attn_totals = (
        lax.psum_scatter(grad_query, "dp", scatter_dimension=0, tiled=True),
        lax.psum_scatter(grad_key, "dp", scatter_dimension=0, tiled=True),
        lax.psum_scatter(grad_value, "dp", scatter_dimension=0, tiled=True),
        lax.psum_scatter(output_gradient, "dp", scatter_dimension=1, tiled=True),
    )
    table_full = lax.dynamic_update_slice_in_dim(
        jnp.zeros((head_count * tensor_size, bucket_count), jnp.float32),
        table_acc,
        tensor_index * head_count,
        0,
    )
    small_totals = lax.psum(
        (gain_one_part, gain_two_part, router_part, table_full), ("dp", "tensor")
    )
    flat_index = lax.axis_index("dp") * tensor_size + tensor_index
    share = model_width // (dp_size * tensor_size)
    grad_gain_one = lax.dynamic_slice_in_dim(small_totals[0], flat_index * share, share, 0)
    grad_gain_two = lax.dynamic_slice_in_dim(small_totals[1], flat_index * share, share, 0)
    grad_router = lax.dynamic_slice_in_dim(small_totals[2], flat_index * share, share, 0)
    grad_table = lax.dynamic_slice_in_dim(small_totals[3], tensor_index * head_count, head_count, 0)
    return (
        out_rows,
        in_grad,
        grad_gain_one,
        attn_totals[0],
        attn_totals[1],
        attn_totals[2],
        attn_totals[3],
        grad_table,
        grad_gain_two,
        grad_router,
        grad_gate_out,
        grad_up_out,
        grad_down_out,
    )


def solution(mesh):
    placed = (
        P(("dp", "tensor"), None),
        P(("dp", "tensor"), None),
        P("dp"),
        P("dp", "tensor"),
        P("dp", "tensor"),
        P("dp", "tensor"),
        P("tensor", "dp"),
        P("tensor", None),
        P("dp"),
        P("dp", None),
        P(None, "dp", "tensor"),
        P(None, "dp", "tensor"),
        P(None, "tensor", "dp"),
        P("dp", None),
        P("dp", None),
    )
    return jax.shard_map(
        on_device,
        mesh=mesh,
        in_specs=placed,
        out_specs=(
            P(("dp", "tensor"), None),
            P(("dp", "tensor"), None),
            P(("dp", "tensor")),
            P("dp", "tensor"),
            P("dp", "tensor"),
            P("dp", "tensor"),
            P("tensor", "dp"),
            P("tensor", None),
            P(("dp", "tensor")),
            P(("dp", "tensor"), None),
            P(None, "dp", "tensor"),
            P(None, "dp", "tensor"),
            P(None, "tensor", "dp"),
        ),
        check_vma=False,
    )
```

profile of v0, /device:TPU:14, one launch (start us, length us, event | category | flops | bytes accessed | tf_op | source)
XLA Modules:
  0.0 1546.1 jit_solution(7688429661529637202)
XLA Ops:
  8.8 7.8 all-gather
  17.4 9.8 all_gather.46
  27.2 9.2 all_gather.47
  36.4 9.5 all_gather.48
  45.9 10.9 all_gather.49
  64.3 150.9 %while.39 = (s32[]{:T(128)}, bf16[2,512,4,64]{1,3,2,0:T(8,128)(2,1)S(1)}, f32[2,4,512,1]{2,1,3,0:T(4,128)S(1)}, s32[2]{0:T(128)S(1)}, s32[1024]{0:T(1024)S(1)}, ...) while((s32[]{:T(128)}, ...), condition=%wide.region_5.6_spmd.clone, body=%wide.region_2.5_spmd.clone.sunk | while | flops 558889984 | bytes 149849328 | solution.py:226
  68.6 19.9 %copy.76 = f32[1,4,512,1536]{3,1,2,0:T(4,128)S(1)} copy(f32[1,4,512,1536]{3,2,1,0:T(8,128)S(1)} %broadcast_bitcast_fusion.4) | data formatting | bytes 25165824 | tf_op jit(solution)/shard_map/while
  88.5 8.7 slice.149
  97.2 14.1 reshape.725
  111.3 19.6 %reshape.726 = f32[4,512,1535]{2,1,0:T(8,128)} reshape(f32[3143680]{0:T(1024)} %reshape.725) | data formatting | bytes 25149440 | tf_op jit(solution)/shard_map/while/body/eval_jaxpr/reshape | solution.py:97
  143.8 19.9 %copy.76 = f32[1,4,512,1536]{3,1,2,0:T(4,128)S(1)} copy(f32[1,4,512,1536]{3,2,1,0:T(8,128)S(1)} %broadcast_bitcast_fusion.4) | data formatting | bytes 25165824 | tf_op jit(solution)/shard_map/while
  163.6 8.7 slice.149
  172.3 14.1 reshape.725
  186.4 19.6 %reshape.726 = f32[4,512,1535]{2,1,0:T(8,128)} reshape(f32[3143680]{0:T(1024)} %reshape.725) | data formatting | bytes 25149440 | tf_op jit(solution)/shard_map/while/body/eval_jaxpr/reshape | solution.py:97
  220.7 8.1 all-gather.1
  228.8 8.6 all_gather.51
  250.3 54.1 %all-reduce.9.cloned.1.call-done = bf16[1024,1024]{1,0:T(8,128)(2,1)} async-done(((bf16[1024,1024]{1,0:T(8,128)(2,1)}), bf16[1024,1024]{1,0:T(8,128)(2,1)}) %all-reduce.9.cloned.1.call-update) | async-done | bytes 2097168 | tf_op jit(solution)/shard_map/psum | solution.py:229
  309.0 7.8 fusion.61
  316.8 11.9 fusion.115
  328.7 12.4 multiply_convert_fusion.3
  341.1 16.1 %all-gather.14.cloned.1.call-done = bf16[4,704,1024]{2,1,0:T(8,128)(2,1)} async-done(((bf16[4,704,128]{2,1,0:T(8,128)(2,1)}), bf16[4,704,1024]{2,1,0:T(8,128)(2,1)}) %all-gather.14.cloned.1.call-update) | async-done | bytes 5767184 | tf_op jit(solution)/shard_map/all_gather | solution.py:151
  357.3 7.6 fusion.116
  370.1 10.4 gather_fusion.1
  380.5 10.5 gather_fusion
  390.9 13.2 all-gather.16.cloned.1.call-done
  409.9 17.6 %gather_fusion.4 = f32[2048]{0:T(1024)S(1)} fusion(f32[1024,4]{0,1:T(4,128)S(1)} %get-tuple-element.710, s32[2048]{0:T(1024)S(1)} %reshape.650), kind=kCustom, calls=%fused_computation.4 | custom fusion | bytes 32768 | tf_op jit(solution)/shard_map/jit(take_along_axis)/gather | solution.py:233
  437.0 8.1 multiply_convert_fusion.1
  445.2 16.5 %multiply_convert_fusion.2 = (bf16[4,640,704]{1,2,0:T(8,128)(2,1)}, bf16[4,640,704]{1,2,0:T(8,128)(2,1)}) fusion(f32[4,640,704]{1,2,0:T(8,128)} %fusion.115, f32[4,640,704]{1,2,0:T(8,128)} %get-tuple-element.728, bf16[4,640,1024]{2,1,0:T(8,128)(2,1)} %bitcast.268, bf16[4,704,1024]{2,1,0:T(8,128)(2,1)} %all-gather.14.cloned.1.call-done), kind=kOutput, calls=%fused_computation.94 | convolution fusion | flops 3734241280 | bytes 32636928 | tf_op jit(solution)/shard_map/ecd,efd->ecf/dot_general | solution.py:281
  461.7 12.1 fusion.117
  473.7 11.3 convolution_add_fusion.1
  490.2 10.4 gather_fusion.3
  500.7 10.7 gather_fusion.2
  511.4 6.8 add_convert_fusion.1
  523.9 79.7 %all-reduce.11.cloned.1.call-done = bf16[1024,1024]{1,0:T(8,128)(2,1)} async-done(((bf16[1024,1024]{1,0:T(8,128)(2,1)}), bf16[1024,1024]{1,0:T(8,128)(2,1)}) %all-reduce.11.cloned.1.call-update) | async-done | bytes 2097168 | tf_op jit(solution)/shard_map/psum | solution.py:308
  617.1 440.6 %while.40 = (s32[]{:T(128)}, f32[1024,4,64]{0,2,1:T(8,128)S(1)}, f32[1024,4,64]{0,2,1:T(8,128)S(1)}, f32[4,32]{1,0:T(4,128)S(1)}, bf16[2,512,4,64]{1,3,2,0:T(8,1...) while((s32[]{:T(128)}, f32[1024,4,64]{0,2,1:T(8,128)S(1)}, ...), condition=%wide.region_29.30_spmd.clone.clone, body=%wide.region_26.29_spmd.clone.clone.sunk | while | flops 1376470272 | bytes 302160288 | solution.py:371
  650.3 19.9 %copy.78 = f32[1,4,512,1536]{3,1,2,0:T(4,128)S(1)} copy(f32[1,4,512,1536]{3,2,1,0:T(8,128)S(1)} %broadcast_bitcast_fusion.5) | data formatting | bytes 25165824 | tf_op jit(solution)/shard_map/while
  670.2 8.7 slice.151
  678.9 14.1 reshape.728
  693.0 19.6 %reshape.729 = f32[4,512,1535]{2,1,0:T(8,128)} reshape(f32[3143680]{0:T(1024)} %reshape.728) | data formatting | bytes 25149440 | tf_op jit(solution)/shard_map/while/body/eval_jaxpr/reshape | solution.py:97
  712.5 7.7 multiply_reduce_fusion.7
  728.6 6.0 pad_convert_fusion.2
  734.7 19.0 %reshape.730 = f32[3143680]{0:T(1024)} reshape(f32[4,512,1535]{2,1,0:T(8,128)} %pad_convert_fusion.2) | data formatting | bytes 25149440 | tf_op jit(solution)/shard_map/while
  753.7 14.9 reshape.731
  770.0 64.9 %dynamic-update-slice.7 = f32[4,786432]{1,0:T(4,128)} dynamic-update-slice(f32[4,786432]{1,0:T(4,128)} %dynamic-update-slice.6, f32[4,785920]{1,0:T(4,128)} %reshape.731, s32[]{} %constant.605..sunk, s32[]{} %constant.606..sunk) | dynamic-update-slice | bytes 25149444 | tf_op jit(solution)/shard_map/while
  836.2 7.9 bitcast_reduce_fusion.2
  856.4 19.9 %copy.78 = f32[1,4,512,1536]{3,1,2,0:T(4,128)S(1)} copy(f32[1,4,512,1536]{3,2,1,0:T(8,128)S(1)} %broadcast_bitcast_fusion.5) | data formatting | bytes 25165824 | tf_op jit(solution)/shard_map/while
  876.3 8.7 slice.151
  885.0 14.1 reshape.728
  899.1 19.6 %reshape.729 = f32[4,512,1535]{2,1,0:T(8,128)} reshape(f32[3143680]{0:T(1024)} %reshape.728) | data formatting | bytes 25149440 | tf_op jit(solution)/shard_map/while/body/eval_jaxpr/reshape | solution.py:97
  918.6 7.7 multiply_reduce_fusion.7
  940.9 19.0 %reshape.730 = f32[3143680]{0:T(1024)} reshape(f32[4,512,1535]{2,1,0:T(8,128)} %pad_convert_fusion.2) | data formatting | bytes 25149440 | tf_op jit(solution)/shard_map/while
  959.9 14.9 reshape.731
  976.2 64.9 %dynamic-update-slice.7 = f32[4,786432]{1,0:T(4,128)} dynamic-update-slice(f32[4,786432]{1,0:T(4,128)} %dynamic-update-slice.6, f32[4,785920]{1,0:T(4,128)} %reshape.731, s32[]{} %constant.605..sunk, s32[]{} %constant.606..sunk) | dynamic-update-slice | bytes 25149444 | tf_op jit(solution)/shard_map/while
  1042.4 7.9 bitcast_reduce_fusion.2
  1073.6 12.6 fusion.123
  1086.4 12.5 fusion.125
  1099.0 12.5 fusion.124
  1123.5 40.8 %all-reduce.5 = (f32[1024]{0:T(1024)S(1)}, f32[16,32]{1,0:T(8,128)S(1)}, f32[1024]{0:T(1024)S(1)}, f32[1024,4]{0,1:T(4,128)S(1)}) all-reduce(f32[1024]{0:T(1024)S(1)} %get-tuple-element.651, f32[16,32]{1,0:T(8,128)S(1)} %constant_dynamic-update-slice_fusion, ...), channel_id=1, replica_groups=mesh['dp'=8,'tensor'=4] {'dp','tensor'}, use_global_device_ids=true, to_apply=%region_34.35 | all-reduce | flops 6656 | bytes 53248 | tf_op jit(solution)/shard_map/psum | solution.py:408
  1169.4 16.9 %reduce-scatter.18.cloned.1.call-done = f32[128,256]{1,0:T(8,128)} async-done(((f32[1024,256]{1,0:T(8,128)}), f32[128,256]{1,0:T(8,128)}) %reduce-scatter.18.cloned.1.call-update) | async-done | bytes 131088 | tf_op jit(solution)/shard_map/reduce_scatter | solution.py:399
  1186.3 39.8 %reduce-scatter.14.cloned.1.call-done = f32[128,256]{1,0:T(8,128)} async-done(((f32[1024,256]{1,0:T(8,128)}), f32[128,256]{1,0:T(8,128)}) %reduce-scatter.14.cloned.1.call-update) | async-done | bytes 131088 | tf_op jit(solution)/shard_map/reduce_scatter | solution.py:397
  1226.0 39.8 %reduce-scatter.16.cloned.1.call-done = f32[128,256]{1,0:T(8,128)} async-done(((f32[1024,256]{1,0:T(8,128)}), f32[128,256]{1,0:T(8,128)}) %reduce-scatter.16.cloned.1.call-update) | async-done | bytes 131088 | tf_op jit(solution)/shard_map/reduce_scatter | solution.py:398
  1265.9 90.7 %reduce-scatter.26.cloned.1.call-done = f32[4,704,128]{2,1,0:T(8,128)} async-done(((f32[4,704,1024]{2,1,0:T(8,128)}), f32[4,704,128]{2,1,0:T(8,128)}) %reduce-scatter.26.cloned.1.call-update) | async-done | bytes 1441808 | tf_op jit(solution)/shard_map/reduce_scatter | solution.py:298
  1356.6 90.9 %reduce-scatter.24.cloned.1.call-done = f32[4,128,704]{1,2,0:T(8,128)} async-done(((f32[4,1024,704]{1,2,0:T(8,128)}), f32[4,128,704]{1,2,0:T(8,128)}) %reduce-scatter.24.cloned.1.call-update) | async-done | bytes 1441808 | tf_op jit(solution)/shard_map/reduce_scatter | solution.py:297
  1447.5 90.8 %reduce-scatter.22.cloned.1.call-done = f32[4,128,704]{1,2,0:T(8,128)} async-done(((f32[4,1024,704]{1,2,0:T(8,128)}), f32[4,128,704]{1,2,0:T(8,128)}) %reduce-scatter.22.cloned.1.call-update) | async-done | bytes 1441808 | tf_op jit(solution)/shard_map/reduce_scatter | solution.py:296
  (374 shorter events, 180.9 us)
Async XLA Ops:
  8.0 48.8 %copy-start = (f32[4,32]{1,0:T(4,128)S(1)}, f32[4,32]{1,0:T(4,128)}, u32[]{:S(2)}) copy-start(f32[4,32]{1,0:T(4,128)} %param.26) | copy-start | bytes 1540
  8.0 49.5 %all-gather.8.cloned.1.call-start = ((), (), s32[]{:S(2)}) async-start(), calls=%async_computation.9 | async-start | bytes 2621440 | tf_op jit(solution)/shard_map/all_gather | solution.py:178
  8.8 295.6 %all-reduce.9.cloned.1.call-start = ((), (), s32[]{:S(2)}) async-start(), calls=%async_computation.10 | async-start | bytes 4194304 | tf_op jit(solution)/shard_map/psum | solution.py:229
  16.6 45.2 %copy-start.68 = (f32[8,1,128]{2,1,0:T(1,128)}, f32[8,1,128]{2,1,0:T(1,128)S(1)}, u32[]{:S(2)}) copy-start(f32[8,1,128]{2,1,0:T(1,128)S(1)} %convert_element_type.347) | copy-start | bytes 12292
  27.2 36.2 %copy-start.38 = (bf16[1024,256]{1,0:T(8,128)(2,1)}, bf16[1024,256]{1,0:T(8,128)(2,1)S(1)}, u32[]{:S(2)}) copy-start(bf16[1024,256]{1,0:T(8,128)(2,1)S(1)} %all_gather.46) | copy-start | bytes 1572868
  36.4 26.2 %copy-start.36 = (bf16[1024,256]{1,0:T(8,128)(2,1)}, bf16[1024,256]{1,0:T(8,128)(2,1)S(1)}, u32[]{:S(2)}) copy-start(bf16[1024,256]{1,0:T(8,128)(2,1)S(1)} %all_gather.47) | copy-start | bytes 1572868
  45.9 15.9 %copy-start.34 = (bf16[1024,256]{1,0:T(8,128)(2,1)}, bf16[1024,256]{1,0:T(8,128)(2,1)S(1)}, u32[]{:S(2)}) copy-start(bf16[1024,256]{1,0:T(8,128)(2,1)S(1)} %all_gather.48) | copy-start | bytes 1572868
  64.3 151.6 %copy-start.30 = (bf16[256,1024]{1,0:T(8,128)(2,1)S(1)}, bf16[256,1024]{1,0:T(8,128)(2,1)}, u32[]{:S(2)}) copy-start(bf16[256,1024]{1,0:T(8,128)(2,1)} %all_gather.49) | copy-start | bytes 1572868
  215.8 25.2 %copy-start.32 = (bf16[32,8,2,512]{3,1,2,0:T(8,128)(2,1)}, bf16[32,8,2,512]{3,1,2,0:T(8,128)(2,1)S(1)}, u32[]{:S(2)}) copy-start(bf16[32,8,2,512]{3,1,2,0:T(8,128)(2,1)S(1)} %copy.63) | copy-start | bytes 1572868
  215.8 4.8 copy-start.52
  215.9 4.9 copy-start.82
  215.9 12.9 copy-start.81
  218.0 98.8 %all-gather.10.cloned.1.call-start = ((), (), s32[]{:S(2)}) async-start(), calls=%async_computation.11 | async-start | bytes 6488064 | tf_op jit(solution)/shard_map/all_gather | solution.py:149
  218.6 110.1 %all-gather.12.cloned.1.call-start = ((), (), s32[]{:S(2)}) async-start(), calls=%async_computation.12 | async-start | bytes 6488064 | tf_op jit(solution)/shard_map/all_gather | solution.py:150
  219.3 138.0 %all-gather.14.cloned.1.call-start = ((), (), s32[]{:S(2)}) async-start(), calls=%async_computation.13 | async-start | bytes 6488064 | tf_op jit(solution)/shard_map/all_gather | solution.py:151
  219.9 184.3 %all-gather.16.cloned.1.call-start = ((), (), s32[]{:S(2)}) async-start(), calls=%async_computation.15 | async-start | bytes 2621440 | tf_op jit(solution)/shard_map/all_gather | solution.py:179
  220.6 383.0 %all-reduce.11.cloned.1.call-start = ((), (), s32[]{:S(2)}) async-start(), calls=%async_computation.16 | async-start | bytes 4194304 | tf_op jit(solution)/shard_map/psum | solution.py:308
  220.7 188.5 %copy-start.46 = (s32[1024,1]{0,1:T(1,128)}, s32[1024,1]{0,1:T(1,128)S(1)}, u32[]{:S(2)}) copy-start(s32[1024,1]{0,1:T(1,128)S(1)} %get-tuple-element.725) | copy-start | bytes 12292
  220.7 188.5 %copy-start.49 = (s32[1024,1]{0,1:T(1,128)}, s32[1024,1]{0,1:T(1,128)S(1)}, u32[]{:S(2)}) copy-start(s32[1024,1]{0,1:T(1,128)S(1)} %get-tuple-element.726) | copy-start | bytes 12292
  228.8 78.7 %copy-start.60 = (f32[8,1,128]{2,1,0:T(1,128)}, f32[8,1,128]{2,1,0:T(1,128)S(1)}, u32[]{:S(2)}) copy-start(f32[8,1,128]{2,1,0:T(1,128)S(1)} %convert_element_type.348) | copy-start | bytes 12292
  237.4 70.9 %copy-start.56 = (bf16[1024,4]{0,1:T(4,128)(2,1)}, bf16[1024,4]{0,1:T(4,128)(2,1)S(1)}, u32[]{:S(2)}) copy-start(bf16[1024,4]{0,1:T(4,128)(2,1)S(1)} %all_gather.51) | copy-start | bytes 24580
  241.0 4.7 copy-start.80
  241.0 9.3 copy-start.58
  241.1 139.4 %copy-start.72 = (s32[1024]{0:T(1024)}, s32[1024]{0:T(1024)S(1)}, u32[]{:S(2)}) copy-start(s32[1024]{0:T(1024)S(1)} %broadcast_clamp_fusion.1) | copy-start | bytes 12292
  241.1 129.0 %copy-start.74 = (s32[1024]{0:T(1024)}, s32[1024]{0:T(1024)S(1)}, u32[]{:S(2)}) copy-start(s32[1024]{0:T(1024)S(1)} %broadcast_clamp_fusion) | copy-start | bytes 12292
  245.9 58.5 %copy-start.8 = (bf16[1024,1024]{1,0:T(8,128)(2,1)S(1)}, bf16[1024,1024]{1,0:T(8,128)(2,1)}, u32[]{:S(2)}) copy-start(bf16[1024,1024]{1,0:T(8,128)(2,1)} %all-gather.8.cloned.1.call-done) | copy-start | bytes 6291460
  250.3 58.6 %copy-start.4 = (s32[2561]{0:T(1024)}, s32[2561]{0:T(1024)S(1)}, u32[]{:S(2)}) copy-start(s32[2561]{0:T(1024)S(1)} %scatter_fusion) | copy-start | bytes 30736
  308.3 8.5 copy-start.19
  409.8 101.5 %copy-start.2 = (f32[1024,4]{0,1:T(4,128)}, f32[1024,4]{0,1:T(4,128)S(1)}, u32[]{:S(2)}) copy-start(f32[1024,4]{0,1:T(4,128)S(1)} %get-tuple-element.710) | copy-start | bytes 49156
  409.9 18.3 %copy-start.53 = (s32[1024,2]{0,1:T(2,128)S(1)}, s32[1024,2]{0,1:T(2,128)}, u32[]{:S(2)}) copy-start(s32[1024,2]{0,1:T(2,128)} %param.32) | copy-start | bytes 24580
  409.9 22.8 %copy-start.59 = (s32[1024,1]{0,1:T(1,128)S(1)}, s32[1024,1]{0,1:T(1,128)}, u32[]{:S(2)}) copy-start(s32[1024,1]{0,1:T(1,128)} %copy-done.58) | copy-start | bytes 12292
  432.7 4.4 copy-start.5
  432.7 4.4 copy-start.21
  485.1 5.2 copy-start.75
  490.2 10.4 copy-start.73
  500.6 10.8 copy-start.47
  500.6 10.8 copy-start.50
  500.6 10.8 copy-start.57
  500.6 10.8 copy-start.63
  500.6 10.8 copy-start.66
  500.7 10.8 copy-start.76
  518.2 600.9 %reduce-scatter.10.cloned.1.call-start = ((), (), s32[]{:S(2)}) async-start(), calls=%async_computation.14 | async-start | bytes 2621440 | tf_op jit(solution)/shard_map/reduce_scatter | solution.py:252
  518.3 85.3 %copy-start.61 = (f32[8,1,128]{2,1,0:T(1,128)S(1)}, f32[8,1,128]{2,1,0:T(1,128)}, u32[]{:S(2)}) copy-start(f32[8,1,128]{2,1,0:T(1,128)} %copy-done.60) | copy-start | bytes 12292
  523.9 83.8 %copy-start.79 = (f32[1024]{0:T(1024)S(1)}, f32[1024]{0:T(1024)}, u32[]{:S(2)}) copy-start(f32[1024]{0:T(1024)} %copy-done.78) | copy-start | bytes 12292
  523.9 83.8 %copy-start.71 = (f32[1024]{0:T(1024)S(1)}, f32[1024]{0:T(1024)}, u32[]{:S(2)}) copy-start(f32[1024]{0:T(1024)} %copy-done.70) | copy-start | bytes 12292
  523.9 598.1 %reduce-scatter.12.cloned.1.call-start = ((), (), s32[]{:S(2)}) async-start(), calls=%async_computation.17 | async-start | bytes 2621440 | tf_op jit(solution)/shard_map/reduce_scatter | solution.py:382
  603.6 4.7 copy-start.22
  608.3 6.4 copy-start.31
  612.7 4.4 copy-start.7
  612.8 4.4 copy-start.41
  612.8 4.4 copy-start.43
  612.8 4.4 copy-start.45
  612.8 4.4 copy-start.55
  720.3 4.3 copy-start.16
  926.4 4.3 copy-start.16
  1063.8 105.6 %reduce-scatter.20.cloned.1.call-start = ((), (), s32[]{:S(2)}) async-start(), calls=%async_computation.21 | async-start | bytes 1179648 | tf_op jit(solution)/shard_map/reduce_scatter | solution.py:400
  1067.9 118.4 %reduce-scatter.18.cloned.1.call-start = ((), (), s32[]{:S(2)}) async-start(), calls=%async_computation.20 | async-start | bytes 1179648 | tf_op jit(solution)/shard_map/reduce_scatter | solution.py:399
  1069.8 156.2 %reduce-scatter.14.cloned.1.call-start = ((), (), s32[]{:S(2)}) async-start(), calls=%async_computation.18 | async-start | bytes 1179648 | tf_op jit(solution)/shard_map/reduce_scatter | solution.py:397
  1071.6 194.2 %reduce-scatter.16.cloned.1.call-start = ((), (), s32[]{:S(2)}) async-start(), calls=%async_computation.19 | async-start | bytes 1179648 | tf_op jit(solution)/shard_map/reduce_scatter | solution.py:398
  1073.5 283.1 %reduce-scatter.26.cloned.1.call-start = ((), (), s32[]{:S(2)}) async-start(), calls=%async_computation.24 | async-start | bytes 12976128 | tf_op jit(solution)/shard_map/reduce_scatter | solution.py:298
  1086.1 361.3 %reduce-scatter.24.cloned.1.call-start = ((), (), s32[]{:S(2)}) async-start(), calls=%async_computation.23 | async-start | bytes 12976128 | tf_op jit(solution)/shard_map/reduce_scatter | solution.py:297
  1098.9 439.3 %reduce-scatter.22.cloned.1.call-start = ((), (), s32[]{:S(2)}) async-start(), calls=%async_computation.22 | async-start | bytes 12976128 | tf_op jit(solution)/shard_map/reduce_scatter | solution.py:296
  1115.3 6.7 copy-start.69
  1117.7 420.6 %copy-start.1 = (f32[4,32]{1,0:T(4,128)S(1)}, f32[4,32]{1,0:T(4,128)}, u32[]{:S(2)}) copy-start(f32[4,32]{1,0:T(4,128)} %param.26) | copy-start | bytes 1540
  (37 other events, 89.0 us)
Sparse Core Ops, SparseCore 0:
  10.4 45.4 all-gather.7
  218.2 86.2 all-reduce.8
  518.4 85.2 all-reduce.10
  605.8 41.9 reduce-scatter.9
  1063.9 41.9 reduce-scatter.11
  1109.5 36.9 reduce-scatter.19
  1150.2 36.0 reduce-scatter.17
  1190.0 35.9 reduce-scatter.13
  1229.8 36.0 reduce-scatter.15
  1269.8 86.7 reduce-scatter.25
  1360.7 86.7 reduce-scatter.23
  1451.4 86.8 reduce-scatter.21
Sparse Core Ops, SparseCore 1:
  220.5 44.4 all-gather.9
  266.9 44.2 all-gather.11
  313.1 44.1 all-gather.13
  359.0 45.1 all-gather.15
where the time goes:
time: 1560 us; the launch traced here: 1550 us
  local copies, waits for them, and re-layouts  561 us (36%)
  waiting for transfers between devices  535 us (34%)
  matrix products  204 us (13%)
  blocking collectives  105 us (7%)
  other arithmetic  86.9 us (6%)
  loops' own time  35.8 us (2%)
  between operations  17.4 us (1%)
    while x26, local copies, waits for them, and re-layouts  313 us
    reduce_scatter x1, waiting for transfers between devices, on_device(): lax.psum_scatter(grad_up, 'dp', scatter_dimension=1, tiled=True)  90.9 us
    reduce_scatter x1, waiting for transfers between devices, on_device(): lax.psum_scatter(grad_gate, 'dp', scatter_dimension=1, tiled=True)  90.8 us
    reduce_scatter x1, waiting for transfers between devices, on_device(): lax.psum_scatter(grad_down, 'dp', scatter_dimension=2, tiled=True)  90.7 us
    psum x1, waiting for transfers between devices, on_device(): lax.psum(norm_two_part.astype(jnp.bfloat16), 'tensor').astype(jnp.float32)  79.7 us
    reshape x4, local copies, waits for them, and re-layouts, skew_rows(): return cut.reshape(head_count, row_count, width_full - 1)[:, :, :key_count]  78.2 us
    psum x1, waiting for transfers between devices, on_device(): lax.psum(attn_part.astype(jnp.bfloat16), 'tensor').astype(jnp.float32)  54.1 us
    psum x1, blocking collectives, on_device(): lax.psum((gain_one_part, gain_two_part, router_part, table_full), ('dp',...  40.8 us
  transfers between devices with their start and end apart: 16, of which 10 were waited for; matrix products, arithmetic and copies ran while one was open for 37% of the time, Pallas kernels for 0%

commit v1 on v0

v1 whole, which is shorter than its diff:
```python
import functools

import jax
import jax.numpy as jnp
import numpy as np
from jax import lax
from jax.experimental import pallas as pl
from jax.experimental.pallas import tpu as pltpu
from jax.sharding import PartitionSpec as P

EXPERTS = 4
PIECE = 256
CAP = 640
BUCKETS = 32
EPSILON = 1e-06
PRECISE = lax.Precision.HIGHEST
LIMITS = (12, 16, 23, 32, 46, 64, 91)
MASKED = -1e30
BF = jnp.bfloat16
F32 = jnp.float32
BLOCK = 256
VMEM_LIMIT = 56 * 1024 * 1024


def params(semantics=None):
    return pltpu.CompilerParams(dimension_semantics=semantics, vmem_limit_bytes=VMEM_LIMIT)


def dot_nn(a, b):
    return lax.dot_general(a, b, (((1,), (0,)), ((), ())), preferred_element_type=F32)


def dot_nt(a, b):
    return lax.dot_general(a, b, (((1,), (1,)), ((), ())), preferred_element_type=F32)


def dot_tn(a, b):
    return lax.dot_general(a, b, (((0,), (0,)), ((), ())), preferred_element_type=F32)


def bucket_of(offsets):
    distance = np.abs(offsets)
    far = np.full_like(distance, 8)
    for bound in LIMITS:
        far = far + (distance >= bound)
    return np.where(distance < 8, distance, far) + np.where(offsets > 0, 16, 0)


def onehot_of(offsets):
    return (bucket_of(offsets)[..., None] == np.arange(BUCKETS)).astype(np.float32)


def cost(flops, nbytes):
    return pl.CostEstimate(flops=int(flops), bytes_accessed=int(nbytes), transcendentals=0)


def vspec():
    return pl.BlockSpec(memory_space=pltpu.VMEM)


def sspec():
    return pl.BlockSpec(memory_space=pltpu.SMEM)


def z_swap(x, mask, size):
    return lax.ppermute(x, "tensor", [(i, i ^ mask) for i in range(size)])


def z_gather(x, size):
    return [x] + [z_swap(x, mask, size) for mask in range(1, size)]


def dp_slots(size):
    if size == 8:
        return np.array([((k >> 1) & 3) | ((k & 1) << 2) for k in range(8)], np.int32)
    return None


def dp_gather(x):
    for bit in (2, 4, 1):
        other = lax.ppermute(x, "dp", [(i, i ^ bit) for i in range(8)])
        x = jnp.concatenate([x, other], 0)
    return x


def dp_scatter_slots():
    return np.array([((k & 1) << 2) | (((k >> 1) & 1) << 1) | ((k >> 2) & 1) for k in range(8)], np.int32)


def dp_scatter(x):
    for bit in (1, 2, 4):
        half = x.shape[0] // 2
        other = lax.ppermute(x[half:], "dp", [(i, i ^ bit) for i in range(8)])
        x = (x[:half].astype(F32) + other.astype(F32)).astype(x.dtype)
    return x[0]


def join_rows(ref, index_ref, count, rows):
    if count == 1:
        return ref[0, 0:rows, :]
    return jnp.concatenate([ref[index_ref[c], 0:rows, :] for c in range(count)], 0)


def qkv_body(count, chunks, rows, index_ref, place_ref, *refs):
    toks = refs[:chunks]
    pack_ref, gain_ref = refs[chunks : chunks + 2]
    n1_ref, q_ref, k_ref, v_ref, kt_ref, vt_ref = refs[chunks + 2 :]
    depth = n1_ref.shape[1] // count
    weights = join_rows(pack_ref, index_ref, count, depth)
    width = q_ref.shape[1]
    gain = gain_ref[0:1, :]
    for c in range(chunks):
        at = pl.ds(pl.multiple_of(place_ref[c] * rows, rows), rows)
        x = toks[c][...].astype(F32)
        scale = lax.rsqrt(jnp.mean(x * x, axis=1, keepdims=True) + EPSILON)
        normed = (x * scale * gain).astype(BF)
        n1_ref[at, :] = normed
        out = dot_nn(normed, weights)
        q_ref[at, :] = (out[:, :width].astype(BF).astype(F32) * 0.125).astype(BF)
        key = out[:, width : 2 * width]
        value = out[:, 2 * width :]
        k_ref[at, :] = key.astype(BF)
        v_ref[at, :] = value.astype(BF)
        kt_ref[:, at] = jnp.transpose(key).astype(BF)
        vt_ref[:, at] = jnp.transpose(value).astype(BF)


def qkv_call(index, place, toks, pack, gain, width):
    chunks, rows, depth = len(toks), toks[0].shape[0], toks[0].shape[1]
    total = chunks * rows
    shapes = [(total, depth)] + [(total, width)] * 3 + [(width, total)] * 2
    return pl.pallas_call(
        functools.partial(qkv_body, pack.shape[0], chunks, rows),
        in_specs=[sspec(), sspec()] + [vspec()] * (chunks + 2),
        out_specs=[vspec()] * 6,
        out_shape=[jax.ShapeDtypeStruct(s, BF) for s in shapes],
        compiler_params=params(),
        cost_estimate=cost(2 * total * depth * 3 * width, 8 * total * depth),
        name="norm_qkv",
    )(index, place, *toks, pack, gain)


def extents(total):
    blocks = total // BLOCK
    return [(i, min(BLOCK * (i + 2), total)) for i in range(blocks)]


def fwd_body(total, starts_ref, q_ref, k_ref, vt_ref, line_ref, p_ref, ot_ref, att_ref, attt_ref, strip_ref, mask_ref):
    head = pl.program_id(0)
    heads = pl.num_programs(0)
    blocks = total // BLOCK
    width = q_ref.shape[1]
    dim = width // 4

    @pl.when(head == 0)
    def _():
        def label(pos):
            first = (pos >= starts_ref[0, 0]) & (pos < starts_ref[0, 0] + PIECE)
            second = (pos >= starts_ref[0, 1]) & (pos < starts_ref[0, 1] + PIECE)
            return first, second

        for i in range(blocks):
            for j in (i, i + 1):
                if j >= blocks:
                    continue
                kpos = lax.broadcasted_iota(jnp.int32, (BLOCK, BLOCK), 0) + BLOCK * j
                qpos = lax.broadcasted_iota(jnp.int32, (BLOCK, BLOCK), 1) + BLOCK * i
                k1, k2 = label(kpos)
                q1, q2 = label(qpos)
                seen = (kpos <= qpos) | (k1 & q1) | (k2 & q2)
                mask_ref[2 * i + j - i] = jnp.where(seen, 0.0, MASKED)

    for beta in range(blocks + 1):
        start = BLOCK * (blocks - beta)
        window = line_ref[0, 0:1, start : start + 2 * BLOCK]
        spread = jnp.broadcast_to(window, (BLOCK, 2 * BLOCK))
        rolled = pltpu.roll(spread, BLOCK + 1, 1, stride=1, stride_axis=0)
        strip_ref[BLOCK * beta : BLOCK * (beta + 1), :] = rolled[:, :BLOCK]

    lanes = lax.broadcasted_iota(jnp.int32, (BLOCK, width), 1)
    own = (lanes >= head * dim) & (lanes < (head + 1) * dim)
    at_head = pl.ds(pl.multiple_of(head * dim, dim), dim)
    for i, extent in extents(total):
        q_rows = q_ref[BLOCK * i : BLOCK * (i + 1), :]
        q_own = jnp.where(own, q_rows, jnp.zeros_like(q_rows))
        base = BLOCK * (blocks - 1 - i)
        scores = dot_nt(k_ref[0:extent, :], q_own) + strip_ref[base : base + extent, :]
        parts = [scores[BLOCK * j : BLOCK * (j + 1)] for j in range(extent // BLOCK)]
        for j in (i, i + 1):
            if j < blocks:
                parts[j] = parts[j] + mask_ref[2 * i + j - i]
        top = functools.reduce(jnp.maximum, parts)
        top = jnp.max(top, axis=0, keepdims=True)
        parts = [jnp.exp(part - top) for part in parts]
        total_sum = jnp.sum(functools.reduce(jnp.add, parts), axis=0, keepdims=True)
        inverse = 1.0 / total_sum
        chances = jnp.concatenate([(part * inverse).astype(BF) for part in parts], 0)
        p_ref[0, 0:extent, BLOCK * i : BLOCK * (i + 1)] = chances
        ot_ref[at_head, BLOCK * i : BLOCK * (i + 1)] = dot_nn(vt_ref[at_head, 0:extent], chances)

    @pl.when(head == heads - 1)
    def _():
        mixed = ot_ref[...]
        attt_ref[...] = mixed.astype(BF)
        att_ref[...] = jnp.transpose(mixed).astype(BF)


def attn_fwd(starts, q, k, vt, line):
    total, width = q.shape
    heads = line.shape[0]
    blocks = total // BLOCK
    whole = lambda shape: pl.BlockSpec(shape, lambda h: (0,) * len(shape))
    return pl.pallas_call(
        functools.partial(fwd_body, total),
        grid=(heads,),
        in_specs=[
            sspec(),
            whole((total, width)),
            whole((total, width)),
            whole((width, total)),
            pl.BlockSpec((1, 1, line.shape[2]), lambda h: (h, 0, 0)),
        ],
        out_specs=[
            pl.BlockSpec((1, total, total), lambda h: (h, 0, 0)),
            whole((width, total)),
            whole((total, width)),
            whole((width, total)),
        ],
        out_shape=[
            jax.ShapeDtypeStruct((heads, total, total), BF),
            jax.ShapeDtypeStruct((width, total), F32),
            jax.ShapeDtypeStruct((total, width), BF),
            jax.ShapeDtypeStruct((width, total), BF),
        ],
        scratch_shapes=[
            pltpu.VMEM((BLOCK * (blocks + 1), BLOCK), F32),
            pltpu.VMEM((2 * blocks, BLOCK, BLOCK), F32),
        ],
        compiler_params=params(("arbitrary",)),
        cost_estimate=cost(heads * 4 * total * total * width, 10 * total * total),
        name="attn_forward",
    )(starts, q, k, vt, line)


def diagonal_sums(acc):
    half = BLOCK // 2
    low, high = acc[:half], acc[half:]
    rows = jnp.concatenate(
        [high[:, :half], high[:, half:] + low[:, :half], low[:, half:], jnp.zeros((half, half), F32)], 1
    )
    step = half // 2
    while step >= 8:
        rows = rows[step:] + pltpu.roll(rows[:step], step, 1)
        step //= 2
    index = lax.broadcasted_iota(jnp.int32, rows.shape, 0)
    for step in (4, 2, 1):
        rows = jnp.where((index & step) == 0, pltpu.roll(rows, step, 1), rows)
    return jnp.sum(rows, axis=0, keepdims=True)


def bwd_body(total, chunks, place_ref, *refs):
    grads = refs[:chunks]
    p_ref, q_ref, k_ref, v_ref, kt_ref, ot_ref = refs[chunks : chunks + 6]
    dq_ref, dk_ref, dv_ref, diag_ref = refs[chunks + 6 : chunks + 10]
    do_ref, dot_ref, dqt_ref, dka_ref, dva_ref, ds_ref, acc_ref = refs[chunks + 10 :]
    head = pl.program_id(0)
    heads = pl.num_programs(0)
    blocks = total // BLOCK
    rows = total // chunks
    width = q_ref.shape[1]
    dim = width // 4

    @pl.when(head == 0)
    def _():
        for c in range(chunks):
            at = pl.ds(pl.multiple_of(place_ref[c] * rows, rows), rows)
            do_ref[at, :] = grads[c][...]
        dot_ref[...] = jnp.transpose(do_ref[...].astype(F32))
        dka_ref[...] = jnp.zeros_like(dka_ref)
        dva_ref[...] = jnp.zeros_like(dva_ref)

    at_head = pl.ds(pl.multiple_of(head * dim, dim), dim)
    inner = jnp.sum(dot_ref[at_head, :] * ot_ref[at_head, :], axis=0, keepdims=True)
    lanes = lax.broadcasted_iota(jnp.int32, (total, width), 1)
    own = (lanes >= head * dim) & (lanes < (head + 1) * dim)
    q_own = jnp.where(own, q_ref[...], jnp.zeros_like(q_ref))
    do_own = jnp.where(own, do_ref[...], jnp.zeros_like(do_ref))
    written = 0
    for i, extent in reversed(extents(total)):
        cols = slice(BLOCK * i, BLOCK * (i + 1))
        chance_grad = dot_nt(v_ref[0:extent, :], do_own[cols, :])
        chances = p_ref[0, 0:extent, cols].astype(F32)
        score_grad = (chances * (chance_grad - inner[:, cols])).astype(BF)
        ds_ref[0:extent, cols] = score_grad
        dqt_ref[at_head, cols] = dot_nn(kt_ref[at_head, 0:extent], score_grad)
        base = BLOCK * (blocks - 1 - i)
        wide = score_grad.astype(F32)
        if i == blocks - 1:
            acc_ref[0:extent, :] = wide
            written = extent
        else:
            old = written - base
            acc_ref[base:written, :] += wide[:old]
            if base + extent > written:
                acc_ref[written : base + extent, :] = wide[old:]
                written = base + extent
    for j in range(blocks):
        first = max(0, BLOCK * (j - 1))
        keys = slice(BLOCK * j, BLOCK * (j + 1))
        dka_ref[keys, :] += dot_nn(ds_ref[keys, first:], q_own[first:, :])
        dva_ref[keys, :] += dot_nn(p_ref[0, keys, first:], do_own[first:, :])
    for beta in range(blocks + 1):
        diag_ref[0, beta : beta + 1, :] = diagonal_sums(acc_ref[BLOCK * beta : BLOCK * (beta + 1), :])

    @pl.when(head == heads - 1)
    def _():
        dq_ref[...] = (jnp.transpose(dqt_ref[...]) * 0.125).astype(BF)
        dk_ref[...] = dka_ref[...].astype(BF)
        dv_ref[...] = dva_ref[...].astype(BF)


def attn_bwd(place, grads, chances, q, k, v, kt, ot):
    total, width = q.shape
    heads = chances.shape[0]
    blocks = total // BLOCK
    chunks = len(grads)
    whole = lambda shape: pl.BlockSpec(shape, lambda h: (0,) * len(shape))
    return pl.pallas_call(
        functools.partial(bwd_body, total, chunks),
        grid=(heads,),
        in_specs=[sspec()]
        + [whole(grads[0].shape)] * chunks
        + [pl.BlockSpec((1, total, total), lambda h: (h, 0, 0))]
        + [whole((total, width))] * 3
        + [whole((width, total))] * 2,
        out_specs=[whole((total, width))] * 3 + [pl.BlockSpec((1, blocks + 1, 2 * BLOCK), lambda h: (h, 0, 0))],
        out_shape=[jax.ShapeDtypeStruct((total, width), BF)] * 3
        + [jax.ShapeDtypeStruct((heads, blocks + 1, 2 * BLOCK), F32)],
        scratch_shapes=[
            pltpu.VMEM((total, width), BF),
            pltpu.VMEM((width, total), F32),
            pltpu.VMEM((width, total), F32),
            pltpu.VMEM((total, width), F32),
            pltpu.VMEM((total, width), F32),
            pltpu.VMEM((total, total), BF),
            pltpu.VMEM((BLOCK * (blocks + 1), BLOCK), F32),
        ],
        compiler_params=params(("arbitrary",)),
        cost_estimate=cost(heads * 8 * total * total * width, 10 * total * total),
        name="attn_backward",
    )(place, *grads, chances, q, k, v, kt, ot)


def join_lanes(ref, index_ref, count, slot):
    if count == 1:
        return ref[0, slot]
    return jnp.concatenate([ref[index_ref[c], slot] for c in range(count)], 1)


def mid_body(count, chunks, index_ref, *refs):
    atts = refs[:chunks]
    w_ref, tok_ref, gain_ref, mid_ref, n2_ref = refs[chunks:]
    u = tok_ref[...].astype(F32)
    for c in range(chunks):
        u = u + dot_nn(atts[c][...], join_lanes(w_ref, index_ref, count, c))
    mid_ref[...] = u
    scale = lax.rsqrt(jnp.mean(u * u, axis=1, keepdims=True) + EPSILON)
    n2_ref[...] = (u * scale * gain_ref[1:2, :]).astype(BF)


def mid_call(index, atts, w_out, tok, gains):
    chunks = len(atts)
    return pl.pallas_call(
        functools.partial(mid_body, w_out.shape[0], chunks),
        in_specs=[sspec()] + [vspec()] * (chunks + 3),
        out_specs=[vspec()] * 2,
        out_shape=[jax.ShapeDtypeStruct(tok.shape, F32), jax.ShapeDtypeStruct(tok.shape, BF)],
        compiler_params=params(),
        cost_estimate=cost(2 * tok.shape[0] * tok.shape[1] ** 2, 4 * tok.shape[1] ** 2),
        name="out_projection_norm",
    )(index, *atts, w_out, tok, gains)


def split_dot(a, b, dot):
    high = a.astype(BF)
    low = (a - high.astype(F32)).astype(BF)
    return dot(high, b) + dot(low, b)


def moe_body(count, chunks, unit, place_ref, *refs):
    n2s = refs[:chunks]
    gs = refs[chunks : 2 * chunks]
    sel_ref, rout_ref, w_ref = refs[2 * chunks : 2 * chunks + 3]
    rest = refs[2 * chunks + 3 :]
    outs = rest[:chunks]
    ngs = rest[chunks : 2 * chunks]
    hg_ref, gg_ref, ug_ref, rpart_ref = rest[2 * chunks : 2 * chunks + 4]
    out_acc, ng_acc, gate_ref, sum_ref, prob_ref = rest[2 * chunks + 4 :]
    step = pl.program_id(0)
    steps = pl.num_programs(0)
    rows = n2s[0].shape[0]
    fb = hg_ref.shape[1]
    lane = lax.broadcasted_iota(jnp.int32, (rows, 128), 1)

    @pl.when(step == 0)
    def _():
        out_acc[...] = jnp.zeros_like(out_acc)
        ng_acc[...] = jnp.zeros_like(ng_acc)
        sum_ref[...] = jnp.zeros_like(sum_ref)
        for c in range(chunks):
            logits = dot_nt(n2s[c][...], rout_ref[...])
            logits = jnp.where(lane < EXPERTS, logits, MASKED)
            raised = jnp.exp(logits - jnp.max(logits, axis=1, keepdims=True))
            probs = raised / jnp.sum(raised, axis=1, keepdims=True)
            prob_ref[c] = probs
            at = pl.ds(pl.multiple_of(place_ref[c] * rows, rows), rows)
            gates = probs * sel_ref[at, :]
            for e in range(EXPERTS):
                one = jnp.sum(jnp.where(lane == e, gates, 0.0), axis=1, keepdims=True)
                gate_ref[e, c] = jnp.broadcast_to(one, (rows, 128))

    def joined(which):
        if count == 1:
            return w_ref[0, which]
        return jnp.concatenate([w_ref[d, which] for d in range(count)], 1)

    wg, wu, wd = joined(0), joined(1), joined(2)
    for c in range(chunks):
        n2 = n2s[c][...]
        gate_pre = dot_nt(n2, wg)
        up_pre = dot_nt(n2, wu)
        raw = dot_nt(gs[c][...], wd)
        square = gate_pre * gate_pre
        c0 = float(np.sqrt(2.0 / np.pi))
        th = jnp.tanh(gate_pre * (c0 + (c0 * 0.044715) * square))
        half = 0.5 + 0.5 * th
        act = gate_pre * half
        slope = half + gate_pre * (0.5 * c0 + (1.5 * c0 * 0.044715) * square) * (1.0 - th * th)
        hidden = act * up_pre
        prod = raw * hidden
        hgs, ggs, ugs = [], [], []
        for m in range(fb // 128):
            col = step * (fb // 128) + m
            e_low = (col * 128) // unit
            e_high = (col * 128 + 127) // unit
            bound = jnp.where(e_high > e_low, unit * e_high - col * 128, 128)
            is_low = lane < bound
            part = slice(128 * m, 128 * (m + 1))
            gate = jnp.where(is_low, gate_ref[e_low, c], gate_ref[e_high, c])
            sum_ref[e_low, c] += jnp.where(is_low, prod[:, part], 0.0)
            sum_ref[e_high, c] += jnp.where(is_low, 0.0, prod[:, part])
            hgs.append((gate * hidden[:, part]).astype(BF))
            hidden_grad = gate * raw[:, part]
            ggs.append((hidden_grad * up_pre[:, part] * slope[:, part]).astype(BF))
            ugs.append((hidden_grad * act[:, part]).astype(BF))
        hg, gg, ug = [jnp.concatenate(x, 1) for x in (hgs, ggs, ugs)]
        at = slice(rows * c, rows * (c + 1))
        hg_ref[at, :] = hg
        gg_ref[at, :] = gg
        ug_ref[at, :] = ug
        out_acc[c] += dot_nn(hg, wd)
        ng_acc[c] += dot_nn(gg, wg) + dot_nn(ug, wu)

    @pl.when(step == steps - 1)
    def _():
        router_grad = jnp.zeros((128, n2s[0].shape[1]), F32)
        for c in range(chunks):
            outs[c][...] = out_acc[c].astype(BF)
            at = pl.ds(pl.multiple_of(place_ref[c] * rows, rows), rows)
            grad = jnp.zeros((rows, 128), F32)
            for e in range(EXPERTS):
                grad = grad + jnp.where(lane == e, jnp.sum(sum_ref[e, c], axis=1, keepdims=True), 0.0)
            grad = grad * sel_ref[at, :]
            probs = prob_ref[c]
            logit_grad = probs * (grad - jnp.sum(probs * grad, axis=1, keepdims=True))
            ngs[c][...] = (ng_acc[c] + split_dot(logit_grad, rout_ref[...], dot_nn)).astype(BF)
            router_grad = router_grad + split_dot(logit_grad, n2s[c][...], dot_tn)
        rpart_ref[...] = router_grad[0:8, :]


def moe_call(place, n2s, gs, sel, router, weights, unit):
    chunks, rows, depth = len(n2s), n2s[0].shape[0], n2s[0].shape[1]
    count, _, ff, part = weights.shape
    tokens = chunks * rows
    whole = lambda shape: pl.BlockSpec(shape, lambda s: (0,) * len(shape))
    kept = [jax.ShapeDtypeStruct((tokens, ff), BF)] * 3
    return pl.pallas_call(
        functools.partial(moe_body, count, chunks, unit),
        grid=(ff // BLOCK,),
        in_specs=[sspec()]
        + [whole((rows, depth))] * (2 * chunks)
        + [whole(sel.shape), whole(router.shape), pl.BlockSpec((count, 3, BLOCK, part), lambda s: (0, 0, s, 0))],
        out_specs=[whole((rows, depth))] * (2 * chunks)
        + [pl.BlockSpec((tokens, BLOCK), lambda s: (0, s))] * 3
        + [whole((8, depth))],
        out_shape=[jax.ShapeDtypeStruct((rows, depth), BF)] * (2 * chunks)
        + kept
        + [jax.ShapeDtypeStruct((8, depth), F32)],
        scratch_shapes=[
            pltpu.VMEM((chunks, rows, depth), F32),
            pltpu.VMEM((chunks, rows, depth), F32),
            pltpu.VMEM((EXPERTS, chunks, rows, 128), F32),
            pltpu.VMEM((EXPERTS, chunks, rows, 128), F32),
            pltpu.VMEM((chunks, rows, 128), F32),
        ],
        compiler_params=params(("arbitrary",)),
        cost_estimate=cost(12 * tokens * depth * ff, 6 * depth * ff + 12 * tokens * depth),
        name="experts",
    )(place, *n2s, *gs, sel, router, weights)


def wgrad_body(count, groups, chunks, *refs):
    kept = refs[: 3 * groups]
    n2s = refs[3 * groups : 3 * groups + chunks]
    gs = refs[3 * groups + chunks : 3 * groups + 2 * chunks]
    out_ref = refs[-1]
    part = out_ref.shape[3]
    rows = n2s[0].shape[0]
    per = chunks // groups
    for which, (pick, sides) in enumerate(((1, n2s), (2, n2s), (0, gs))):
        total = None
        for c in range(chunks):
            at = slice(rows * (c % per), rows * (c % per + 1))
            term = dot_tn(kept[3 * (c // per) + pick][at, :], sides[c][...])
            total = term if total is None else total + term
        total = total.astype(BF)
        for d in range(count):
            out_ref[d, which] = total[:, part * d : part * (d + 1)]


def wgrad_call(count, kept, n2s, gs):
    groups = len(kept) // 3
    tokens, ff = kept[0].shape
    chunks, rows, depth = len(n2s), n2s[0].shape[0], n2s[0].shape[1]
    whole = lambda shape: pl.BlockSpec(shape, lambda s: (0,) * len(shape))
    return pl.pallas_call(
        functools.partial(wgrad_body, count, groups, chunks),
        grid=(ff // BLOCK,),
        in_specs=[pl.BlockSpec((tokens, BLOCK), lambda s: (0, s))] * (3 * groups)
        + [whole((rows, depth))] * (2 * chunks),
        out_specs=pl.BlockSpec((count, 3, BLOCK, depth // count), lambda s: (0, 0, s, 0)),
        out_shape=jax.ShapeDtypeStruct((count, 3, ff, depth // count), BF),
        compiler_params=params(("arbitrary",)),
        cost_estimate=cost(6 * chunks * rows * depth * ff, 12 * depth * ff),
        name="expert_weight_grads",
    )(*kept, *n2s, *gs)


def norm_back(grad, u, gain):
    scale = lax.rsqrt(jnp.mean(u * u, axis=1, keepdims=True) + EPSILON)
    m = grad * gain
    back = scale * m - u * (scale * scale * scale) * jnp.mean(u * m, axis=1, keepdims=True)
    return back, jnp.sum(grad * u * scale, axis=0, keepdims=True)


def resid_body(count, chunks, index_ref, *refs):
    parts = refs[:chunks]
    mid_ref, g_ref, gains_ref, w_ref = refs[chunks : chunks + 4]
    rest = refs[chunks + 4 :]
    resid_ref, aog_ref, gain_ref = rest[:3]
    dos = rest[3:]
    grad = functools.reduce(jnp.add, [p[...].astype(F32) for p in parts])
    back, gain_part = norm_back(grad, mid_ref[...], gains_ref[1:2, :])
    resid = g_ref[...].astype(F32) + back
    resid_ref[...] = resid
    low = resid.astype(BF)
    aog_ref[...] = low
    gain_ref[...] = jnp.broadcast_to(gain_part, gain_ref.shape)
    for c in range(chunks):
        dos[c][...] = dot_nt(low, join_lanes(w_ref, index_ref, count, c)).astype(BF)


def resid_call(index, parts, mid, grad, gains, w_out):
    chunks = len(parts)
    shape = mid.shape
    width = w_out.shape[2]
    return pl.pallas_call(
        functools.partial(resid_body, w_out.shape[0], chunks),
        in_specs=[sspec()] + [vspec()] * (chunks + 4),
        out_specs=[vspec()] * (3 + chunks),
        out_shape=[
            jax.ShapeDtypeStruct(shape, F32),
            jax.ShapeDtypeStruct(shape, BF),
            jax.ShapeDtypeStruct((8, shape[1]), F32),
        ]
        + [jax.ShapeDtypeStruct((shape[0], width), BF)] * chunks,
        compiler_params=params(),
        cost_estimate=cost(2 * shape[0] * shape[1] ** 2, 4 * shape[1] ** 2),
        name="resid_grad",
    )(index, *parts, mid, grad, gains, w_out)


def final_body(chunks, *refs):
    parts = refs[:chunks]
    tok_ref, resid_ref, gains_ref, out_ref = refs[chunks:]
    grad = functools.reduce(jnp.add, [p[...].astype(F32) for p in parts])
    back, _ = norm_back(grad, tok_ref[...].astype(F32), gains_ref[0:1, :])
    out_ref[...] = resid_ref[...] + back


def final_call(parts, tok, resid, gains):
    return pl.pallas_call(
        functools.partial(final_body, len(parts)),
        in_specs=[vspec()] * (len(parts) + 3),
        out_specs=vspec(),
        out_shape=jax.ShapeDtypeStruct(tok.shape, F32),
        compiler_params=params(),
        cost_estimate=cost(20 * tok.size, 12 * tok.size),
        name="in_grad",
    )(*parts, tok, resid, gains)


def proj_body(count, chunks, rows, index_ref, place_ref, dq_ref, dk_ref, dv_ref, pack_ref, *refs):
    toks = refs[:chunks]
    outs = refs[chunks : 2 * chunks]
    gain_ref = refs[2 * chunks]
    depth = outs[0].shape[1]
    width = dq_ref.shape[1]
    weights = join_rows(pack_ref, index_ref, count, depth // count)
    gain = jnp.zeros((1, depth), F32)
    for c in range(chunks):
        at = pl.ds(pl.multiple_of(place_ref[c] * rows, rows), rows)
        grad = dot_nt(dq_ref[at, :], weights[:, :width])
        grad = grad + dot_nt(dk_ref[at, :], weights[:, width : 2 * width])
        grad = grad + dot_nt(dv_ref[at, :], weights[:, 2 * width :])
        outs[c][...] = grad.astype(BF)
        x = toks[c][...].astype(F32)
        scale = lax.rsqrt(jnp.mean(x * x, axis=1, keepdims=True) + EPSILON)
        gain = gain + jnp.sum(grad * x * scale, axis=0, keepdims=True)
    gain_ref[...] = jnp.broadcast_to(gain, gain_ref.shape)


def proj_call(index, place, dq, dk, dv, pack, toks):
    chunks, rows, depth = len(toks), toks[0].shape[0], toks[0].shape[1]
    return pl.pallas_call(
        functools.partial(proj_body, pack.shape[0], chunks, rows),
        in_specs=[sspec(), sspec()] + [vspec()] * (4 + chunks),
        out_specs=[vspec()] * (chunks + 1),
        out_shape=[jax.ShapeDtypeStruct((rows, depth), BF)] * chunks + [jax.ShapeDtypeStruct((8, depth), F32)],
        compiler_params=params(),
        cost_estimate=cost(6 * chunks * rows * depth * dq.shape[1], 8 * chunks * rows * depth),
        name="projection_grads",
    )(index, place, dq, dk, dv, pack, *toks)


def attn_weights_body(count, chunks, rows, slot_ref, place_ref, n1_ref, dq_ref, dk_ref, dv_ref, attt_ref, *refs):
    aogs = refs[:chunks]
    out_ref = refs[chunks]
    depth = n1_ref.shape[1]
    width = dq_ref.shape[1]
    part = depth // count
    normed = n1_ref[...]
    for m, ref in enumerate((dq_ref, dk_ref, dv_ref)):
        grad = dot_tn(normed, ref[...]).astype(BF)
        for d in range(count):
            slot = slot_ref[d]
            for half in range(width // 128):
                at = (m * (width // 128) + half) * part
                out_ref[slot, at : at + part, :] = grad[part * d : part * (d + 1), 128 * half : 128 * (half + 1)]
    grad = None
    for c in range(chunks):
        at = pl.ds(pl.multiple_of(place_ref[c] * rows, rows), rows)
        term = dot_nn(attt_ref[:, at], aogs[c][...])
        grad = term if grad is None else grad + term
    grad = grad.astype(BF)
    for d in range(count):
        at = 3 * (width // 128) * part
        out_ref[slot_ref[d], at : at + width, :] = grad[:, part * d : part * (d + 1)]


def attn_weights_call(slots, place, n1, dq, dk, dv, attt, aogs, count):
    total, depth = n1.shape
    width = dq.shape[1]
    part = depth // count
    chunks, rows = len(aogs), aogs[0].shape[0]
    out = (count, 3 * width * part // 128 + width, 128)
    return pl.pallas_call(
        functools.partial(attn_weights_body, count, chunks, rows),
        in_specs=[sspec(), sspec()] + [vspec()] * (5 + chunks),
        out_specs=vspec(),
        out_shape=jax.ShapeDtypeStruct(out, BF),
        compiler_params=params(),
        cost_estimate=cost(8 * total * depth * width, 8 * total * depth),
        name="attn_weight_grads",
    )(slots, place, n1, dq, dk, dv, attt, *aogs)


def kept_choices(ids):
    lanes = jnp.arange(128, dtype=jnp.int32)[None, :]
    expert_range = jnp.arange(EXPERTS, dtype=jnp.int32)[None, :]
    first = (ids[:, 0:1] == expert_range).astype(jnp.int32)
    second = (ids[:, 1:2] == expert_range).astype(jnp.int32)
    runs = jnp.cumsum(jnp.concatenate([first, second], 1), axis=0)
    first_run = runs[:, :EXPERTS]
    second_run = runs[:, EXPERTS:] + first_run[-1][None, :]
    place_one = jnp.sum(first_run * first, axis=1, keepdims=True) - 1
    place_two = jnp.sum(second_run * second, axis=1, keepdims=True) - 1
    kept = ((ids[:, 0:1] == lanes) & (place_one < CAP)) | ((ids[:, 1:2] == lanes) & (place_two < CAP))
    return kept.astype(F32)


def on_device(
    tokens_in,
    out_grad,
    attn_gain,
    w_query,
    w_key,
    w_value,
    w_output,
    rel_table,
    moe_gain,
    w_router,
    w_gate,
    w_up,
    down_weight,
    expert_ids,
    piece_starts,
):
    rows, depth = tokens_in.shape
    width = w_query.shape[1]
    z_size = lax.axis_size("tensor")
    dp_size = lax.axis_size("dp")
    z_rank = lax.axis_index("tensor").astype(jnp.int32)
    dp_rank = lax.axis_index("dp").astype(jnp.int32)
    total = rows * z_size
    share = depth // dp_size
    unit = w_gate.shape[2]
    ff = EXPERTS * unit
    heads = rel_table.shape[0]
    direct = dp_size == 8 and share == 128
    place = z_rank ^ jnp.arange(z_size, dtype=jnp.int32)

    local = jnp.stack(
        [
            jnp.swapaxes(w_gate, 1, 2).reshape(ff, share),
            jnp.swapaxes(w_up, 1, 2).reshape(ff, share),
            down_weight.reshape(ff, share),
        ]
    )
    if direct:
        experts_w = lax.all_gather(local, "dp", axis=0)
    else:
        experts_w = lax.all_gather(local, "dp", axis=2, tiled=True)[None]

    toks = z_gather(tokens_in, z_size)
    small = jnp.concatenate([attn_gain, moe_gain, w_router.T.reshape(-1)])[None, :]
    packed = jnp.concatenate([w_query, w_key, w_value], 1)
    wo_slots = jnp.stack(z_gather(w_output, z_size))
    if direct:
        index = jnp.asarray(dp_slots(8))[dp_rank ^ jnp.arange(8, dtype=jnp.int32)]
        pad = jnp.zeros((15, packed.shape[1]), BF)
        pack = dp_gather(jnp.concatenate([packed, small, pad], 0)[None])
        wo_all = dp_gather(wo_slots[None])
        small_all = pack[:, share, :][index]
    else:
        index = jnp.zeros((1,), jnp.int32)
        pack = lax.all_gather(packed, "dp", axis=0, tiled=True)[None]
        small_all = lax.all_gather(small[0], "dp", axis=0)
        wo_all = lax.all_gather(wo_slots, "dp", axis=2, tiled=True)[None]
    small_all = small_all.reshape(dp_size, 2 + EXPERTS, share)
    small_all = jnp.swapaxes(small_all, 0, 1).reshape(2 + EXPERTS, depth)
    gains = jnp.concatenate([small_all[:2].astype(F32), jnp.zeros((6, depth), F32)], 0)
    router = jnp.concatenate([small_all[2:], jnp.zeros((128 - EXPERTS, depth), BF)], 0)

    line_at = 2 * BLOCK - 1 - np.arange(total + 2 * BLOCK)
    line = jnp.dot(rel_table, jnp.asarray(onehot_of(line_at).T), precision=PRECISE)[:, None, :]
    sel = kept_choices(expert_ids)

    n1, q, k, v, kt, vt = qkv_call(index, place, toks, pack, gains, width)
    chances, ot, att, attt = attn_fwd(piece_starts, q, k, vt, line)

    atts = []
    for mask in range(z_size):
        piece = lax.dynamic_slice_in_dim(att, place[mask] * rows, rows, 0)
        atts.append(piece if mask == 0 else z_swap(piece, mask, z_size))
    mid, n2 = mid_call(index, atts, wo_all, tokens_in, gains)

    gs = z_gather(out_grad, z_size)
    n2s = z_gather(n2, z_size)
    moe = moe_call(place, n2s, gs, sel, router, experts_w, unit)
    outs, ngs = moe[:z_size], moe[z_size : 2 * z_size]
    kept = moe[2 * z_size : 2 * z_size + 3]
    router_part = moe[2 * z_size + 3]

    ng_parts = [ngs[0]] + [z_swap(ngs[m], m, z_size) for m in range(1, z_size)]
    weight_grads = wgrad_call(experts_w.shape[0], kept, n2s, gs)
    if direct:
        expert_grads = lax.psum_scatter(weight_grads, "dp", scatter_dimension=0, tiled=False)
    else:
        expert_grads = lax.psum_scatter(weight_grads[0], "dp", scatter_dimension=2, tiled=True)

    resid = resid_call(index, ng_parts, mid, out_grad, gains, wo_all)
    resid_grad, aog, gain_two = resid[:3]
    dos = [resid[3]] + [z_swap(resid[3 + m], m, z_size) for m in range(1, z_size)]
    dq, dk, dv, diag = attn_bwd(place, dos, chances, q, k, v, kt, ot)
    out_parts = [outs[0]] + [z_swap(outs[m], m, z_size) for m in range(1, z_size)]
    out_rows = (mid + functools.reduce(jnp.add, [p.astype(F32) for p in out_parts])).astype(BF)
    aogs = z_gather(aog, z_size)

    proj = proj_call(index, place, dq, dk, dv, pack, toks)
    n1_parts = [proj[0]] + [z_swap(proj[m], m, z_size) for m in range(1, z_size)]
    gain_one = proj[z_size]
    in_grad = final_call(n1_parts, tokens_in, resid_grad, gains)

    if direct:
        slots = jnp.asarray(dp_scatter_slots())[dp_rank ^ jnp.arange(8, dtype=jnp.int32)]
        attn_grads = dp_scatter(attn_weights_call(slots, place, n1, dq, dk, dv, attt, aogs, 8)).astype(F32)
        per = width // 128
        cut = attn_grads[: 3 * per * share].reshape(3, per, share, 128)
        cut = jnp.swapaxes(cut, 1, 2).reshape(3, share, width)
        grad_wo = attn_grads[3 * per * share :]
    else:
        ordered = lax.all_gather(aog, "tensor", axis=0, tiled=True)
        cut = jnp.stack([jnp.dot(n1.T, d, preferred_element_type=F32) for d in (dq, dk, dv)])
        cut = lax.psum_scatter(cut, "dp", scatter_dimension=1, tiled=True)
        grad_wo = jnp.dot(attt, ordered, preferred_element_type=F32)
        grad_wo = lax.psum_scatter(grad_wo, "dp", scatter_dimension=1, tiled=True)

    diag_at = (
        BLOCK * np.arange(total // BLOCK + 1)[:, None] - (BLOCK * (total // BLOCK - 2) + 1) - np.arange(2 * BLOCK)[None, :]
    )
    table = jnp.einsum("hbt,btk->hk", diag, jnp.asarray(onehot_of(diag_at)), precision=PRECISE)

    smalls = jnp.concatenate([gain_one[:1], gain_two[:1], router_part[:EXPERTS]], 0)
    table_row = jnp.pad(table.reshape(1, -1), ((0, 0), (0, depth - heads * BUCKETS)))
    if direct:
        for bit in (1, 2):
            smalls = smalls + z_swap(smalls, bit, z_size)
        smalls = jnp.concatenate([smalls, table_row], 0)
        for bit in (1, 2, 4):
            smalls = smalls + lax.ppermute(smalls, "dp", [(i, i ^ bit) for i in range(8)])
        table_row = smalls[2 + EXPERTS :]
    else:
        smalls = lax.psum(smalls, ("dp", "tensor"))
        table_row = lax.psum(table_row, "dp")
    grad_table = table_row[0, : heads * BUCKETS].reshape(heads, BUCKETS)
    per_device = depth // (dp_size * z_size)
    own = lax.dynamic_slice_in_dim(smalls, (dp_rank * z_size + z_rank) * per_device, per_device, 1)

    wide = expert_grads.astype(F32).reshape(3, EXPERTS, unit, share)
    return (
        out_rows,
        in_grad,
        own[0],
        cut[0],
        cut[1],
        cut[2],
        grad_wo,
        grad_table,
        own[1],
        own[2 : 2 + EXPERTS].T,
        jnp.swapaxes(wide[0], 1, 2),
        jnp.swapaxes(wide[1], 1, 2),
        wide[2],
    )


def solution(mesh):
    rows = P(("dp", "tensor"), None)
    grid = P("dp", "tensor")
    flat = P(("dp", "tensor"))
    weights = (P(None, "dp", "tensor"), P(None, "dp", "tensor"), P(None, "tensor", "dp"))
    in_specs = (rows, rows, P("dp"), grid, grid, grid, P("tensor", "dp"), P("tensor", None), P("dp"), P("dp", None))
    out_specs = (rows, rows, flat, grid, grid, grid, P("tensor", "dp"), P("tensor", None), flat, rows)
    return jax.shard_map(
        on_device,
        mesh=mesh,
        in_specs=in_specs + weights + (P("dp", None), P("dp", None)),
        out_specs=out_specs + weights,
        check_vma=False,
    )
```

time: 1560 us -> 522 us (0.33)
  local copies, waits for them, and re-layouts: 561 us -> 26.9 us
  waiting for transfers between devices: 535 us -> 267 us
  matrix products: 204 us -> 0.57 us
  Pallas kernels: 0 us -> 146 us
  blocking collectives: 105 us -> 0 us
  other arithmetic: 86.9 us -> 16.3 us
  starting transfers between devices: 0.87 us -> 46.3 us
  loops' own time: 35.8 us -> 0 us
    reduce_scatter x9 -> x1, waiting for transfers between devices: 369 us -> 0.01 us  [on_device(): lax.psum_scatter(weight_grads, 'dp', scatter_dimension=0, tiled=False)]
    while x26 -> x0, local copies, waits for them, and re-layouts: 313 us -> none
    ppermute x0 -> x44, waiting for transfers between devices: none -> 267 us  [the longest x32 242 us: z_swap(): return lax.ppermute(x, 'tensor', [(i, i ^ mask) for i in range(size)])]
    dot_general x43 -> x2, matrix products: 204 us -> 0.57 us  [the longest x1 0.35 us: on_device(): jnp.einsum('hbt,btk->hk', diag, jnp.asarray(onehot_of(diag_at)), precisio...]
    pallas_call x0 -> x10, Pallas kernels: none -> 146 us  [the longest x1 58.6 us: moe_call(): pl.pallas_call(functools.partial(moe_body, count, chunks, unit), grid=(ff...]
    psum x2 -> x0, waiting for transfers between devices: 134 us -> none  [the longest x1 79.7 us: on_device(): lax.psum(norm_two_part.astype(jnp.bfloat16), 'tensor').astype(jnp.float32)]
    reshape x6 -> x1, local copies, waits for them, and re-layouts: 108 us -> 0.09 us  [on_device(): table.reshape(1, -1)]
    all_gather x7 -> x0, blocking collectives: 63.9 us -> none  [the longest x1 10.9 us: fetch_dense(): lax.all_gather(w_output, 'dp', axis=1, tiled=True)]
  transfers between devices with their start and end apart: 16 -> 46, of which waited for: 10 -> 26; matrix products, arithmetic and copies ran while one was open for 37% -> 6% of each run, Pallas kernels for 0% -> 12%
where the time goes in v1:
time: 522 us; the launch traced here: 521 us
  waiting for transfers between devices  267 us (51%)
  Pallas kernels  146 us (28%)
  starting transfers between devices  46.3 us (9%)
  local copies, waits for them, and re-layouts  26.9 us (5%)
  between operations  17.3 us (3%)
  other arithmetic  16.3 us (3%)
    ppermute x32, waiting for transfers between devices, z_swap(): return lax.ppermute(x, 'tensor', [(i, i ^ mask) for i in range(size)])  242 us
    pallas_call x1, Pallas kernels, moe_call(): pl.pallas_call(functools.partial(moe_body, count, chunks, unit), grid=(ff...  58.6 us
    ppermute x32, starting transfers between devices, z_swap(): return lax.ppermute(x, 'tensor', [(i, i ^ mask) for i in range(size)])  44 us
    pallas_call x1, Pallas kernels, wgrad_call(): pl.pallas_call(functools.partial(wgrad_body, count, groups, chunks), grid...  24.7 us
    ppermute x6, waiting for transfers between devices, dp_gather(): other = lax.ppermute(x, 'dp', [(i, i ^ bit) for i in range(8)])  21.8 us
    pallas_call x1, Pallas kernels, attn_fwd(): pl.pallas_call(functools.partial(fwd_body, total), grid=(heads,), in_spec...  16.5 us
    pallas_call x1, Pallas kernels, attn_bwd(): pl.pallas_call(functools.partial(bwd_body, total, chunks), grid=(heads,),...  14.9 us
  transfers between devices with their start and end apart: 46, of which 26 were waited for; matrix products, arithmetic and copies ran while one was open for 6% of the time, Pallas kernels for 12%

profile of v1, /device:TPU:14, one launch (start us, length us, event | category | flops | bytes accessed | tf_op | source)
XLA Modules:
  0.0 520.5 jit_solution(6545319074542870151)
XLA Ops:
  7.2 3.1 pad_maximum_fusion
  11.6 2.7 collective-permute-start.11
  14.3 1.2 collective-permute-start.10
  16.4 1.6 collective-permute-start.2
  18.1 2.3 reduce-window.6
  22.8 1.7 collective-permute-start.1
  24.5 16.2 %collective-permute-done.11 = bf16[256,128]{1,0:T(8,128)(2,1)S(1)} collective-permute-done((bf16[256,128]{1,0:T(8,128)(2,1)S(1)}, bf16[256,128]{1,0:T(8,128)(2,1)S(1)}, u32[]{:S(2)}, u32[]{:S(2)}) %collective-permute-start.11) | collective-permute-done | bytes 65568 | tf_op jit(solution)/shard_map/ppermute | solution.py:66
  40.7 2.1 collective-permute-done.10
  43.7 1.0 pad_maximum_fusion.4
  48.6 2.8 collective-permute-done.12
  52.4 17.7 %collective-permute-done.13 = bf16[2,4,256,128]{3,2,1,0:T(8,128)(2,1)S(1)} collective-permute-done((bf16[2,4,256,128]{3,2,1,0:T(8,128)(2,1)S(1)}, bf16[2,4,256,128]{3,2,1,0:T(8,128)(2,1)S(1)}, u32[]{:S(2)}, u32[]{:S(2)}) %collective-permute-start.13) | collective-permute-done | bytes 524320 | tf_op jit(solution)/shard_map/ppermute | solution.py:81
  70.1 1.4 collective-permute-start.20
  71.5 1.1 pad_maximum_fusion.3
  72.8 1.2 copy-done.7
  75.3 1.7 collective-permute-start.19
  77.0 6.0 %norm_qkv.1 = (bf16[1024,1024]{1,0:T(8,128)(2,1)}, bf16[1024,256]{1,0:T(8,128)(2,1)}, bf16[1024,256]{1,0:T(8,128)(2,1)}, bf16[1024,256]{1,0:T(8,128)(2,1)}, bf16...) custom-call(s32[8]{0:T(128)} %copy-done.32, s32[4]{0:T(128)} %copy-done.29, bf16[256,1024]{1,0:T(8,128)(2,1)} %refs_4_.3, ...), custom_call_target="tpu_custom_call" | custom-call | flops 1610612736 | bytes 8388608 | tf_op jit(solution)/shard_map/norm_qkv/pallas_call | solution.py:132
  83.0 16.5 %attn_forward.1 = (bf16[4,1024,1024]{2,1,0:T(8,128)(2,1)}, f32[256,1024]{1,0:T(8,128)}, bf16[1024,256]{1,0:T(8,128)(2,1)}, bf16[256,1024]{1,0:T(8,128)(2,1)}) custom-call(s32[1,2]{1,0:T(1,128)} %starts_ref.1, bf16[1024,256]{1,0:T(8,128)(2,1)} %get-tuple-element.53.q_ref.refs_5_, bf16[1024,256]{1,0:T(8,128)(2,1)} %get-tuple-element.54.k_ref.refs_6_, ...), custom_call_target="tpu_custom_call" | custom-call | flops 4294967296 | bytes 10485760 | tf_op jit(solution)/shard_map/attn_forward/pallas_call | solution.py:213
  99.5 1.8 constant_dynamic-slice_fusion.1
  102.3 1.7 collective-permute-start.7
  104.8 2.7 pad_maximum_fusion.1.refs_4_.refs_7_
  107.5 18.3 %collective-permute-done.8.refs_3_ = bf16[256,256]{1,0:T(8,128)(2,1)S(1)} collective-permute-done((bf16[256,256]{1,0:T(8,128)(2,1)S(1)}, bf16[256,256]{1,0:T(8,128)(2,1)S(1)}, u32[]{:S(2)}, u32[]{:S(2)}) %collective-permute-start.8) | collective-permute-done | bytes 131104 | tf_op jit(solution)/shard_map/ppermute | solution.py:66
  127.0 3.9 out_projection_norm.1
  131.8 4.3 collective-permute-start.16
  136.2 1.6 fusion.2.refs_8_
  139.1 29.2 %collective-permute-done.17.refs_3_.refs_6_ = bf16[256,1024]{1,0:T(8,128)(2,1)S(1)} collective-permute-done((bf16[256,1024]{1,0:T(8,128)(2,1)}, bf16[256,1024]{1,0:T(8,128)(2,1)S(1)}, u32[]{:S(2)}, u32[]{:S(2)}) %collective-permute-start.17) | collective-permute-done | bytes 524320 | tf_op jit(solution)/shard_map/ppermute | solution.py:66
  168.4 8.2 %collective-permute-done.16.refs_2_.refs_5_ = bf16[256,1024]{1,0:T(8,128)(2,1)S(1)} collective-permute-done((bf16[256,1024]{1,0:T(8,128)(2,1)}, bf16[256,1024]{1,0:T(8,128)(2,1)S(1)}, u32[]{:S(2)}, u32[]{:S(2)}) %collective-permute-start.16) | collective-permute-done | bytes 524320 | tf_op jit(solution)/shard_map/ppermute | solution.py:66
  177.4 58.6 %experts.1 = (bf16[256,1024]{1,0:T(8,128)(2,1)}, bf16[256,1024]{1,0:T(8,128)(2,1)}, bf16[256,1024]{1,0:T(8,128)(2,1)}, bf16[256,1024]{1,0:T(8,128)(2,1)}, bf16[2...) custom-call(s32[4]{0:T(128)} %copy-done.29, ...), custom_call_target="tpu_custom_call" | custom-call | flops 35433480192 | bytes 29884416 | tf_op jit(solution)/shard_map/experts/pallas_call | solution.py:487
  236.0 24.7 %expert_weight_grads.1 = bf16[8,3,2816,128]{3,2,1,0:T(8,128)(2,1)} custom-call(bf16[1024,2816]{1,0:T(8,128)(2,1)} %get-tuple-element.90.refs_0_, bf16[1024,2816]{1,0:T(8,128)(2,1)} %get-tuple-element.91.refs_1_, bf16[1024,2816]{1,0:T(8,128)(2,1)} %get-tuple-element.92.refs_2_, bf16[256,1024]{1,0:T(8,128)(2,1)} %get-tuple-element.58.refs_0_.refs_3_, ...), custom_call_target="tpu_custom_call" | custom-call | flops 17716740096 | bytes 34603008 | tf_op jit(solution)/shard_map/expert_weight_grads/pallas_call | solution.py:536
  260.8 1.0 copy-done.43
  261.8 3.6 collective-permute-start.24
  265.3 1.6 collective-permute-start.26
  266.9 18.9 %collective-permute-done.24.refs_1_ = bf16[256,1024]{1,0:T(8,128)(2,1)S(1)} collective-permute-done((bf16[256,1024]{1,0:T(8,128)(2,1)S(1)}, bf16[256,1024]{1,0:T(8,128)(2,1)S(1)}, u32[]{:S(2)}, u32[]{:S(2)}) %collective-permute-start.24) | collective-permute-done | bytes 524320 | tf_op jit(solution)/shard_map/ppermute | solution.py:66
  285.9 14.3 %collective-permute-done.25.refs_2_ = bf16[256,1024]{1,0:T(8,128)(2,1)S(1)} collective-permute-done((bf16[256,1024]{1,0:T(8,128)(2,1)S(1)}, bf16[256,1024]{1,0:T(8,128)(2,1)S(1)}, u32[]{:S(2)}, u32[]{:S(2)}) %collective-permute-start.25) | collective-permute-done | bytes 524320 | tf_op jit(solution)/shard_map/ppermute | solution.py:66
  300.2 11.5 %collective-permute-done.26.refs_3_ = bf16[256,1024]{1,0:T(8,128)(2,1)S(1)} collective-permute-done((bf16[256,1024]{1,0:T(8,128)(2,1)S(1)}, bf16[256,1024]{1,0:T(8,128)(2,1)S(1)}, u32[]{:S(2)}, u32[]{:S(2)}) %collective-permute-start.26) | collective-permute-done | bytes 524320 | tf_op jit(solution)/shard_map/ppermute | solution.py:66
  312.5 5.2 %resid_grad.1 = (f32[256,1024]{1,0:T(8,128)}, bf16[256,1024]{1,0:T(8,128)(2,1)}, f32[8,1024]{1,0:T(8,128)}, bf16[256,256]{1,0:T(8,128)(2,1)}, bf16[256,256]{1,0:...) custom-call(s32[8]{0:T(128)} %copy-done.32, bf16[256,1024]{1,0:T(8,128)(2,1)} %get-tuple-element.63.refs_0_, ...), custom_call_target="tpu_custom_call" | custom-call | flops 536870912 | bytes 4194304 | tf_op jit(solution)/shard_map/resid_grad/pallas_call | solution.py:577
  317.7 1.7 collective-permute-start.28
  319.4 1.8 collective-permute-start.29
  321.2 1.2 gather_fusion.2
  322.6 3.1 collective-permute-start.39
  325.8 22.7 %collective-permute-done.28.refs_2_ = bf16[256,256]{1,0:T(8,128)(2,1)S(1)} collective-permute-done((bf16[256,256]{1,0:T(8,128)(2,1)}, bf16[256,256]{1,0:T(8,128)(2,1)S(1)}, u32[]{:S(2)}, u32[]{:S(2)}) %collective-permute-start.28) | collective-permute-done | bytes 131104 | tf_op jit(solution)/shard_map/ppermute | solution.py:66
  348.5 6.3 %collective-permute-done.29.refs_3_ = bf16[256,256]{1,0:T(8,128)(2,1)S(1)} collective-permute-done((bf16[256,256]{1,0:T(8,128)(2,1)}, bf16[256,256]{1,0:T(8,128)(2,1)S(1)}, u32[]{:S(2)}, u32[]{:S(2)}) %collective-permute-start.29) | collective-permute-done | bytes 131104 | tf_op jit(solution)/shard_map/ppermute | solution.py:66
  355.4 14.9 %attn_backward.1 = (bf16[1024,256]{1,0:T(8,128)(2,1)}, bf16[1024,256]{1,0:T(8,128)(2,1)}, bf16[1024,256]{1,0:T(8,128)(2,1)}, f32[4,5,512]{2,1,0:T(8,128)}) custom-call(s32[4]{0:T(128)} %copy-done.29, bf16[256,256]{1,0:T(8,128)(2,1)} %get-tuple-element.67.refs_0_, bf16[256,256]{1,0:T(8,128)(2,1)} %copy-done.44, bf16[256,256]{1,0:T(8,128)(2,1)} %copy-done.45, ...), custom_call_target="tpu_custom_call" | custom-call | flops 8589934592 | bytes 10485760 | tf_op jit(solution)/shard_map/attn_backward/pallas_call | solution.py:328
  370.4 3.9 collective-permute-done.39.refs_2_
  375.2 6.6 %attn_weight_grads.1 = bf16[8,1024,128]{2,1,0:T(8,128)(2,1)} custom-call(s32[8]{0:T(128)} %gather_fusion.2, s32[4]{0:T(128)} %copy-done.29, bf16[1024,1024]{1,0:T(8,128)(2,1)} %get-tuple-element.87.n1_ref, bf16[1024,256]{1,0:T(8,128)(2,1)} %get-tuple-element.75.dq_ref, bf16[1024,256]{1,0:T(8,128)(2,1)} %get-tuple-element.76.dk_ref, ...), custom_call_target="tpu_custom_call" | custom-call | flops 2147483648 | bytes 8388608 | tf_op jit(solution)/shard_map/attn_weight_grads/pallas_call | solution.py:677
  381.8 2.3 slice.178
  384.9 5.8 %projection_grads.1 = (bf16[256,1024]{1,0:T(8,128)(2,1)}, bf16[256,1024]{1,0:T(8,128)(2,1)}, bf16[256,1024]{1,0:T(8,128)(2,1)}, bf16[256,1024]{1,0:T(8,128)(2,1)}, f32[8,1024]{1,0:T(8,128)}) custom-call(s32[8]{0:T(128)} %copy-done.32, s32[4]{0:T(128)} %copy-done.29, bf16[1024,256]{1,0:T(8,128)(2,1)} %get-tuple-element.75.dq_ref, ...), custom_call_target="tpu_custom_call" | custom-call | flops 1610612736 | bytes 8388608 | tf_op jit(solution)/shard_map/projection_grads/pallas_call | solution.py:635
  391.4 3.4 collective-permute-start.33
  394.8 2.1 collective-permute-done.33
  396.9 2.0 collective-permute-start.34
  399.3 2.5 collective-permute-done.34
  401.8 1.9 collective-permute-start.21
  404.0 1.4 collective-permute-start.23
  405.5 3.9 collective-permute-done.36
  409.9 16.1 %collective-permute-done.21 = bf16[256,1024]{1,0:T(8,128)(2,1)} collective-permute-done((bf16[256,1024]{1,0:T(8,128)(2,1)}, bf16[256,1024]{1,0:T(8,128)(2,1)}, u32[]{:S(2)}, u32[]{:S(2)}) %collective-permute-start.21) | collective-permute-done | bytes 524320 | tf_op jit(solution)/shard_map/ppermute | solution.py:66
  426.0 13.1 %collective-permute-done.22 = bf16[256,1024]{1,0:T(8,128)(2,1)} collective-permute-done((bf16[256,1024]{1,0:T(8,128)(2,1)}, bf16[256,1024]{1,0:T(8,128)(2,1)}, u32[]{:S(2)}, u32[]{:S(2)}) %collective-permute-start.22) | collective-permute-done | bytes 524320 | tf_op jit(solution)/shard_map/ppermute | solution.py:66
  439.1 12.5 %collective-permute-done.23 = bf16[256,1024]{1,0:T(8,128)(2,1)} collective-permute-done((bf16[256,1024]{1,0:T(8,128)(2,1)}, bf16[256,1024]{1,0:T(8,128)(2,1)}, u32[]{:S(2)}, u32[]{:S(2)}) %collective-permute-start.23) | collective-permute-done | bytes 524320 | tf_op jit(solution)/shard_map/ppermute | solution.py:66
  451.5 2.5 add_convert_fusion.2
  454.0 2.1 collective-permute-start.31
  456.1 1.4 collective-permute-start.32
  459.6 15.6 %collective-permute-done.30.refs_1_ = bf16[256,1024]{1,0:T(8,128)(2,1)S(1)} collective-permute-done((bf16[256,1024]{1,0:T(8,128)(2,1)}, bf16[256,1024]{1,0:T(8,128)(2,1)S(1)}, u32[]{:S(2)}, u32[]{:S(2)}) %collective-permute-start.30) | collective-permute-done | bytes 524320 | tf_op jit(solution)/shard_map/ppermute | solution.py:66
  475.2 16.0 %collective-permute-done.31.refs_2_ = bf16[256,1024]{1,0:T(8,128)(2,1)S(1)} collective-permute-done((bf16[256,1024]{1,0:T(8,128)(2,1)}, bf16[256,1024]{1,0:T(8,128)(2,1)S(1)}, u32[]{:S(2)}, u32[]{:S(2)}) %collective-permute-start.31) | collective-permute-done | bytes 524320 | tf_op jit(solution)/shard_map/ppermute | solution.py:66
  491.2 11.2 %collective-permute-done.32.refs_3_ = bf16[256,1024]{1,0:T(8,128)(2,1)S(1)} collective-permute-done((bf16[256,1024]{1,0:T(8,128)(2,1)S(1)}, bf16[256,1024]{1,0:T(8,128)(2,1)S(1)}, u32[]{:S(2)}, u32[]{:S(2)}) %collective-permute-start.32) | collective-permute-done | bytes 524320 | tf_op jit(solution)/shard_map/ppermute | solution.py:66
  503.2 3.6 in_grad.1
  510.0 3.7 fusion.12
  (215 shorter events, 26.8 us)
Async XLA Ops:
  7.2 14.3 %copy-start = (f32[4,32]{1,0:T(4,128)S(1)}, f32[4,32]{1,0:T(4,128)}, u32[]{:S(2)}) copy-start(f32[4,32]{1,0:T(4,128)} %param.26) | copy-start | bytes 1540
  7.2 169.4 %all-gather.3.cloned.1.call-start = ((), (), s32[]{:S(2)}) async-start(), calls=%async_computation.2 | async-start | bytes 19464192 | tf_op jit(solution)/shard_map/all_gather | solution.py:741
  10.4 11.0 %copy-start.20 = (f32[32,1536]{1,0:T(8,128)S(1)}, f32[32,1536]{1,0:T(8,128)}, u32[]{:S(2)}) copy-start(f32[32,1536]{1,0:T(8,128)} %constant.53.clone) | copy-start | bytes 589828
  10.5 499.5 %reduce-scatter.2.cloned.1.call-start = ((), (), s32[]{:S(2)}) async-start(), calls=%async_computation.1 | async-start | bytes 19464192 | tf_op jit(solution)/shard_map/reduce_scatter | solution.py:788
  11.2 11.6 %collective-permute-start.9 = (bf16[256,128]{1,0:T(8,128)(2,1)S(1)}, bf16[256,128]{1,0:T(8,128)(2,1)S(1)}, u32[]{:S(2)}, u32[]{:S(2)}) collective-permute-start(bf16[256,128]{1,0:T(8,128)(2,1)S(1)} %copy-done.27), channel_id=1, source_target_pairs={{0,1},{1,0},{2,3},{3,2},{4,5},{5,4},{6,7},{7,6},{8,9},{9,8},{10,11... | collective-permute-start | bytes 196616 | tf_op jit(solution)/shard_map/ppermute | solution.py:66
  11.6 29.1 %collective-permute-start.11 = (bf16[256,128]{1,0:T(8,128)(2,1)S(1)}, bf16[256,128]{1,0:T(8,128)(2,1)S(1)}, u32[]{:S(2)}, u32[]{:S(2)}) collective-permute-start(bf16[256,128]{1,0:T(8,128)(2,1)S(1)} %copy-done.27), channel_id=1, source_target_pairs={{0,3},{1,2},{2,1},{3,0},{4,7},{5,6},{6,5},{7,4},{8,11},{9,10},{10,... | collective-permute-start | bytes 196616 | tf_op jit(solution)/shard_map/ppermute | solution.py:66
  14.3 28.5 %collective-permute-start.10 = (bf16[256,128]{1,0:T(8,128)(2,1)S(1)}, bf16[256,128]{1,0:T(8,128)(2,1)S(1)}, u32[]{:S(2)}, u32[]{:S(2)}) collective-permute-start(bf16[256,128]{1,0:T(8,128)(2,1)S(1)} %copy-done.27), channel_id=1, source_target_pairs={{0,2},{1,3},{2,0},{3,1},{4,6},{5,7},{6,4},{7,5},{8,10},{9,11},{10,... | collective-permute-start | bytes 196616 | tf_op jit(solution)/shard_map/ppermute | solution.py:66
  15.8 6.4 %collective-permute-start.3 = (bf16[1,144,768]{2,1,0:T(8,128)(2,1)S(1)}, bf16[1,144,768]{2,1,0:T(8,128)(2,1)S(1)}, u32[]{:S(2)}, u32[]{:S(2)}) collective-permute-start(bf16[1,144,768]{2,1,0:T(8,128)(2,1)S(1)} %maximum_bitcast_fusion.1), channel_id=1, source_target_pairs={{0,8},{4,12},{8,0},{12,4},{16,24},{20,28},{24,16},{28,20},{1,9},{5... | collective-permute-start | bytes 663560 | tf_op jit(solution)/shard_map/ppermute | solution.py:81
  16.4 58.9 %collective-permute-start.2 = (bf16[256,1024]{1,0:T(8,128)(2,1)S(1)}, bf16[256,1024]{1,0:T(8,128)(2,1)}, u32[]{:S(2)}, u32[]{:S(2)}) collective-permute-start(bf16[256,1024]{1,0:T(8,128)(2,1)S(1)} %copy-done.6), channel_id=1, source_target_pairs={{0,3},{1,2},{2,1},{3,0},{4,7},{5,6},{6,5},{7,4},{8,11},{9,10},{10,... | collective-permute-start | bytes 1572872 | tf_op jit(solution)/shard_map/ppermute | solution.py:66
  21.5 30.0 %copy-start.32 = (s32[8]{0:T(128)}, s32[8]{0:T(128)S(1)}, u32[]{:S(2)}) copy-start(s32[8]{0:T(128)S(1)} %gather_fusion) | copy-start | bytes 100
  22.2 21.5 %collective-permute-start.4 = (bf16[2,144,768]{2,1,0:T(8,128)(2,1)S(1)}, bf16[2,144,768]{2,1,0:T(8,128)(2,1)S(1)}, u32[]{:S(2)}, u32[]{:S(2)}) collective-permute-start(bf16[2,144,768]{2,1,0:T(8,128)(2,1)S(1)} %pad_maximum_fusion.6), channel_id=1, source_target_pairs={{0,16},{4,20},{8,24},{12,28},{16,0},{20,4},{24,8},{28,12},{1,17},{... | collective-permute-start | bytes 1327112 | tf_op jit(solution)/shard_map/ppermute | solution.py:81
  22.8 54.1 %collective-permute-start.1 = (bf16[256,1024]{1,0:T(8,128)(2,1)S(1)}, bf16[256,1024]{1,0:T(8,128)(2,1)}, u32[]{:S(2)}, u32[]{:S(2)}) collective-permute-start(bf16[256,1024]{1,0:T(8,128)(2,1)S(1)} %copy-done.6), channel_id=1, source_target_pairs={{0,2},{1,3},{2,0},{3,1},{4,6},{5,7},{6,4},{7,5},{8,10},{9,11},{10,... | collective-permute-start | bytes 1572872 | tf_op jit(solution)/shard_map/ppermute | solution.py:66
  40.7 36.3 %collective-permute-start = (bf16[256,1024]{1,0:T(8,128)(2,1)S(1)}, bf16[256,1024]{1,0:T(8,128)(2,1)}, u32[]{:S(2)}, u32[]{:S(2)}) collective-permute-start(bf16[256,1024]{1,0:T(8,128)(2,1)S(1)} %copy-done.6), channel_id=1, source_target_pairs={{0,1},{1,0},{2,3},{3,2},{4,5},{5,4},{6,7},{7,6},{8,9},{9,8},{10,11... | collective-permute-start | bytes 1572872 | tf_op jit(solution)/shard_map/ppermute | solution.py:66
  42.8 8.6 %collective-permute-start.12 = (bf16[1,4,256,128]{3,2,1,0:T(8,128)(2,1)S(1)}, bf16[1,4,256,128]{3,2,1,0:T(8,128)(2,1)S(1)}, u32[]{:S(2)}, u32[]{:S(2)}) collective-permute-start(bf16[1,4,256,128]{3,2,1,0:T(8,128)(2,1)S(1)} %maximum_bitcast_fusion), channel_id=1, source_target_pairs={{0,8},{4,12},{8,0},{12,4},{16,24},{20,28},{24,16},{28,20},{1,9},{5... | collective-permute-start | bytes 786440 | tf_op jit(solution)/shard_map/ppermute | solution.py:81
  42.9 29.7 %copy-start.29 = (s32[4]{0:T(128)}, s32[4]{0:T(128)S(1)}, u32[]{:S(2)}) copy-start(s32[4]{0:T(128)S(1)} %iota_xor_fusion.place_ref) | copy-start | bytes 52
  44.7 27.9 %collective-permute-start.5 = (bf16[4,144,768]{2,1,0:T(8,128)(2,1)}, bf16[4,144,768]{2,1,0:T(8,128)(2,1)S(1)}, u32[]{:S(2)}, u32[]{:S(2)}) collective-permute-start(bf16[4,144,768]{2,1,0:T(8,128)(2,1)} %pad_maximum_fusion.4), channel_id=1, source_target_pairs={{0,4},{4,0},{8,12},{12,8},{16,20},{20,16},{24,28},{28,24},{1,5},{5... | collective-permute-start | bytes 2654216 | tf_op jit(solution)/shard_map/ppermute | solution.py:81
  51.4 18.7 %collective-permute-start.13 = (bf16[2,4,256,128]{3,2,1,0:T(8,128)(2,1)S(1)}, bf16[2,4,256,128]{3,2,1,0:T(8,128)(2,1)S(1)}, u32[]{:S(2)}, u32[]{:S(2)}) collective-permute-start(bf16[2,4,256,128]{3,2,1,0:T(8,128)(2,1)S(1)} %pad_maximum_fusion.5), channel_id=1, source_target_pairs={{0,16},{4,20},{8,24},{12,28},{16,0},{20,4},{24,8},{28,12},{1,17},{... | collective-permute-start | bytes 1572872 | tf_op jit(solution)/shard_map/ppermute | solution.py:81
  70.1 66.1 %collective-permute-start.20 = (bf16[256,1024]{1,0:T(8,128)(2,1)}, bf16[256,1024]{1,0:T(8,128)(2,1)}, u32[]{:S(2)}, u32[]{:S(2)}) collective-permute-start(bf16[256,1024]{1,0:T(8,128)(2,1)} %refs_7_.1), channel_id=1, source_target_pairs={{0,3},{1,2},{2,1},{3,0},{4,7},{5,6},{6,5},{7,4},{8,11},{9,10},{10,... | collective-permute-start | bytes 1572872 | tf_op jit(solution)/shard_map/ppermute | solution.py:66
  72.6 31.4 %collective-permute-start.14 = (bf16[4,4,256,128]{3,2,1,0:T(8,128)(2,1)}, bf16[4,4,256,128]{3,2,1,0:T(8,128)(2,1)}, u32[]{:S(2)}, u32[]{:S(2)}) collective-permute-start(bf16[4,4,256,128]{3,2,1,0:T(8,128)(2,1)} %pad_maximum_fusion.3), channel_id=1, source_target_pairs={{0,4},{4,0},{8,12},{12,8},{16,20},{20,16},{24,28},{28,24},{1,5},{5... | collective-permute-start | bytes 3145736 | tf_op jit(solution)/shard_map/ppermute | solution.py:81
  75.3 63.3 %collective-permute-start.19 = (bf16[256,1024]{1,0:T(8,128)(2,1)}, bf16[256,1024]{1,0:T(8,128)(2,1)S(1)}, u32[]{:S(2)}, u32[]{:S(2)}) collective-permute-start(bf16[256,1024]{1,0:T(8,128)(2,1)} %refs_7_.1), channel_id=1, source_target_pairs={{0,2},{1,3},{2,0},{3,1},{4,6},{5,7},{6,4},{7,5},{8,10},{9,11},{10,... | collective-permute-start | bytes 1572872 | tf_op jit(solution)/shard_map/ppermute | solution.py:66
  101.3 24.5 %collective-permute-start.8 = (bf16[256,256]{1,0:T(8,128)(2,1)S(1)}, bf16[256,256]{1,0:T(8,128)(2,1)S(1)}, u32[]{:S(2)}, u32[]{:S(2)}) collective-permute-start(bf16[256,256]{1,0:T(8,128)(2,1)S(1)} %get-tuple-element.98), channel_id=1, source_target_pairs={{0,3},{1,2},{2,1},{3,0},{4,7},{5,6},{6,5},{7,4},{8,11},{9,10},{10,... | collective-permute-start | bytes 393224 | tf_op jit(solution)/shard_map/ppermute | solution.py:66
  102.3 24.0 %collective-permute-start.7 = (bf16[256,256]{1,0:T(8,128)(2,1)S(1)}, bf16[256,256]{1,0:T(8,128)(2,1)S(1)}, u32[]{:S(2)}, u32[]{:S(2)}) collective-permute-start(bf16[256,256]{1,0:T(8,128)(2,1)S(1)} %get-tuple-element.99), channel_id=1, source_target_pairs={{0,2},{1,3},{2,0},{3,1},{4,6},{5,7},{6,4},{7,5},{8,10},{9,11},{10,... | collective-permute-start | bytes 393224 | tf_op jit(solution)/shard_map/ppermute | solution.py:66
  104.0 21.8 %copy-start.8 = (bf16[256,1024]{1,0:T(8,128)(2,1)S(1)}, bf16[256,1024]{1,0:T(8,128)(2,1)}, u32[]{:S(2)}) copy-start(bf16[256,1024]{1,0:T(8,128)(2,1)} %refs_7_.1) | copy-start | bytes 1572868
  104.0 22.3 %collective-permute-start.6 = (bf16[256,256]{1,0:T(8,128)(2,1)S(1)}, bf16[256,256]{1,0:T(8,128)(2,1)S(1)}, u32[]{:S(2)}, u32[]{:S(2)}) collective-permute-start(bf16[256,256]{1,0:T(8,128)(2,1)S(1)} %get-tuple-element.100), channel_id=1, source_target_pairs={{0,1},{1,0},{2,3},{3,2},{4,5},{5,4},{6,7},{7,6},{8,9},{9,8},{10,11... | collective-permute-start | bytes 393224 | tf_op jit(solution)/shard_map/ppermute | solution.py:66
  125.8 13.3 %collective-permute-start.18 = (bf16[256,1024]{1,0:T(8,128)(2,1)S(1)}, bf16[256,1024]{1,0:T(8,128)(2,1)S(1)}, u32[]{:S(2)}, u32[]{:S(2)}) collective-permute-start(bf16[256,1024]{1,0:T(8,128)(2,1)S(1)} %copy-done.8), channel_id=1, source_target_pairs={{0,1},{1,0},{2,3},{3,2},{4,5},{5,4},{6,7},{7,6},{8,9},{9,8},{10,11... | collective-permute-start | bytes 1572872 | tf_op jit(solution)/shard_map/ppermute | solution.py:66
  130.9 37.5 %collective-permute-start.17 = (bf16[256,1024]{1,0:T(8,128)(2,1)}, bf16[256,1024]{1,0:T(8,128)(2,1)S(1)}, u32[]{:S(2)}, u32[]{:S(2)}) collective-permute-start(bf16[256,1024]{1,0:T(8,128)(2,1)} %get-tuple-element.58.refs_0_.refs_3_), channel_id=1, source_target_pairs={{0,3},{1,2},{2,1},{3,0},{4,7},{5,6},{6,5},{7,4},{8,11},{9,10},{10,... | collective-permute-start | bytes 1572872 | tf_op jit(solution)/shard_map/ppermute | solution.py:66
  131.8 44.7 %collective-permute-start.16 = (bf16[256,1024]{1,0:T(8,128)(2,1)}, bf16[256,1024]{1,0:T(8,128)(2,1)S(1)}, u32[]{:S(2)}, u32[]{:S(2)}) collective-permute-start(bf16[256,1024]{1,0:T(8,128)(2,1)} %get-tuple-element.58.refs_0_.refs_3_), channel_id=1, source_target_pairs={{0,2},{1,3},{2,0},{3,1},{4,6},{5,7},{6,4},{7,5},{8,10},{9,11},{10,... | collective-permute-start | bytes 1572872 | tf_op jit(solution)/shard_map/ppermute | solution.py:66
  136.2 40.4 %collective-permute-start.15 = (bf16[256,1024]{1,0:T(8,128)(2,1)}, bf16[256,1024]{1,0:T(8,128)(2,1)}, u32[]{:S(2)}, u32[]{:S(2)}) collective-permute-start(bf16[256,1024]{1,0:T(8,128)(2,1)} %get-tuple-element.58.refs_0_.refs_3_), channel_id=1, source_target_pairs={{0,1},{1,0},{2,3},{3,2},{4,5},{5,4},{6,7},{7,6},{8,9},{9,8},{10,11... | collective-permute-start | bytes 1572872 | tf_op jit(solution)/shard_map/ppermute | solution.py:66
  138.6 38.0 %copy-start.37 = (bf16[256,1024]{1,0:T(8,128)(2,1)}, bf16[256,1024]{1,0:T(8,128)(2,1)S(1)}, u32[]{:S(2)}) copy-start(bf16[256,1024]{1,0:T(8,128)(2,1)S(1)} %collective-permute-done.19.refs_6_.refs_9_) | copy-start | bytes 1572868
  139.1 37.5 %copy-start.38 = (bf16[256,1024]{1,0:T(8,128)(2,1)}, bf16[256,1024]{1,0:T(8,128)(2,1)S(1)}, u32[]{:S(2)}) copy-start(bf16[256,1024]{1,0:T(8,128)(2,1)S(1)} %collective-permute-done.18.refs_5_.refs_8_) | copy-start | bytes 1572868
  261.8 24.1 %collective-permute-start.24 = (bf16[256,1024]{1,0:T(8,128)(2,1)S(1)}, bf16[256,1024]{1,0:T(8,128)(2,1)S(1)}, u32[]{:S(2)}, u32[]{:S(2)}) collective-permute-start(bf16[256,1024]{1,0:T(8,128)(2,1)S(1)} %copy-done.43), channel_id=1, source_target_pairs={{0,1},{1,0},{2,3},{3,2},{4,5},{5,4},{6,7},{7,6},{8,9},{9,8},{10,11... | collective-permute-start | bytes 1572872 | tf_op jit(solution)/shard_map/ppermute | solution.py:66
  265.3 34.9 %collective-permute-start.25 = (bf16[256,1024]{1,0:T(8,128)(2,1)S(1)}, bf16[256,1024]{1,0:T(8,128)(2,1)S(1)}, u32[]{:S(2)}, u32[]{:S(2)}) collective-permute-start(bf16[256,1024]{1,0:T(8,128)(2,1)S(1)} %copy-done.42), channel_id=1, source_target_pairs={{0,2},{1,3},{2,0},{3,1},{4,6},{5,7},{6,4},{7,5},{8,10},{9,11},{10,... | collective-permute-start | bytes 1572872 | tf_op jit(solution)/shard_map/ppermute | solution.py:66
  265.3 46.3 %collective-permute-start.26 = (bf16[256,1024]{1,0:T(8,128)(2,1)S(1)}, bf16[256,1024]{1,0:T(8,128)(2,1)S(1)}, u32[]{:S(2)}, u32[]{:S(2)}) collective-permute-start(bf16[256,1024]{1,0:T(8,128)(2,1)S(1)} %copy-done.41), channel_id=1, source_target_pairs={{0,3},{1,2},{2,1},{3,0},{4,7},{5,6},{6,5},{7,4},{8,11},{9,10},{10,... | collective-permute-start | bytes 1572872 | tf_op jit(solution)/shard_map/ppermute | solution.py:66
  285.9 25.8 %copy-start.16 = (bf16[256,1024]{1,0:T(8,128)(2,1)}, bf16[256,1024]{1,0:T(8,128)(2,1)S(1)}, u32[]{:S(2)}) copy-start(bf16[256,1024]{1,0:T(8,128)(2,1)S(1)} %collective-permute-done.24.refs_1_) | copy-start | bytes 1572868
  300.2 11.5 %copy-start.17 = (bf16[256,1024]{1,0:T(8,128)(2,1)}, bf16[256,1024]{1,0:T(8,128)(2,1)S(1)}, u32[]{:S(2)}) copy-start(bf16[256,1024]{1,0:T(8,128)(2,1)S(1)} %collective-permute-done.25.refs_2_) | copy-start | bytes 1572868
  317.7 8.0 %collective-permute-start.27 = (bf16[256,256]{1,0:T(8,128)(2,1)}, bf16[256,256]{1,0:T(8,128)(2,1)S(1)}, u32[]{:S(2)}, u32[]{:S(2)}) collective-permute-start(bf16[256,256]{1,0:T(8,128)(2,1)} %get-tuple-element.68), channel_id=1, source_target_pairs={{0,1},{1,0},{2,3},{3,2},{4,5},{5,4},{6,7},{7,6},{8,9},{9,8},{10,11... | collective-permute-start | bytes 393224 | tf_op jit(solution)/shard_map/ppermute | solution.py:66
  317.7 30.8 %collective-permute-start.28 = (bf16[256,256]{1,0:T(8,128)(2,1)}, bf16[256,256]{1,0:T(8,128)(2,1)S(1)}, u32[]{:S(2)}, u32[]{:S(2)}) collective-permute-start(bf16[256,256]{1,0:T(8,128)(2,1)} %get-tuple-element.69), channel_id=1, source_target_pairs={{0,2},{1,3},{2,0},{3,1},{4,6},{5,7},{6,4},{7,5},{8,10},{9,11},{10,... | collective-permute-start | bytes 393224 | tf_op jit(solution)/shard_map/ppermute | solution.py:66
  319.4 35.4 %collective-permute-start.29 = (bf16[256,256]{1,0:T(8,128)(2,1)}, bf16[256,256]{1,0:T(8,128)(2,1)S(1)}, u32[]{:S(2)}, u32[]{:S(2)}) collective-permute-start(bf16[256,256]{1,0:T(8,128)(2,1)} %get-tuple-element.70), channel_id=1, source_target_pairs={{0,3},{1,2},{2,1},{3,0},{4,7},{5,6},{6,5},{7,4},{8,11},{9,10},{10,... | collective-permute-start | bytes 393224 | tf_op jit(solution)/shard_map/ppermute | solution.py:66
  322.3 48.0 %collective-permute-start.40 = (bf16[256,1024]{1,0:T(8,128)(2,1)}, bf16[256,1024]{1,0:T(8,128)(2,1)S(1)}, u32[]{:S(2)}, u32[]{:S(2)}) collective-permute-start(bf16[256,1024]{1,0:T(8,128)(2,1)} %get-tuple-element.89.refs_0_), channel_id=1, source_target_pairs={{0,3},{1,2},{2,1},{3,0},{4,7},{5,6},{6,5},{7,4},{8,11},{9,10},{10,... | collective-permute-start | bytes 1572872 | tf_op jit(solution)/shard_map/ppermute | solution.py:66
  322.6 51.7 %collective-permute-start.39 = (bf16[256,1024]{1,0:T(8,128)(2,1)}, bf16[256,1024]{1,0:T(8,128)(2,1)S(1)}, u32[]{:S(2)}, u32[]{:S(2)}) collective-permute-start(bf16[256,1024]{1,0:T(8,128)(2,1)} %get-tuple-element.89.refs_0_), channel_id=1, source_target_pairs={{0,2},{1,3},{2,0},{3,1},{4,6},{5,7},{6,4},{7,5},{8,10},{9,11},{10,... | collective-permute-start | bytes 1572872 | tf_op jit(solution)/shard_map/ppermute | solution.py:66
  325.6 29.1 %copy-start.44 = (bf16[256,256]{1,0:T(8,128)(2,1)}, bf16[256,256]{1,0:T(8,128)(2,1)S(1)}, u32[]{:S(2)}) copy-start(bf16[256,256]{1,0:T(8,128)(2,1)S(1)} %collective-permute-done.27.refs_1_) | copy-start | bytes 393220
  325.6 48.6 %collective-permute-start.38 = (bf16[256,1024]{1,0:T(8,128)(2,1)}, bf16[256,1024]{1,0:T(8,128)(2,1)S(1)}, u32[]{:S(2)}, u32[]{:S(2)}) collective-permute-start(bf16[256,1024]{1,0:T(8,128)(2,1)} %get-tuple-element.89.refs_0_), channel_id=1, source_target_pairs={{0,1},{1,0},{2,3},{3,2},{4,5},{5,4},{6,7},{7,6},{8,9},{9,8},{10,11... | collective-permute-start | bytes 1572872 | tf_op jit(solution)/shard_map/ppermute | solution.py:66
  384.1 25.4 %collective-permute-start.41 = (bf16[4,1024,128]{2,1,0:T(8,128)(2,1)}, bf16[4,1024,128]{2,1,0:T(8,128)(2,1)S(1)}, u32[]{:S(2)}, u32[]{:S(2)}) collective-permute-start(bf16[4,1024,128]{2,1,0:T(8,128)(2,1)} %slice.178), channel_id=1, source_target_pairs={{0,4},{4,0},{8,12},{12,8},{16,20},{20,16},{24,28},{28,24},{1,5},{5... | collective-permute-start | bytes 3145736 | tf_op jit(solution)/shard_map/ppermute | solution.py:93
  384.9 14.0 %copy-start.19 = (f32[5,512,32]{1,2,0:T(8,128)S(1)}, f32[5,512,32]{1,2,0:T(8,128)}, u32[]{:S(2)}) copy-start(f32[5,512,32]{1,2,0:T(8,128)} %constant.55.clone) | copy-start | bytes 983044
  384.9 14.0 %copy-start.28 = (f32[4,5,512]{2,1,0:T(8,128)S(1)}, f32[4,5,512]{2,1,0:T(8,128)}, u32[]{:S(2)}) copy-start(f32[4,5,512]{2,1,0:T(8,128)} %get-tuple-element.86) | copy-start | bytes 122884
  384.9 24.6 %copy-start.4 = (bf16[8,1024,128]{2,1,0:T(8,128)(2,1)S(1)}, bf16[8,1024,128]{2,1,0:T(8,128)(2,1)}, u32[]{:S(2)}) copy-start(bf16[8,1024,128]{2,1,0:T(8,128)(2,1)} %attn_weight_grads.1) | copy-start | bytes 6291460
  391.4 5.4 %collective-permute-start.33 = (f32[6,1024]{1,0:T(8,128)S(1)}, f32[6,1024]{1,0:T(8,128)S(1)}, u32[]{:S(2)}, u32[]{:S(2)}) collective-permute-start(f32[6,1024]{1,0:T(8,128)S(1)} %pad_maximum_fusion.7), channel_id=1, source_target_pairs={{0,1},{1,0},{2,3},{3,2},{4,5},{5,4},{6,7},{7,6},{8,9},{9,8},{10,11... | collective-permute-start | bytes 73736 | tf_op jit(solution)/shard_map/ppermute | solution.py:66
  396.9 4.9 collective-permute-start.34
  401.8 3.6 collective-permute-start.35
  401.8 24.2 %collective-permute-start.21 = (bf16[256,1024]{1,0:T(8,128)(2,1)}, bf16[256,1024]{1,0:T(8,128)(2,1)}, u32[]{:S(2)}, u32[]{:S(2)}) collective-permute-start(bf16[256,1024]{1,0:T(8,128)(2,1)} %get-tuple-element.60), channel_id=1, source_target_pairs={{0,1},{1,0},{2,3},{3,2},{4,5},{5,4},{6,7},{7,6},{8,9},{9,8},{10,11... | collective-permute-start | bytes 1572872 | tf_op jit(solution)/shard_map/ppermute | solution.py:66
  403.8 35.3 %collective-permute-start.22 = (bf16[256,1024]{1,0:T(8,128)(2,1)}, bf16[256,1024]{1,0:T(8,128)(2,1)}, u32[]{:S(2)}, u32[]{:S(2)}) collective-permute-start(bf16[256,1024]{1,0:T(8,128)(2,1)} %get-tuple-element.61), channel_id=1, source_target_pairs={{0,2},{1,3},{2,0},{3,1},{4,6},{5,7},{6,4},{7,5},{8,10},{9,11},{10,... | collective-permute-start | bytes 1572872 | tf_op jit(solution)/shard_map/ppermute | solution.py:66
  404.0 47.6 %collective-permute-start.23 = (bf16[256,1024]{1,0:T(8,128)(2,1)}, bf16[256,1024]{1,0:T(8,128)(2,1)}, u32[]{:S(2)}, u32[]{:S(2)}) collective-permute-start(bf16[256,1024]{1,0:T(8,128)(2,1)} %get-tuple-element.62), channel_id=1, source_target_pairs={{0,3},{1,2},{2,1},{3,0},{4,7},{5,6},{6,5},{7,4},{8,11},{9,10},{10,... | collective-permute-start | bytes 1572872 | tf_op jit(solution)/shard_map/ppermute | solution.py:66
  405.4 4.0 collective-permute-start.36
  409.4 42.1 %copy-start.5 = (f32[256,1024]{1,0:T(8,128)S(1)}, f32[256,1024]{1,0:T(8,128)}, u32[]{:S(2)}) copy-start(f32[256,1024]{1,0:T(8,128)} %get-tuple-element.57.refs_4_) | copy-start | bytes 3145732
  409.4 42.1 %copy-start.9 = (bf16[256,1024]{1,0:T(8,128)(2,1)S(1)}, bf16[256,1024]{1,0:T(8,128)(2,1)}, u32[]{:S(2)}) copy-start(bf16[256,1024]{1,0:T(8,128)(2,1)} %get-tuple-element.59) | copy-start | bytes 1572868
  409.4 48.1 %collective-permute-start.37 = (f32[7,1024]{1,0:T(8,128)S(1)}, f32[7,1024]{1,0:T(8,128)S(1)}, u32[]{:S(2)}, u32[]{:S(2)}) collective-permute-start(f32[7,1024]{1,0:T(8,128)S(1)} %add.121), channel_id=1, source_target_pairs={{0,16},{4,20},{8,24},{12,28},{16,0},{20,4},{24,8},{28,12},{1,17},{... | collective-permute-start | bytes 86024 | tf_op jit(solution)/shard_map/ppermute | solution.py:831
  409.8 46.2 %copy-start.36 = (bf16[256,1024]{1,0:T(8,128)(2,1)S(1)}, bf16[256,1024]{1,0:T(8,128)(2,1)}, u32[]{:S(2)}) copy-start(bf16[256,1024]{1,0:T(8,128)(2,1)} %get-tuple-element.81) | copy-start | bytes 1572868
  409.8 48.3 %collective-permute-start.42 = (bf16[2,1024,128]{2,1,0:T(8,128)(2,1)S(1)}, bf16[2,1024,128]{2,1,0:T(8,128)(2,1)S(1)}, u32[]{:S(2)}, u32[]{:S(2)}) collective-permute-start(bf16[2,1024,128]{2,1,0:T(8,128)(2,1)S(1)} %slice.180), channel_id=1, source_target_pairs={{0,8},{4,12},{8,0},{12,4},{16,24},{20,28},{24,16},{28,20},{1,9},{5... | collective-permute-start | bytes 1572872 | tf_op jit(solution)/shard_map/ppermute | solution.py:93
  454.0 21.2 %collective-permute-start.30 = (bf16[256,1024]{1,0:T(8,128)(2,1)}, bf16[256,1024]{1,0:T(8,128)(2,1)S(1)}, u32[]{:S(2)}, u32[]{:S(2)}) collective-permute-start(bf16[256,1024]{1,0:T(8,128)(2,1)} %get-tuple-element.79), channel_id=1, source_target_pairs={{0,1},{1,0},{2,3},{3,2},{4,5},{5,4},{6,7},{7,6},{8,9},{9,8},{10,11... | collective-permute-start | bytes 1572872 | tf_op jit(solution)/shard_map/ppermute | solution.py:66
  454.0 37.2 %collective-permute-start.31 = (bf16[256,1024]{1,0:T(8,128)(2,1)}, bf16[256,1024]{1,0:T(8,128)(2,1)S(1)}, u32[]{:S(2)}, u32[]{:S(2)}) collective-permute-start(bf16[256,1024]{1,0:T(8,128)(2,1)} %get-tuple-element.80), channel_id=1, source_target_pairs={{0,2},{1,3},{2,0},{3,1},{4,6},{5,7},{6,4},{7,5},{8,10},{9,11},{10,... | collective-permute-start | bytes 1572872 | tf_op jit(solution)/shard_map/ppermute | solution.py:66
  456.1 46.4 %collective-permute-start.32 = (bf16[256,1024]{1,0:T(8,128)(2,1)S(1)}, bf16[256,1024]{1,0:T(8,128)(2,1)S(1)}, u32[]{:S(2)}, u32[]{:S(2)}) collective-permute-start(bf16[256,1024]{1,0:T(8,128)(2,1)S(1)} %copy-done.36), channel_id=1, source_target_pairs={{0,3},{1,2},{2,1},{3,0},{4,7},{5,6},{6,5},{7,4},{8,11},{9,10},{10,... | collective-permute-start | bytes 1572872 | tf_op jit(solution)/shard_map/ppermute | solution.py:66
  458.3 48.5 %collective-permute-start.43 = (bf16[1,1024,128]{2,1,0:T(8,128)(2,1)S(1)}, bf16[1,1024,128]{2,1,0:T(8,128)(2,1)S(1)}, u32[]{:S(2)}, u32[]{:S(2)}) collective-permute-start(bf16[1,1024,128]{2,1,0:T(8,128)(2,1)S(1)} %slice.182), channel_id=1, source_target_pairs={{0,16},{4,20},{8,24},{12,28},{16,0},{20,4},{24,8},{28,12},{1,17},{... | collective-permute-start | bytes 786440 | tf_op jit(solution)/shard_map/ppermute | solution.py:93
  475.2 27.3 %copy-start.10 = (bf16[256,1024]{1,0:T(8,128)(2,1)}, bf16[256,1024]{1,0:T(8,128)(2,1)S(1)}, u32[]{:S(2)}) copy-start(bf16[256,1024]{1,0:T(8,128)(2,1)S(1)} %collective-permute-done.30.refs_1_) | copy-start | bytes 1572868
  491.2 11.2 %copy-start.11 = (bf16[256,1024]{1,0:T(8,128)(2,1)}, bf16[256,1024]{1,0:T(8,128)(2,1)S(1)}, u32[]{:S(2)}) copy-start(bf16[256,1024]{1,0:T(8,128)(2,1)S(1)} %collective-permute-done.31.refs_2_) | copy-start | bytes 1572868
  (29 other events, 107.9 us)
Sparse Core Ops, SparseCore 0:
  10.6 105.1 all-gather.2
  260.9 119.4 reduce-scatter.1

commit v2 on v1

--- a/solution.py
+++ b/solution.py
@@ -67,32 +67,42 @@
 
 
 def z_gather(x, size):
-    return [x] + [z_swap(x, mask, size) for mask in range(1, size)]
-
-
-def dp_slots(size):
-    if size == 8:
-        return np.array([((k >> 1) & 3) | ((k & 1) << 2) for k in range(8)], np.int32)
-    return None
-
-
-def dp_gather(x):
-    for bit in (2, 4, 1):
-        other = lax.ppermute(x, "dp", [(i, i ^ bit) for i in range(8)])
-        x = jnp.concatenate([x, other], 0)
-    return x
-
-
-def dp_scatter_slots():
-    return np.array([((k & 1) << 2) | (((k >> 1) & 1) << 1) | ((k >> 2) & 1) for k in range(8)], np.int32)
-
-
-def dp_scatter(x):
-    for bit in (1, 2, 4):
-        half = x.shape[0] // 2
-        other = lax.ppermute(x[half:], "dp", [(i, i ^ bit) for i in range(8)])
-        x = (x[:half].astype(F32) + other.astype(F32)).astype(x.dtype)
-    return x[0]
+    near = z_swap(x, 1, size)
+    far = z_swap(x, 2, size)
+    return [x, near, far, z_swap(far, 1, size)]
+
+
+def z_direct(parts, size):
+    return [parts[0]] + [z_swap(parts[mask], mask, size) for mask in range(1, size)]
+
+
+def z_reduce(parts, size):
+    passed = z_swap(parts[3], 1, size)
+    far = z_swap((parts[2].astype(F32) + passed.astype(F32)).astype(BF), 2, size)
+    return [parts[0], z_swap(parts[1], 1, size), far]
+
+
+def after(x, *others):
+    return lax.optimization_barrier((x,) + others)[0]
+
+
+def dp_slots(ranks):
+    return ((ranks >> 1) & 3) | ((ranks & 1) << 2)
+
+
+def dp_step(x, bit):
+    other = lax.ppermute(x, "dp", [(i, i ^ bit) for i in range(8)])
+    return jnp.concatenate([x, other], 0)
+
+
+def dp_fold(x, bit):
+    half = x.shape[0] // 2
+    other = lax.ppermute(x[half:], "dp", [(i, i ^ bit) for i in range(8)])
+    return (x[:half].astype(F32) + other.astype(F32)).astype(x.dtype)
+
+
+def dp_scatter_slots(ranks):
+    return ((ranks & 1) << 2) | (((ranks >> 1) & 1) << 1) | ((ranks >> 2) & 1)
 
 
 def join_rows(ref, index_ref, count, rows):
@@ -103,12 +113,24 @@
 
 def qkv_body(count, chunks, rows, index_ref, place_ref, *refs):
     toks = refs[:chunks]
-    pack_ref, gain_ref = refs[chunks : chunks + 2]
-    n1_ref, q_ref, k_ref, v_ref, kt_ref, vt_ref = refs[chunks + 2 :]
+    pack_ref, small_ref = refs[chunks : chunks + 2]
+    n1_ref, q_ref, k_ref, v_ref, kt_ref, vt_ref, gains_ref, router_ref = refs[chunks + 2 :]
     depth = n1_ref.shape[1] // count
     weights = join_rows(pack_ref, index_ref, count, depth)
     width = q_ref.shape[1]
-    gain = gain_ref[0:1, :]
+    if count == 1:
+        small = [small_ref[r : r + 1, :] for r in range(2 + EXPERTS)]
+    else:
+        lines = [small_ref[index_ref[d], depth : depth + 1, :].astype(F32) for d in range(count)]
+        small = [
+            jnp.concatenate([x[:, depth * r : depth * (r + 1)] for x in lines], 1) for r in range(2 + EXPERTS)
+        ]
+    small = jnp.concatenate([x.astype(F32) for x in small] + [jnp.zeros((2, depth * count), F32)], 0)
+    gains_ref[...] = small
+    routers = jnp.concatenate([small[2:], jnp.zeros((10, depth * count), F32)], 0)
+    router_ref[...] = jnp.zeros_like(router_ref)
+    router_ref[0:16, :] = routers.astype(BF)
+    gain = small[0:1, :]
     for c in range(chunks):
         at = pl.ds(pl.multiple_of(place_ref[c] * rows, rows), rows)
         x = toks[c][...].astype(F32)
@@ -125,19 +147,20 @@
         vt_ref[:, at] = jnp.transpose(value).astype(BF)
 
 
-def qkv_call(index, place, toks, pack, gain, width):
+def qkv_call(index, place, toks, pack, small, width):
     chunks, rows, depth = len(toks), toks[0].shape[0], toks[0].shape[1]
     total = chunks * rows
     shapes = [(total, depth)] + [(total, width)] * 3 + [(width, total)] * 2
     return pl.pallas_call(
         functools.partial(qkv_body, pack.shape[0], chunks, rows),
         in_specs=[sspec(), sspec()] + [vspec()] * (chunks + 2),
-        out_specs=[vspec()] * 6,
-        out_shape=[jax.ShapeDtypeStruct(s, BF) for s in shapes],
+        out_specs=[vspec()] * 8,
+        out_shape=[jax.ShapeDtypeStruct(s, BF) for s in shapes]
+        + [jax.ShapeDtypeStruct((8, depth), F32), jax.ShapeDtypeStruct((128, depth), BF)],
         compiler_params=params(),
         cost_estimate=cost(2 * total * depth * 3 * width, 8 * total * depth),
         name="norm_qkv",
-    )(index, place, *toks, pack, gain)
+    )(index, place, *toks, pack, small)
 
 
 def extents(total):
@@ -145,7 +168,7 @@
     return [(i, min(BLOCK * (i + 2), total)) for i in range(blocks)]
 
 
-def fwd_body(total, starts_ref, q_ref, k_ref, vt_ref, line_ref, p_ref, ot_ref, att_ref, attt_ref, strip_ref, mask_ref):
+def fwd_body(total, starts_ref, q_ref, k_ref, vt_ref, line_ref, p_ref, ot_ref, att_ref, strip_ref, mask_ref):
     head = pl.program_id(0)
     heads = pl.num_programs(0)
     blocks = total // BLOCK
@@ -201,7 +224,6 @@
     @pl.when(head == heads - 1)
     def _():
         mixed = ot_ref[...]
-        attt_ref[...] = mixed.astype(BF)
         att_ref[...] = jnp.transpose(mixed).astype(BF)
 
 
@@ -224,13 +246,11 @@
             pl.BlockSpec((1, total, total), lambda h: (h, 0, 0)),
             whole((width, total)),
             whole((total, width)),
-            whole((width, total)),
         ],
         out_shape=[
             jax.ShapeDtypeStruct((heads, total, total), BF),
             jax.ShapeDtypeStruct((width, total), F32),
             jax.ShapeDtypeStruct((total, width), BF),
-            jax.ShapeDtypeStruct((width, total), BF),
         ],
         scratch_shapes=[
             pltpu.VMEM((BLOCK * (blocks + 1), BLOCK), F32),
@@ -346,7 +366,7 @@
             pltpu.VMEM((BLOCK * (blocks + 1), BLOCK), F32),
         ],
         compiler_params=params(("arbitrary",)),
-        cost_estimate=cost(heads * 8 * total * total * width, 10 * total * total),
+        cost_estimate=cost(heads * 160 * total * total * width, 10 * total * total),
         name="attn_backward",
     )(place, *grads, chances, q, k, v, kt, ot)
 
@@ -387,161 +407,182 @@
     return dot(high, b) + dot(low, b)
 
 
-def moe_body(count, chunks, unit, place_ref, *refs):
+def joined(ref, which):
+    if ref.shape[0] == 1:
+        return ref[0, which]
+    return jnp.concatenate([ref[d, which] for d in range(ref.shape[0])], 1)
+
+
+def units_body(chunks, unit, place_ref, *refs):
     n2s = refs[:chunks]
     gs = refs[chunks : 2 * chunks]
     sel_ref, rout_ref, w_ref = refs[2 * chunks : 2 * chunks + 3]
-    rest = refs[2 * chunks + 3 :]
-    outs = rest[:chunks]
-    ngs = rest[chunks : 2 * chunks]
-    hg_ref, gg_ref, ug_ref, rpart_ref = rest[2 * chunks : 2 * chunks + 4]
-    out_acc, ng_acc, gate_ref, sum_ref, prob_ref = rest[2 * chunks + 4 :]
+    hg_ref, gg_ref, ug_ref, lg_ref, rpart_ref = refs[2 * chunks + 3 : 2 * chunks + 8]
+    n2_ref, g_ref, gate_ref, sum_ref, prob_ref, pick_ref = refs[2 * chunks + 8 :]
     step = pl.program_id(0)
     steps = pl.num_programs(0)
     rows = n2s[0].shape[0]
-    fb = hg_ref.shape[1]
-    lane = lax.broadcasted_iota(jnp.int32, (rows, 128), 1)
+    tokens = chunks * rows
+    lane = lax.broadcasted_iota(jnp.int32, (tokens, 128), 1)
 
     @pl.when(step == 0)
     def _():
-        out_acc[...] = jnp.zeros_like(out_acc)
-        ng_acc[...] = jnp.zeros_like(ng_acc)
+        for c in range(chunks):
+            n2_ref[rows * c : rows * (c + 1), :] = n2s[c][...]
+            g_ref[rows * c : rows * (c + 1), :] = gs[c][...]
+        logits = dot_nt(n2_ref[...], rout_ref[...])
+        logits = jnp.where(lane < EXPERTS, logits, MASKED)
+        raised = jnp.exp(logits - jnp.max(logits, axis=1, keepdims=True))
+        prob_ref[...] = raised / jnp.sum(raised, axis=1, keepdims=True)
+        for c in range(chunks):
+            at = pl.ds(pl.multiple_of(place_ref[c] * rows, rows), rows)
+            pick_ref[rows * c : rows * (c + 1), :] = sel_ref[at, :]
+        gates = prob_ref[...] * pick_ref[...]
+        for e in range(EXPERTS):
+            one = jnp.sum(jnp.where(lane == e, gates, 0.0), axis=1, keepdims=True)
+            gate_ref[e] = jnp.broadcast_to(one, (tokens, 128))
         sum_ref[...] = jnp.zeros_like(sum_ref)
-        for c in range(chunks):
-            logits = dot_nt(n2s[c][...], rout_ref[...])
-            logits = jnp.where(lane < EXPERTS, logits, MASKED)
-            raised = jnp.exp(logits - jnp.max(logits, axis=1, keepdims=True))
-            probs = raised / jnp.sum(raised, axis=1, keepdims=True)
-            prob_ref[c] = probs
-            at = pl.ds(pl.multiple_of(place_ref[c] * rows, rows), rows)
-            gates = probs * sel_ref[at, :]
-            for e in range(EXPERTS):
-                one = jnp.sum(jnp.where(lane == e, gates, 0.0), axis=1, keepdims=True)
-                gate_ref[e, c] = jnp.broadcast_to(one, (rows, 128))
-
-    def joined(which):
-        if count == 1:
-            return w_ref[0, which]
-        return jnp.concatenate([w_ref[d, which] for d in range(count)], 1)
-
-    wg, wu, wd = joined(0), joined(1), joined(2)
-    for c in range(chunks):
-        n2 = n2s[c][...]
-        gate_pre = dot_nt(n2, wg)
-        up_pre = dot_nt(n2, wu)
-        raw = dot_nt(gs[c][...], wd)
-        square = gate_pre * gate_pre
-        c0 = float(np.sqrt(2.0 / np.pi))
-        th = jnp.tanh(gate_pre * (c0 + (c0 * 0.044715) * square))
-        half = 0.5 + 0.5 * th
-        act = gate_pre * half
-        slope = half + gate_pre * (0.5 * c0 + (1.5 * c0 * 0.044715) * square) * (1.0 - th * th)
-        hidden = act * up_pre
-        prod = raw * hidden
-        hgs, ggs, ugs = [], [], []
-        for m in range(fb // 128):
-            col = step * (fb // 128) + m
-            e_low = (col * 128) // unit
-            e_high = (col * 128 + 127) // unit
-            bound = jnp.where(e_high > e_low, unit * e_high - col * 128, 128)
-            is_low = lane < bound
-            part = slice(128 * m, 128 * (m + 1))
-            gate = jnp.where(is_low, gate_ref[e_low, c], gate_ref[e_high, c])
-            sum_ref[e_low, c] += jnp.where(is_low, prod[:, part], 0.0)
-            sum_ref[e_high, c] += jnp.where(is_low, 0.0, prod[:, part])
-            hgs.append((gate * hidden[:, part]).astype(BF))
-            hidden_grad = gate * raw[:, part]
-            ggs.append((hidden_grad * up_pre[:, part] * slope[:, part]).astype(BF))
-            ugs.append((hidden_grad * act[:, part]).astype(BF))
-        hg, gg, ug = [jnp.concatenate(x, 1) for x in (hgs, ggs, ugs)]
-        at = slice(rows * c, rows * (c + 1))
-        hg_ref[at, :] = hg
-        gg_ref[at, :] = gg
-        ug_ref[at, :] = ug
-        out_acc[c] += dot_nn(hg, wd)
-        ng_acc[c] += dot_nn(gg, wg) + dot_nn(ug, wu)
+
+    wg, wu, wd = joined(w_ref, 0), joined(w_ref, 1), joined(w_ref, 2)
+    gate_pre = dot_nt(n2_ref[...], wg)
+    up_pre = dot_nt(n2_ref[...], wu)
+    raw = dot_nt(g_ref[...], wd)
+    c0 = float(np.sqrt(2.0 / np.pi))
+    square = gate_pre * gate_pre
+    th = jnp.tanh(gate_pre * (c0 + (c0 * 0.044715) * square))
+    half = 0.5 + 0.5 * th
+    act = gate_pre * half
+    slope = half + gate_pre * (0.5 * c0 + (1.5 * c0 * 0.044715) * square) * (1.0 - th * th)
+    hidden = act * up_pre
+    prod = raw * hidden
+    for m in range(hg_ref.shape[1] // 128):
+        col = step * (hg_ref.shape[1] // 128) + m
+        e_low = (col * 128) // unit
+        e_high = (col * 128 + 127) // unit
+        is_low = lane < jnp.where(e_high > e_low, unit * e_high - col * 128, 128)
+        part = slice(128 * m, 128 * (m + 1))
+        gate = jnp.where(is_low, gate_ref[e_low], gate_ref[e_high])
+        sum_ref[e_low] += jnp.where(is_low, prod[:, part], 0.0)
+        sum_ref[e_high] += jnp.where(is_low, 0.0, prod[:, part])
+        hg_ref[:, part] = (gate * hidden[:, part]).astype(BF)
+        hidden_grad = gate * raw[:, part]
+        gg_ref[:, part] = (hidden_grad * up_pre[:, part] * slope[:, part]).astype(BF)
+        ug_ref[:, part] = (hidden_grad * act[:, part]).astype(BF)
 
     @pl.when(step == steps - 1)
     def _():
-        router_grad = jnp.zeros((128, n2s[0].shape[1]), F32)
-        for c in range(chunks):
-            outs[c][...] = out_acc[c].astype(BF)
-            at = pl.ds(pl.multiple_of(place_ref[c] * rows, rows), rows)
-            grad = jnp.zeros((rows, 128), F32)
-            for e in range(EXPERTS):
-                grad = grad + jnp.where(lane == e, jnp.sum(sum_ref[e, c], axis=1, keepdims=True), 0.0)
-            grad = grad * sel_ref[at, :]
-            probs = prob_ref[c]
-            logit_grad = probs * (grad - jnp.sum(probs * grad, axis=1, keepdims=True))
-            ngs[c][...] = (ng_acc[c] + split_dot(logit_grad, rout_ref[...], dot_nn)).astype(BF)
-            router_grad = router_grad + split_dot(logit_grad, n2s[c][...], dot_tn)
-        rpart_ref[...] = router_grad[0:8, :]
-
-
-def moe_call(place, n2s, gs, sel, router, weights, unit):
+        grad = jnp.zeros((tokens, 128), F32)
+        for e in range(EXPERTS):
+            grad = grad + jnp.where(lane == e, jnp.sum(sum_ref[e], axis=1, keepdims=True), 0.0)
+        grad = grad * pick_ref[...]
+        probs = prob_ref[...]
+        logit_grad = probs * (grad - jnp.sum(probs * grad, axis=1, keepdims=True))
+        lg_ref[...] = logit_grad
+        rpart_ref[...] = split_dot(logit_grad, n2_ref[...], dot_tn)[0:8, :]
+
+
+def units_call(place, n2s, gs, sel, router, weights, unit):
     chunks, rows, depth = len(n2s), n2s[0].shape[0], n2s[0].shape[1]
     count, _, ff, part = weights.shape
     tokens = chunks * rows
     whole = lambda shape: pl.BlockSpec(shape, lambda s: (0,) * len(shape))
-    kept = [jax.ShapeDtypeStruct((tokens, ff), BF)] * 3
-    return pl.pallas_call(
-        functools.partial(moe_body, count, chunks, unit),
+    return pl.pallas_call(
+        functools.partial(units_body, chunks, unit),
         grid=(ff // BLOCK,),
         in_specs=[sspec()]
         + [whole((rows, depth))] * (2 * chunks)
         + [whole(sel.shape), whole(router.shape), pl.BlockSpec((count, 3, BLOCK, part), lambda s: (0, 0, s, 0))],
-        out_specs=[whole((rows, depth))] * (2 * chunks)
-        + [pl.BlockSpec((tokens, BLOCK), lambda s: (0, s))] * 3
-        + [whole((8, depth))],
-        out_shape=[jax.ShapeDtypeStruct((rows, depth), BF)] * (2 * chunks)
-        + kept
-        + [jax.ShapeDtypeStruct((8, depth), F32)],
+        out_specs=[pl.BlockSpec((tokens, BLOCK), lambda s: (0, s))] * 3 + [whole((tokens, 128)), whole((8, depth))],
+        out_shape=[jax.ShapeDtypeStruct((tokens, ff), BF)] * 3
+        + [jax.ShapeDtypeStruct((tokens, 128), F32), jax.ShapeDtypeStruct((8, depth), F32)],
         scratch_shapes=[
-            pltpu.VMEM((chunks, rows, depth), F32),
-            pltpu.VMEM((chunks, rows, depth), F32),
-            pltpu.VMEM((EXPERTS, chunks, rows, 128), F32),
-            pltpu.VMEM((EXPERTS, chunks, rows, 128), F32),
-            pltpu.VMEM((chunks, rows, 128), F32),
+            pltpu.VMEM((tokens, depth), BF),
+            pltpu.VMEM((tokens, depth), BF),
+            pltpu.VMEM((EXPERTS, tokens, 128), F32),
+            pltpu.VMEM((EXPERTS, tokens, 128), F32),
+            pltpu.VMEM((tokens, 128), F32),
+            pltpu.VMEM((tokens, 128), F32),
         ],
         compiler_params=params(("arbitrary",)),
-        cost_estimate=cost(12 * tokens * depth * ff, 6 * depth * ff + 12 * tokens * depth),
-        name="experts",
+        cost_estimate=cost(6 * tokens * depth * ff, 6 * depth * ff + 12 * tokens * depth),
+        name="expert_units",
     )(place, *n2s, *gs, sel, router, weights)
 
 
-def wgrad_body(count, groups, chunks, *refs):
-    kept = refs[: 3 * groups]
-    n2s = refs[3 * groups : 3 * groups + chunks]
-    gs = refs[3 * groups + chunks : 3 * groups + 2 * chunks]
-    out_ref = refs[-1]
+def product_body(terms, chunks, extra, *refs):
+    xs = refs[:terms]
+    ws = refs[terms : 2 * terms]
+    at = 2 * terms + (2 if extra else 0)
+    outs = refs[at : at + chunks]
+    total = None
+    for x, w in zip(xs, ws):
+        term = dot_nn(x[...], joined(w, 0))
+        total = term if total is None else total + term
+    if extra:
+        lg_ref, rout_ref = refs[2 * terms : 2 * terms + 2]
+        total = total + split_dot(lg_ref[...], rout_ref[...], dot_nn)
+    rows = outs[0].shape[0]
+    for c in range(chunks):
+        outs[c][...] = total[rows * c : rows * (c + 1)].astype(BF)
+
+
+def product_call(xs, picks, weights, chunks, extra, name):
+    tokens, ff = xs[0].shape
+    count, _, _, part = weights.shape
+    depth = count * part
+    rows = tokens // chunks
+    per = max(1, BLOCK // part)
+    wide = min(part * per, BLOCK)
+    whole = lambda shape: pl.BlockSpec(shape, lambda s: (0,) * len(shape))
+    place_at = (lambda i, s: (s, i, 0, 0)) if count > 1 else (lambda i, s: (0, i, 0, s))
+    w_specs = [pl.BlockSpec((min(per, count), 1, ff, wide // min(per, count)), functools.partial(place_at, i)) for i in picks]
+    return pl.pallas_call(
+        functools.partial(product_body, len(xs), chunks, bool(extra)),
+        grid=(depth // wide,),
+        in_specs=[whole((tokens, ff))] * len(xs)
+        + w_specs
+        + ([whole(extra[0].shape), pl.BlockSpec((128, wide), lambda s: (0, s))] if extra else []),
+        out_specs=[pl.BlockSpec((rows, wide), lambda s: (0, s))] * chunks,
+        out_shape=[jax.ShapeDtypeStruct((rows, depth), BF)] * chunks,
+        compiler_params=params(("arbitrary",)),
+        cost_estimate=cost(2 * len(xs) * tokens * depth * ff, 4 * len(xs) * depth * ff),
+        name=name,
+    )(*xs, *([weights] * len(xs)), *extra)
+
+
+def wgrad_body(count, chunks, *refs):
+    hg_ref, gg_ref, ug_ref = refs[:3]
+    n2s = refs[3 : 3 + chunks]
+    gs = refs[3 + chunks : 3 + 2 * chunks]
+    out_ref, n2_ref, g_ref = refs[3 + 2 * chunks :]
     part = out_ref.shape[3]
     rows = n2s[0].shape[0]
-    per = chunks // groups
-    for which, (pick, sides) in enumerate(((1, n2s), (2, n2s), (0, gs))):
-        total = None
+
+    @pl.when(pl.program_id(0) == 0)
+    def _():
         for c in range(chunks):
-            at = slice(rows * (c % per), rows * (c % per + 1))
-            term = dot_tn(kept[3 * (c // per) + pick][at, :], sides[c][...])
-            total = term if total is None else total + term
-        total = total.astype(BF)
+            n2_ref[rows * c : rows * (c + 1), :] = n2s[c][...]
+            g_ref[rows * c : rows * (c + 1), :] = gs[c][...]
+
+    for which, (kept, side) in enumerate(((gg_ref, n2_ref), (ug_ref, n2_ref), (hg_ref, g_ref))):
+        total = dot_tn(kept[...], side[...]).astype(BF)
         for d in range(count):
             out_ref[d, which] = total[:, part * d : part * (d + 1)]
 
 
 def wgrad_call(count, kept, n2s, gs):
-    groups = len(kept) // 3
     tokens, ff = kept[0].shape
     chunks, rows, depth = len(n2s), n2s[0].shape[0], n2s[0].shape[1]
     whole = lambda shape: pl.BlockSpec(shape, lambda s: (0,) * len(shape))
     return pl.pallas_call(
-        functools.partial(wgrad_body, count, groups, chunks),
+        functools.partial(wgrad_body, count, chunks),
         grid=(ff // BLOCK,),
-        in_specs=[pl.BlockSpec((tokens, BLOCK), lambda s: (0, s))] * (3 * groups)
-        + [whole((rows, depth))] * (2 * chunks),
+        in_specs=[pl.BlockSpec((tokens, BLOCK), lambda s: (0, s))] * 3 + [whole((rows, depth))] * (2 * chunks),
         out_specs=pl.BlockSpec((count, 3, BLOCK, depth // count), lambda s: (0, 0, s, 0)),
         out_shape=jax.ShapeDtypeStruct((count, 3, ff, depth // count), BF),
+        scratch_shapes=[pltpu.VMEM((tokens, depth), BF), pltpu.VMEM((tokens, depth), BF)],
         compiler_params=params(("arbitrary",)),
-        cost_estimate=cost(6 * chunks * rows * depth * ff, 12 * depth * ff),
+        cost_estimate=cost(6 * tokens * depth * ff, 12 * depth * ff),
         name="expert_weight_grads",
     )(*kept, *n2s, *gs)
 
@@ -553,10 +594,10 @@
     return back, jnp.sum(grad * u * scale, axis=0, keepdims=True)
 
 
-def resid_body(count, chunks, index_ref, *refs):
-    parts = refs[:chunks]
-    mid_ref, g_ref, gains_ref, w_ref = refs[chunks : chunks + 4]
-    rest = refs[chunks + 4 :]
+def resid_body(count, chunks, terms, index_ref, *refs):
+    parts = refs[:terms]
+    mid_ref, g_ref, gains_ref, w_ref = refs[terms : terms + 4]
+    rest = refs[terms + 4 :]
     resid_ref, aog_ref, gain_ref = rest[:3]
     dos = rest[3:]
     grad = functools.reduce(jnp.add, [p[...].astype(F32) for p in parts])
@@ -571,12 +612,12 @@
 
 
 def resid_call(index, parts, mid, grad, gains, w_out):
-    chunks = len(parts)
+    chunks, terms = w_out.shape[1], len(parts)
     shape = mid.shape
     width = w_out.shape[2]
     return pl.pallas_call(
-        functools.partial(resid_body, w_out.shape[0], chunks),
-        in_specs=[sspec()] + [vspec()] * (chunks + 4),
+        functools.partial(resid_body, w_out.shape[0], chunks, terms),
+        in_specs=[sspec()] + [vspec()] * (terms + 4),
         out_specs=[vspec()] * (3 + chunks),
         out_shape=[
             jax.ShapeDtypeStruct(shape, F32),
@@ -643,46 +684,63 @@
     )(index, place, dq, dk, dv, pack, *toks)
 
 
-def attn_weights_body(count, chunks, rows, slot_ref, place_ref, n1_ref, dq_ref, dk_ref, dv_ref, attt_ref, *refs):
-    aogs = refs[:chunks]
-    out_ref = refs[chunks]
+def attn_weights_body(count, slot_ref, n1_ref, dq_ref, dk_ref, dv_ref, small_ref, table_ref, out_ref):
     depth = n1_ref.shape[1]
     width = dq_ref.shape[1]
     part = depth // count
     normed = n1_ref[...]
+    pieces = width // 128
     for m, ref in enumerate((dq_ref, dk_ref, dv_ref)):
         grad = dot_tn(normed, ref[...]).astype(BF)
         for d in range(count):
             slot = slot_ref[d]
-            for half in range(width // 128):
-                at = (m * (width // 128) + half) * part
+            for half in range(pieces):
+                at = (m * pieces + half) * part
                 out_ref[slot, at : at + part, :] = grad[part * d : part * (d + 1), 128 * half : 128 * (half + 1)]
-    grad = None
-    for c in range(chunks):
-        at = pl.ds(pl.multiple_of(place_ref[c] * rows, rows), rows)
-        term = dot_nn(attt_ref[:, at], aogs[c][...])
-        grad = term if grad is None else grad + term
-    grad = grad.astype(BF)
+    at = 3 * pieces * part
     for d in range(count):
-        at = 3 * (width // 128) * part
-        out_ref[slot_ref[d], at : at + width, :] = grad[:, part * d : part * (d + 1)]
-
-
-def attn_weights_call(slots, place, n1, dq, dk, dv, attt, aogs, count):
+        rows = jnp.concatenate([small_ref[:, part * d : part * (d + 1)], table_ref[...]], 0)
+        out_ref[slot_ref[d], at : at + 16, :] = rows.astype(BF)
+
+
+def attn_weights_call(slots, n1, dq, dk, dv, small, table, count):
     total, depth = n1.shape
     width = dq.shape[1]
     part = depth // count
-    chunks, rows = len(aogs), aogs[0].shape[0]
-    out = (count, 3 * width * part // 128 + width, 128)
-    return pl.pallas_call(
-        functools.partial(attn_weights_body, count, chunks, rows),
-        in_specs=[sspec(), sspec()] + [vspec()] * (5 + chunks),
+    return pl.pallas_call(
+        functools.partial(attn_weights_body, count),
+        in_specs=[sspec()] + [vspec()] * 6,
         out_specs=vspec(),
-        out_shape=jax.ShapeDtypeStruct(out, BF),
+        out_shape=jax.ShapeDtypeStruct((count, 3 * width * part // 128 + 16, 128), BF),
         compiler_params=params(),
-        cost_estimate=cost(8 * total * depth * width, 8 * total * depth),
+        cost_estimate=cost(6 * total * depth * width, 8 * total * depth),
         name="attn_weight_grads",
-    )(slots, place, n1, dq, dk, dv, attt, *aogs)
+    )(slots, n1, dq, dk, dv, small, table)
+
+
+def wo_grad_body(count, chunks, slot_ref, *refs):
+    atts = refs[:chunks]
+    aog_ref, out_ref = refs[chunks:]
+    width = atts[0].shape[1]
+    for c in range(chunks):
+        grad = dot_tn(atts[c][...], aog_ref[...]).astype(BF)
+        part = grad.shape[1] // count
+        for d in range(count):
+            out_ref[slot_ref[d], c * width : (c + 1) * width, :] = grad[:, part * d : part * (d + 1)]
+
+
+def wo_grad_call(slots, atts, aog, count):
+    chunks, width = len(atts), atts[0].shape[1]
+    rows, depth = aog.shape
+    return pl.pallas_call(
+        functools.partial(wo_grad_body, count, chunks),
+        in_specs=[sspec()] + [vspec()] * (chunks + 1),
+        out_specs=vspec(),
+        out_shape=jax.ShapeDtypeStruct((count, chunks * width, depth // count), BF),
+        compiler_params=params(),
+        cost_estimate=cost(2 * rows * depth * chunks * width, 4 * depth * chunks * width),
+        name="w_output_grad",
+    )(slots, *atts, aog)
 
 
 def kept_choices(ids):
@@ -730,6 +788,32 @@
     direct = dp_size == 8 and share == 128
     place = z_rank ^ jnp.arange(z_size, dtype=jnp.int32)
 
+    near = z_swap(tokens_in, 1, z_size)
+    far = z_swap(tokens_in, 2, z_size)
+    line_at = 2 * BLOCK - 1 - np.arange(total + 2 * BLOCK)
+    line = jnp.dot(rel_table, jnp.asarray(onehot_of(line_at).T), precision=PRECISE)[:, None, :]
+    sel = kept_choices(expert_ids)
+    toks = [tokens_in, near, far, z_swap(after(far, near, sel, line), 1, z_size)]
+    small = jnp.concatenate([attn_gain, moe_gain, w_router.T.reshape(-1)])[None, :]
+    packed = jnp.concatenate([w_query, w_key, w_value], 1)
+    wo_slots = jnp.stack(z_direct([w_output] * z_size, z_size))[None]
+    ranks = dp_rank ^ jnp.arange(8, dtype=jnp.int32)
+    if direct:
+        index, slots = dp_slots(ranks), dp_scatter_slots(ranks)
+        pad = jnp.zeros((15, packed.shape[1]), BF)
+        pack = dp_step(jnp.concatenate([packed, small, pad], 0)[None], 2)
+        pack = dp_step(after(pack, near, far), 4)
+        wo_half = dp_step(after(wo_slots, near, far), 2)
+        pack = dp_step(pack, 1)
+        small_all = pack
+    else:
+        index = slots = jnp.zeros((1,), jnp.int32)
+        pack = lax.all_gather(packed, "dp", axis=0, tiled=True)[None]
+        small_all = lax.all_gather(small[0], "dp", axis=0).reshape(dp_size, 2 + EXPERTS, share)
+        small_all = jnp.swapaxes(small_all, 0, 1).reshape(2 + EXPERTS, depth)
+        small_all = jnp.concatenate([small_all, jnp.zeros((2, depth), BF)], 0)
+        wo_all = lax.all_gather(wo_slots[0], "dp", axis=2, tiled=True)[None]
+
     local = jnp.stack(
         [
             jnp.swapaxes(w_gate, 1, 2).reshape(ff, share),
@@ -742,100 +826,96 @@
     else:
         experts_w = lax.all_gather(local, "dp", axis=2, tiled=True)[None]
 
-    toks = z_gather(tokens_in, z_size)
-    small = jnp.concatenate([attn_gain, moe_gain, w_router.T.reshape(-1)])[None, :]
-    packed = jnp.concatenate([w_query, w_key, w_value], 1)
-    wo_slots = jnp.stack(z_gather(w_output, z_size))
+    n1, q, k, v, kt, vt, gains, router = qkv_call(index, place, toks, pack, small_all, width)
+    g_near = z_swap(after(out_grad, toks[3]), 1, z_size)
+    g_far = z_swap(after(out_grad, toks[3]), 2, z_size)
+    chances, ot, att = attn_fwd(piece_starts, q, k, vt, line)
+
+    att = after(att, g_near, g_far)
     if direct:
-        index = jnp.asarray(dp_slots(8))[dp_rank ^ jnp.arange(8, dtype=jnp.int32)]
-        pad = jnp.zeros((15, packed.shape[1]), BF)
-        pack = dp_gather(jnp.concatenate([packed, small, pad], 0)[None])
-        wo_all = dp_gather(wo_slots[None])
-        small_all = pack[:, share, :][index]
-    else:
-        index = jnp.zeros((1,), jnp.int32)
-        pack = lax.all_gather(packed, "dp", axis=0, tiled=True)[None]
-        small_all = lax.all_gather(small[0], "dp", axis=0)
-        wo_all = lax.all_gather(wo_slots, "dp", axis=2, tiled=True)[None]
-    small_all = small_all.reshape(dp_size, 2 + EXPERTS, share)
-    small_all = jnp.swapaxes(small_all, 0, 1).reshape(2 + EXPERTS, depth)
-    gains = jnp.concatenate([small_all[:2].astype(F32), jnp.zeros((6, depth), F32)], 0)
-    router = jnp.concatenate([small_all[2:], jnp.zeros((128 - EXPERTS, depth), BF)], 0)
-
-    line_at = 2 * BLOCK - 1 - np.arange(total + 2 * BLOCK)
-    line = jnp.dot(rel_table, jnp.asarray(onehot_of(line_at).T), precision=PRECISE)[:, None, :]
-    sel = kept_choices(expert_ids)
-
-    n1, q, k, v, kt, vt = qkv_call(index, place, toks, pack, gains, width)
-    chances, ot, att, attt = attn_fwd(piece_starts, q, k, vt, line)
-
-    atts = []
-    for mask in range(z_size):
-        piece = lax.dynamic_slice_in_dim(att, place[mask] * rows, rows, 0)
-        atts.append(piece if mask == 0 else z_swap(piece, mask, z_size))
-    mid, n2 = mid_call(index, atts, wo_all, tokens_in, gains)
-
-    gs = z_gather(out_grad, z_size)
-    n2s = z_gather(n2, z_size)
-    moe = moe_call(place, n2s, gs, sel, router, experts_w, unit)
-    outs, ngs = moe[:z_size], moe[z_size : 2 * z_size]
-    kept = moe[2 * z_size : 2 * z_size + 3]
-    router_part = moe[2 * z_size + 3]
-
-    ng_parts = [ngs[0]] + [z_swap(ngs[m], m, z_size) for m in range(1, z_size)]
-    weight_grads = wgrad_call(experts_w.shape[0], kept, n2s, gs)
+        wo_all = dp_step(after(dp_step(after(wo_half, n1), 4), att), 1)
+    pieces = [lax.dynamic_slice_in_dim(att, place[mask] * rows, rows, 0) for mask in range(z_size)]
+    atts = z_direct(pieces, z_size)
+    gs = [out_grad, g_near, g_far, z_swap(after(g_far, att), 1, z_size)]
+    mid, n2 = mid_call(index, [after(atts[0], gs[3])] + atts[1:], wo_all, tokens_in, gains)
+
+    n2_near = z_swap(n2, 1, z_size)
+    n2_far = z_swap(n2, 2, z_size)
+    n2s = [n2, n2_near, n2_far, z_swap(after(n2_far, n2_near), 1, z_size)]
+    hg, gg, ug, logit_grad, router_part = units_call(place, n2s, gs, sel, router, experts_w, unit)
+    ngs = product_call([gg, ug], (0, 1), experts_w, z_size, [logit_grad, router], "normed_two_grads")
+    passed = z_swap(ngs[3], 1, z_size)
+    outs = product_call([after(hg, ngs[0])], (2,), experts_w, z_size, [], "expert_out")
+    both = (ngs[2].astype(F32) + after(passed, outs[0]).astype(F32)).astype(BF)
+    far = z_swap(both, 2, z_size)
+    ng_near = z_swap(after(ngs[1], passed), 1, z_size)
+    weight_grads = wgrad_call(experts_w.shape[0], [after(hg, both, *outs), gg, ug], n2s, gs)
+    resid = resid_call(index, [after(ngs[0], weight_grads), ng_near, far], mid, out_grad, gains, wo_all)
+    resid_grad, aog, gain_two = resid[:3]
+    weight_grads = after(weight_grads, aog)
     if direct:
         expert_grads = lax.psum_scatter(weight_grads, "dp", scatter_dimension=0, tiled=False)
     else:
         expert_grads = lax.psum_scatter(weight_grads[0], "dp", scatter_dimension=2, tiled=True)
-
-    resid = resid_call(index, ng_parts, mid, out_grad, gains, wo_all)
-    resid_grad, aog, gain_two = resid[:3]
-    dos = [resid[3]] + [z_swap(resid[3 + m], m, z_size) for m in range(1, z_size)]
+    dos = z_direct(resid[3:], z_size)
+    count = experts_w.shape[0]
+    wo_grads = wo_grad_call(slots, atts, aog, count)
+    dos[0] = after(dos[0], wo_grads)
+    if direct:
+        wo_grads = dp_fold(after(wo_grads, *dos), 1)
     dq, dk, dv, diag = attn_bwd(place, dos, chances, q, k, v, kt, ot)
-    out_parts = [outs[0]] + [z_swap(outs[m], m, z_size) for m in range(1, z_size)]
-    out_rows = (mid + functools.reduce(jnp.add, [p.astype(F32) for p in out_parts])).astype(BF)
-    aogs = z_gather(aog, z_size)
-
+    out_passed = z_swap(after(outs[3], *dos), 1, z_size)
+    out_near = z_swap(after(outs[1], *dos), 1, z_size)
+    if direct:
+        wo_grads = dp_fold(wo_grads, 2)
+        dq = after(dq, wo_grads, out_passed, out_near)
+    out_far = z_swap((outs[2].astype(F32) + after(out_passed, dq).astype(F32)).astype(BF), 2, z_size)
     proj = proj_call(index, place, dq, dk, dv, pack, toks)
-    n1_parts = [proj[0]] + [z_swap(proj[m], m, z_size) for m in range(1, z_size)]
     gain_one = proj[z_size]
-    in_grad = final_call(n1_parts, tokens_in, resid_grad, gains)
-
-    if direct:
-        slots = jnp.asarray(dp_scatter_slots())[dp_rank ^ jnp.arange(8, dtype=jnp.int32)]
-        attn_grads = dp_scatter(attn_weights_call(slots, place, n1, dq, dk, dv, attt, aogs, 8)).astype(F32)
-        per = width // 128
-        cut = attn_grads[: 3 * per * share].reshape(3, per, share, 128)
-        cut = jnp.swapaxes(cut, 1, 2).reshape(3, share, width)
-        grad_wo = attn_grads[3 * per * share :]
-    else:
-        ordered = lax.all_gather(aog, "tensor", axis=0, tiled=True)
-        cut = jnp.stack([jnp.dot(n1.T, d, preferred_element_type=F32) for d in (dq, dk, dv)])
-        cut = lax.psum_scatter(cut, "dp", scatter_dimension=1, tiled=True)
-        grad_wo = jnp.dot(attt, ordered, preferred_element_type=F32)
-        grad_wo = lax.psum_scatter(grad_wo, "dp", scatter_dimension=1, tiled=True)
-
     diag_at = (
         BLOCK * np.arange(total // BLOCK + 1)[:, None] - (BLOCK * (total // BLOCK - 2) + 1) - np.arange(2 * BLOCK)[None, :]
     )
     table = jnp.einsum("hbt,btk->hk", diag, jnp.asarray(onehot_of(diag_at)), precision=PRECISE)
-
-    smalls = jnp.concatenate([gain_one[:1], gain_two[:1], router_part[:EXPERTS]], 0)
-    table_row = jnp.pad(table.reshape(1, -1), ((0, 0), (0, depth - heads * BUCKETS)))
+    smalls = jnp.concatenate([gain_one[:1], gain_two[:1], router_part[:EXPERTS], jnp.zeros((2, depth), F32)], 0)
+    n1_passed = z_swap(proj[3], 1, z_size)
+    n1_near = z_swap(proj[1], 1, z_size)
     if direct:
+        table_rows = jnp.pad(table.reshape(1, -1), ((0, 7), (0, 0)))
+        attn_grads = attn_weights_call(slots, n1, dq, dk, dv, smalls, table_rows, 8)
+        wo_grads = dp_fold(wo_grads, 4)[0]
+        n1_passed = after(n1_passed, attn_grads, out_far, wo_grads)
+    n1_both = (proj[2].astype(F32) + n1_passed.astype(F32)).astype(BF)
+    n1_far = z_swap(n1_both, 2, z_size)
+    in_grad = final_call([proj[0], n1_near, n1_far], tokens_in, resid_grad, gains)
+    out_parts = [outs[0], out_near, out_far]
+    out_rows = (mid + functools.reduce(jnp.add, [p.astype(F32) for p in out_parts])).astype(BF)
+
+    if direct:
+        attn_grads = dp_fold(after(attn_grads, n1_both), 1)
+        attn_grads = dp_fold(after(attn_grads, n1_near), 2)
+        attn_grads = dp_fold(attn_grads, 4)
+        attn_grads = attn_grads[0].astype(F32)
+        per = width // 128
+        cut = attn_grads[: 3 * per * share].reshape(3, per, share, 128)
+        cut = jnp.swapaxes(cut, 1, 2).reshape(3, share, width)
+        smalls = attn_grads[3 * per * share :]
+        grad_table = smalls[8, : heads * BUCKETS].reshape(heads, BUCKETS)
+        smalls = smalls[:8]
         for bit in (1, 2):
             smalls = smalls + z_swap(smalls, bit, z_size)
-        smalls = jnp.concatenate([smalls, table_row], 0)
-        for bit in (1, 2, 4):
-            smalls = smalls + lax.ppermute(smalls, "dp", [(i, i ^ bit) for i in range(8)])
-        table_row = smalls[2 + EXPERTS :]
+        mine = z_rank
+        grad_wo = wo_grads
     else:
+        cut = jnp.stack([jnp.dot(n1.T, d, preferred_element_type=F32) for d in (dq, dk, dv)])
+        cut = lax.psum_scatter(cut, "dp", scatter_dimension=1, tiled=True)
         smalls = lax.psum(smalls, ("dp", "tensor"))
-        table_row = lax.psum(table_row, "dp")
-    grad_table = table_row[0, : heads * BUCKETS].reshape(heads, BUCKETS)
+        grad_table = lax.psum(table, "dp")
+        mine = dp_rank * z_size + z_rank
+        grad_wo = lax.psum_scatter(wo_grads[0], "dp", scatter_dimension=1, tiled=True)
+    wo_parts = z_direct([grad_wo[width * c : width * (c + 1)] for c in range(z_size)], z_size)
+    grad_wo = functools.reduce(jnp.add, [p.astype(F32) for p in wo_parts])
     per_device = depth // (dp_size * z_size)
-    own = lax.dynamic_slice_in_dim(smalls, (dp_rank * z_size + z_rank) * per_device, per_device, 1)
+    own = lax.dynamic_slice_in_dim(smalls, mine * per_device, per_device, 1)
 
     wide = expert_grads.astype(F32).reshape(3, EXPERTS, unit, share)
     return (

time: 522 us -> 434 us (0.83)
  waiting for transfers between devices: 267 us -> 156 us
  Pallas kernels: 146 us -> 155 us
  starting transfers between devices: 46.3 us -> 54 us
    ppermute x32, waiting for transfers between devices: 242 us -> 109 us  [z_swap(): return lax.ppermute(x, 'tensor', [(i, i ^ mask) for i in range(size)])]
    ppermute x12, waiting for transfers between devices: 25.7 us -> 46.9 us  [the longest x6 34.3 us: dp_step(): other = lax.ppermute(x, 'dp', [(i, i ^ bit) for i in range(8)])]
    pallas_call x4 -> x7, Pallas kernels: 95.2 us -> 103 us  [the longest x1 33.8 us: units_call(): pl.pallas_call(functools.partial(units_body, chunks, unit), grid=(ff // B...]
    unnamed x103 -> x111, local copies, waits for them, and re-layouts: 9.71 us -> 10.6 us
  transfers between devices with their start and end apart: 46 -> 46, of which waited for: 26 -> 24; matrix products, arithmetic and copies ran while one was open for 6% -> 7% of each run, Pallas kernels for 12% -> 23%
where the time goes in v2:
time: 434 us; the launch traced here: 430 us
  waiting for transfers between devices  156 us (36%)
  Pallas kernels  155 us (36%)
  starting transfers between devices  54 us (12%)
  local copies, waits for them, and re-layouts  26.9 us (6%)
  other arithmetic  19.4 us (4%)
  between operations  17.4 us (4%)
    ppermute x32, waiting for transfers between devices, z_swap(): return lax.ppermute(x, 'tensor', [(i, i ^ mask) for i in range(size)])  109 us
    ppermute x32, starting transfers between devices, z_swap(): return lax.ppermute(x, 'tensor', [(i, i ^ mask) for i in range(size)])  46.5 us
    ppermute x6, waiting for transfers between devices, dp_step(): other = lax.ppermute(x, 'dp', [(i, i ^ bit) for i in range(8)])  34.3 us
    pallas_call x1, Pallas kernels, units_call(): pl.pallas_call(functools.partial(units_body, chunks, unit), grid=(ff // B...  33.8 us
    pallas_call x2, Pallas kernels, product_call(): pl.pallas_call(functools.partial(product_body, len(xs), chunks, bool(extr...  30.2 us
    pallas_call x1, Pallas kernels, wgrad_call(): pl.pallas_call(functools.partial(wgrad_body, count, chunks), grid=(ff //...  25 us
    pallas_call x1, Pallas kernels, attn_fwd(): pl.pallas_call(functools.partial(fwd_body, total), grid=(heads,), in_spec...  16.3 us
    pallas_call x1, Pallas kernels, attn_bwd(): pl.pallas_call(functools.partial(bwd_body, total, chunks), grid=(heads,),...  16.2 us
  transfers between devices with their start and end apart: 46, of which 24 were waited for; matrix products, arithmetic and copies ran while one was open for 7% of the time, Pallas kernels for 23%

profile of v2, /device:TPU:14, one launch (start us, length us, event | category | flops | bytes accessed | tf_op | source)
XLA Modules:
  0.0 429.5 jit_solution(11934188949093319870)
XLA Ops:
  7.2 3.1 pad_maximum_fusion
  11.6 2.7 collective-permute-start.14
  14.3 1.2 collective-permute-start.1
  16.7 2.3 reduce-window.6
  19.8 2.6 collective-permute-done.3
  22.4 2.5 collective-permute-start.13
  25.0 16.5 %collective-permute-done.1.refs_2_ = bf16[256,1024]{1,0:T(8,128)(2,1)S(1)} collective-permute-done((bf16[256,1024]{1,0:T(8,128)(2,1)S(1)}, bf16[256,1024]{1,0:T(8,128)(2,1)S(1)}, u32[]{:S(2)}, u32[]{:S(2)}) %collective-permute-start.1) | collective-permute-done | bytes 524320 | tf_op jit(solution)/shard_map/ppermute | solution.py:66
  42.0 1.6 fusion.2.refs_8_
  43.6 12.1 %collective-permute-done.4 = bf16[2,144,768]{2,1,0:T(8,128)(2,1)S(1)} collective-permute-done((bf16[2,144,768]{2,1,0:T(8,128)(2,1)S(1)}, bf16[2,144,768]{2,1,0:T(8,128)(2,1)S(1)}, u32[]{:S(2)}, u32[]{:S(2)}) %collective-permute-start.4) | collective-permute-done | bytes 442400 | tf_op jit(solution)/shard_map/ppermute | solution.py:94
  59.7 12.9 %collective-permute-done.15 = bf16[1,4,256,128]{3,2,1,0:T(8,128)(2,1)} collective-permute-done((bf16[1,4,256,128]{3,2,1,0:T(8,128)(2,1)S(1)}, bf16[1,4,256,128]{3,2,1,0:T(8,128)(2,1)}, u32[]{:S(2)}, u32[]{:S(2)}) %collective-permute-start.15) | collective-permute-done | bytes 262176 | tf_op jit(solution)/shard_map/ppermute | solution.py:94
  73.7 2.5 collective-permute-start.7
  78.0 7.0 %norm_qkv.1 = (bf16[1024,1024]{1,0:T(8,128)(2,1)}, bf16[1024,256]{1,0:T(8,128)(2,1)}, bf16[1024,256]{1,0:T(8,128)(2,1)}, bf16[1024,256]{1,0:T(8,128)(2,1)}, bf16...) custom-call(s32[8]{0:T(128)} %and_or_fusion.1.index_ref, ...), custom_call_target="tpu_custom_call" | custom-call | flops 1610612736 | bytes 8388608 | tf_op jit(solution)/shard_map/norm_qkv/pallas_call | solution.py:154
  85.0 1.5 collective-permute-start.16
  86.5 16.3 %attn_forward.1 = (bf16[4,1024,1024]{2,1,0:T(8,128)(2,1)}, f32[256,1024]{1,0:T(8,128)}, bf16[1024,256]{1,0:T(8,128)(2,1)}) custom-call(s32[1,2]{1,0:T(1,128)} %starts_ref.1, bf16[1024,256]{1,0:T(8,128)(2,1)} %get-tuple-element.82.q_ref.refs_5_, bf16[1024,256]{1,0:T(8,128)(2,1)} %get-tuple-element.83.k_ref.refs_6_, ...), custom_call_target="tpu_custom_call" | custom-call | flops 4294967296 | bytes 10485760 | tf_op jit(solution)/shard_map/attn_forward/pallas_call | solution.py:235
  103.6 6.7 %collective-permute-done.16 = bf16[2,4,256,128]{3,2,1,0:T(8,128)(2,1)S(1)} collective-permute-done((bf16[2,4,256,128]{3,2,1,0:T(8,128)(2,1)S(1)}, bf16[2,4,256,128]{3,2,1,0:T(8,128)(2,1)S(1)}, u32[]{:S(2)}, u32[]{:S(2)}) %collective-permute-start.16) | collective-permute-done | bytes 524320 | tf_op jit(solution)/shard_map/ppermute | solution.py:94
  110.5 1.6 collective-permute-start.8
  116.0 2.9 collective-permute-start.10
  119.5 10.8 %collective-permute-done.8.refs_7_.refs_10_ = bf16[256,1024]{1,0:T(8,128)(2,1)S(1)} collective-permute-done((bf16[256,1024]{1,0:T(8,128)(2,1)}, bf16[256,1024]{1,0:T(8,128)(2,1)S(1)}, u32[]{:S(2)}, u32[]{:S(2)}) %collective-permute-start.8) | collective-permute-done | bytes 524320 | tf_op jit(solution)/shard_map/ppermute | solution.py:66
  131.1 2.4 collective-permute-done.9.refs_1_
  134.1 3.9 out_projection_norm.1
  138.7 1.3 collective-permute-start.18
  140.0 21.3 %collective-permute-done.19.refs_2_.refs_5_ = bf16[256,1024]{1,0:T(8,128)(2,1)S(1)} collective-permute-done((bf16[256,1024]{1,0:T(8,128)(2,1)}, bf16[256,1024]{1,0:T(8,128)(2,1)S(1)}, u32[]{:S(2)}, u32[]{:S(2)}) %collective-permute-start.19) | collective-permute-done | bytes 524320 | tf_op jit(solution)/shard_map/ppermute | solution.py:66
  161.3 1.6 collective-permute-done.18.refs_1_.refs_4_
  163.0 2.4 collective-permute-start.20
  165.4 12.1 %collective-permute-done.20.refs_3_.refs_6_ = bf16[256,1024]{1,0:T(8,128)(2,1)S(1)} collective-permute-done((bf16[256,1024]{1,0:T(8,128)(2,1)S(1)}, bf16[256,1024]{1,0:T(8,128)(2,1)S(1)}, u32[]{:S(2)}, u32[]{:S(2)}) %collective-permute-start.20) | collective-permute-done | bytes 524320 | tf_op jit(solution)/shard_map/ppermute | solution.py:66
  178.3 33.8 %expert_units.1 = (bf16[1024,2816]{1,0:T(8,128)(2,1)}, bf16[1024,2816]{1,0:T(8,128)(2,1)}, bf16[1024,2816]{1,0:T(8,128)(2,1)}, f32[1024,128]{1,0:T(8,128)}, f32[8,1024]{1,0:T(8,128)}) custom-call(s32[4]{0:T(128)} %iota_xor_fusion.place_ref, bf16[256,1024]{1,0:T(8,128)(2,1)} %get-tuple-element.96.refs_0_.refs_3_, bf16[256,1024]{1,0:T(8,128)(2,1)} %copy-done.43, ...), custom_call_target="tpu_custom_call" | custom-call | flops 17716740096 | bytes 29884416 | tf_op jit(solution)/shard_map/expert_units/pallas_call | solution.py:489
  212.1 19.7 %normed_two_grads.1 = (bf16[256,1024]{1,0:T(8,128)(2,1)}, bf16[256,1024]{1,0:T(8,128)(2,1)}, bf16[256,1024]{1,0:T(8,128)(2,1)}, bf16[256,1024]{1,0:T(8,128)(2,1)}) custom-call(bf16[1024,2816]{1,0:T(8,128)(2,1)} %get-tuple-element.100.refs_0_.refs_1_, bf16[1024,2816]{1,0:T(8,128)(2,1)} %get-tuple-element.101.refs_1_.refs_2_, ...), custom_call_target="tpu_custom_call" | custom-call | flops 11811160064 | bytes 23068672 | tf_op jit(solution)/shard_map/normed_two_grads/pallas_call | solution.py:539
  231.8 1.8 collective-permute-start.21
  233.7 10.5 %expert_out.1 = (bf16[256,1024]{1,0:T(8,128)(2,1)}, bf16[256,1024]{1,0:T(8,128)(2,1)}, bf16[256,1024]{1,0:T(8,128)(2,1)}, bf16[256,1024]{1,0:T(8,128)(2,1)}) custom-call(bf16[1024,2816]{1,0:T(8,128)(2,1)} %get-tuple-element.112.refs_0_, bf16[8,3,2816,128]{3,2,1,0:T(8,128)(2,1)} %bitcast.94), custom_call_target="tpu_custom_call" | custom-call | flops 5905580032 | bytes 11534336 | tf_op jit(solution)/shard_map/expert_out/pallas_call | solution.py:539
  244.1 1.3 collective-permute-done.21
  245.7 1.5 collective-permute-start.22
  247.2 25.0 %expert_weight_grads.1 = bf16[8,3,2816,128]{3,2,1,0:T(8,128)(2,1)} custom-call(bf16[1024,2816]{1,0:T(8,128)(2,1)} %get-tuple-element.112.refs_0_, bf16[1024,2816]{1,0:T(8,128)(2,1)} %get-tuple-element.100.refs_0_.refs_1_, bf16[1024,2816]{1,0:T(8,128)(2,1)} %get-tuple-element.101.refs_1_.refs_2_, bf16[256,1024]{1,0:T(8,128)(2,1)} %get-tuple-element.96.refs_0_.refs_3_, ...), custom_call_target="tpu_custom_call" | custom-call | flops 17716740096 | bytes 34603008 | tf_op jit(solution)/shard_map/expert_weight_grads/pallas_call | solution.py:577
  273.2 4.7 %resid_grad.1 = (f32[256,1024]{1,0:T(8,128)}, bf16[256,1024]{1,0:T(8,128)(2,1)}, f32[8,1024]{1,0:T(8,128)}, bf16[256,256]{1,0:T(8,128)(2,1)}, bf16[256,256]{1,0:...) custom-call(s32[8]{0:T(128)} %and_or_fusion.1.index_ref, ...), custom_call_target="tpu_custom_call" | custom-call | flops 536870912 | bytes 4194304 | tf_op jit(solution)/shard_map/resid_grad/pallas_call | solution.py:618
  279.4 2.8 collective-permute-start.25
  282.8 3.4 w_output_grad.1
  286.2 3.7 collective-permute-done.25.refs_2_
  289.9 2.1 collective-permute-done.26.refs_3_
  292.0 1.6 slice.168
  293.8 2.0 collective-permute-start.28
  299.1 16.2 %attn_backward.1 = (bf16[1024,256]{1,0:T(8,128)(2,1)}, bf16[1024,256]{1,0:T(8,128)(2,1)}, bf16[1024,256]{1,0:T(8,128)(2,1)}, f32[4,5,512]{2,1,0:T(8,128)}) custom-call(s32[4]{0:T(128)} %iota_xor_fusion.place_ref, bf16[256,256]{1,0:T(8,128)(2,1)} %get-tuple-element.118.refs_0_, bf16[256,256]{1,0:T(8,128)(2,1)} %copy-done.46, bf16[256,256]{1,0:T(8,128)(2,1)} %copy-done.47, ...), custom_call_target="tpu_custom_call" | custom-call | flops 171798691840 | bytes 10485760 | tf_op jit(solution)/shard_map/attn_backward/pallas_call | solution.py:348
  315.3 1.2 add_convert_fusion.5
  316.5 3.1 collective-permute-done.28
  319.6 1.2 add_convert_fusion.4
  320.8 1.4 collective-permute-start.31
  322.2 5.8 %projection_grads.1 = (bf16[256,1024]{1,0:T(8,128)(2,1)}, bf16[256,1024]{1,0:T(8,128)(2,1)}, bf16[256,1024]{1,0:T(8,128)(2,1)}, bf16[256,1024]{1,0:T(8,128)(2,1)}, f32[8,1024]{1,0:T(8,128)}) custom-call(s32[8]{0:T(128)} %and_or_fusion.1.index_ref, s32[4]{0:T(128)} %iota_xor_fusion.place_ref, bf16[1024,256]{1,0:T(8,128)(2,1)} %get-tuple-element.130.dq_ref, ...), custom_call_target="tpu_custom_call" | custom-call | flops 1610612736 | bytes 8388608 | tf_op jit(solution)/shard_map/projection_grads/pallas_call | solution.py:676
  328.1 1.8 collective-permute-start.33
  333.2 5.4 %attn_weight_grads.1 = bf16[8,784,128]{2,1,0:T(8,128)(2,1)} custom-call(s32[8]{0:T(128)} %and_or_fusion.slot_ref, bf16[1024,1024]{1,0:T(8,128)(2,1)} %get-tuple-element.91.n1_ref, bf16[1024,256]{1,0:T(8,128)(2,1)} %get-tuple-element.130.dq_ref, bf16[1024,256]{1,0:T(8,128)(2,1)} %get-tuple-element.132.dk_ref, bf16[1024,256]{1,0:T(8,128)(2,1)} %get-tuple-element.133.dv_ref, ...), custom_call_target="tpu_custom_call" | custom-call | flops 1610612736 | bytes 8388608 | tf_op jit(solution)/shard_map/attn_weight_grads/pallas_call | solution.py:710
  338.6 6.1 %collective-permute-done.31 = bf16[256,1024]{1,0:T(8,128)(2,1)S(1)} collective-permute-done((bf16[256,1024]{1,0:T(8,128)(2,1)S(1)}, bf16[256,1024]{1,0:T(8,128)(2,1)S(1)}, u32[]{:S(2)}, u32[]{:S(2)}) %collective-permute-start.31) | collective-permute-done | bytes 524320 | tf_op jit(solution)/shard_map/ppermute | solution.py:66
  344.7 6.2 %collective-permute-done.33 = bf16[256,1024]{1,0:T(8,128)(2,1)S(1)} collective-permute-done((bf16[256,1024]{1,0:T(8,128)(2,1)}, bf16[256,1024]{1,0:T(8,128)(2,1)S(1)}, u32[]{:S(2)}, u32[]{:S(2)}) %collective-permute-start.33) | collective-permute-done | bytes 524320 | tf_op jit(solution)/shard_map/ppermute | solution.py:66
  351.1 1.5 slice.175
  352.8 1.4 collective-permute-start.40
  354.1 2.1 collective-permute-start.32
  356.3 11.2 %collective-permute-done.40 = bf16[1,1024,128]{2,1,0:T(8,128)(2,1)S(1)} collective-permute-done((bf16[1,1024,128]{2,1,0:T(8,128)(2,1)S(1)}, bf16[1,1024,128]{2,1,0:T(8,128)(2,1)S(1)}, u32[]{:S(2)}, u32[]{:S(2)}) %collective-permute-start.40) | collective-permute-done | bytes 262176 | tf_op jit(solution)/shard_map/ppermute | solution.py:100
  371.1 1.7 collective-permute-start.41
  373.3 2.2 collective-permute-start.42
  376.0 3.5 collective-permute-done.43
  380.2 2.5 collective-permute-start.34
  385.6 2.1 add_convert_fusion.3
  387.8 15.7 %collective-permute-done.34.refs_2_ = bf16[256,1024]{1,0:T(8,128)(2,1)S(1)} collective-permute-done((bf16[256,1024]{1,0:T(8,128)(2,1)S(1)}, bf16[256,1024]{1,0:T(8,128)(2,1)S(1)}, u32[]{:S(2)}, u32[]{:S(2)}) %collective-permute-start.34) | collective-permute-done | bytes 524320 | tf_op jit(solution)/shard_map/ppermute | solution.py:66
  404.3 3.5 in_grad.1
  407.8 3.5 collective-permute-start.38
  411.4 1.6 collective-permute-done.38
  412.9 1.9 collective-permute-start.39
  419.0 3.7 fusion.13
  (228 shorter events, 40.0 us)
Async XLA Ops:
  7.2 48.7 %copy-start = (f32[4,32]{1,0:T(4,128)S(1)}, f32[4,32]{1,0:T(4,128)}, u32[]{:S(2)}) copy-start(f32[4,32]{1,0:T(4,128)} %param.24) | copy-start | bytes 1540
  7.2 170.3 %all-gather.3.cloned.1.call-start = ((), (), s32[]{:S(2)}) async-start(), calls=%async_computation.2 | async-start | bytes 19464192 | tf_op jit(solution)/shard_map/all_gather | solution.py:825
  10.4 45.5 %copy-start.24 = (f32[32,1536]{1,0:T(8,128)S(1)}, f32[32,1536]{1,0:T(8,128)}, u32[]{:S(2)}) copy-start(f32[32,1536]{1,0:T(8,128)} %constant.49.clone) | copy-start | bytes 589828
  10.5 408.5 %reduce-scatter.2.cloned.1.call-start = ((), (), s32[]{:S(2)}) async-start(), calls=%async_computation.1 | async-start | bytes 19464192 | tf_op jit(solution)/shard_map/reduce_scatter | solution.py:857
  11.2 45.6 %collective-permute-start.12 = (bf16[256,128]{1,0:T(8,128)(2,1)S(1)}, bf16[256,128]{1,0:T(8,128)(2,1)}, u32[]{:S(2)}, u32[]{:S(2)}) collective-permute-start(bf16[256,128]{1,0:T(8,128)(2,1)S(1)} %copy-done.29), channel_id=1, source_target_pairs={{0,1},{1,0},{2,3},{3,2},{4,5},{5,4},{6,7},{7,6},{8,9},{9,8},{10,11... | collective-permute-start | bytes 196616 | tf_op jit(solution)/shard_map/ppermute | solution.py:66
  11.6 45.2 %collective-permute-start.14 = (bf16[256,128]{1,0:T(8,128)(2,1)S(1)}, bf16[256,128]{1,0:T(8,128)(2,1)}, u32[]{:S(2)}, u32[]{:S(2)}) collective-permute-start(bf16[256,128]{1,0:T(8,128)(2,1)S(1)} %copy-done.29), channel_id=1, source_target_pairs={{0,3},{1,2},{2,1},{3,0},{4,7},{5,6},{6,5},{7,4},{8,11},{9,10},{10,... | collective-permute-start | bytes 196616 | tf_op jit(solution)/shard_map/ppermute | solution.py:66
  14.3 27.2 %collective-permute-start.1 = (bf16[256,1024]{1,0:T(8,128)(2,1)S(1)}, bf16[256,1024]{1,0:T(8,128)(2,1)S(1)}, u32[]{:S(2)}, u32[]{:S(2)}) collective-permute-start(bf16[256,1024]{1,0:T(8,128)(2,1)S(1)} %copy-done.7), channel_id=1, source_target_pairs={{0,2},{1,3},{2,0},{3,1},{4,6},{5,7},{6,4},{7,5},{8,10},{9,11},{10,... | collective-permute-start | bytes 1572872 | tf_op jit(solution)/shard_map/ppermute | solution.py:66
  15.6 25.9 %collective-permute-start = (bf16[256,1024]{1,0:T(8,128)(2,1)S(1)}, bf16[256,1024]{1,0:T(8,128)(2,1)S(1)}, u32[]{:S(2)}, u32[]{:S(2)}) collective-permute-start(bf16[256,1024]{1,0:T(8,128)(2,1)S(1)} %copy-done.7), channel_id=1, source_target_pairs={{0,1},{1,0},{2,3},{3,2},{4,5},{5,4},{6,7},{7,6},{8,9},{9,8},{10,11... | collective-permute-start | bytes 1572872 | tf_op jit(solution)/shard_map/ppermute | solution.py:66
  16.0 6.4 %collective-permute-start.3 = (bf16[1,144,768]{2,1,0:T(8,128)(2,1)S(1)}, bf16[1,144,768]{2,1,0:T(8,128)(2,1)S(1)}, u32[]{:S(2)}, u32[]{:S(2)}) collective-permute-start(bf16[1,144,768]{2,1,0:T(8,128)(2,1)S(1)} %maximum_bitcast_fusion.1), channel_id=1, source_target_pairs={{0,8},{4,12},{8,0},{12,4},{16,24},{20,28},{24,16},{28,20},{1,9},{5... | collective-permute-start | bytes 663560 | tf_op jit(solution)/shard_map/ppermute | solution.py:94
  22.4 34.4 %collective-permute-start.13 = (bf16[256,128]{1,0:T(8,128)(2,1)S(1)}, bf16[256,128]{1,0:T(8,128)(2,1)}, u32[]{:S(2)}, u32[]{:S(2)}) collective-permute-start(bf16[256,128]{1,0:T(8,128)(2,1)S(1)} %copy-done.29), channel_id=1, source_target_pairs={{0,2},{1,3},{2,0},{3,1},{4,6},{5,7},{6,4},{7,5},{8,10},{9,11},{10,... | collective-permute-start | bytes 196616 | tf_op jit(solution)/shard_map/ppermute | solution.py:66
  41.5 14.2 %copy-start.37 = (bf16[256,1024]{1,0:T(8,128)(2,1)}, bf16[256,1024]{1,0:T(8,128)(2,1)S(1)}, u32[]{:S(2)}) copy-start(bf16[256,1024]{1,0:T(8,128)(2,1)S(1)} %collective-permute-done.1.refs_2_) | copy-start | bytes 1572868
  41.5 14.2 %collective-permute-start.4 = (bf16[2,144,768]{2,1,0:T(8,128)(2,1)S(1)}, bf16[2,144,768]{2,1,0:T(8,128)(2,1)S(1)}, u32[]{:S(2)}, u32[]{:S(2)}) collective-permute-start(bf16[2,144,768]{2,1,0:T(8,128)(2,1)S(1)} %pad_maximum_fusion.4), channel_id=1, source_target_pairs={{0,16},{4,20},{8,24},{12,28},{16,0},{20,4},{24,8},{28,12},{1,17},{... | collective-permute-start | bytes 1327112 | tf_op jit(solution)/shard_map/ppermute | solution.py:94
  55.8 17.8 %copy-start.16 = (bf16[256,1024]{1,0:T(8,128)(2,1)S(1)}, bf16[256,1024]{1,0:T(8,128)(2,1)}, u32[]{:S(2)}) copy-start(bf16[256,1024]{1,0:T(8,128)(2,1)} %refs_4_.3) | copy-start | bytes 1572868
  55.8 20.9 %collective-permute-start.5 = (bf16[4,144,768]{2,1,0:T(8,128)(2,1)S(1)}, bf16[4,144,768]{2,1,0:T(8,128)(2,1)S(1)}, u32[]{:S(2)}, u32[]{:S(2)}) collective-permute-start(bf16[4,144,768]{2,1,0:T(8,128)(2,1)S(1)} %pad_maximum_fusion.2), channel_id=1, source_target_pairs={{0,4},{4,0},{8,12},{12,8},{16,20},{20,16},{24,28},{28,24},{1,5},{5... | collective-permute-start | bytes 2654216 | tf_op jit(solution)/shard_map/ppermute | solution.py:94
  57.8 14.8 %collective-permute-start.15 = (bf16[1,4,256,128]{3,2,1,0:T(8,128)(2,1)S(1)}, bf16[1,4,256,128]{3,2,1,0:T(8,128)(2,1)}, u32[]{:S(2)}, u32[]{:S(2)}) collective-permute-start(bf16[1,4,256,128]{3,2,1,0:T(8,128)(2,1)S(1)} %maximum_bitcast_fusion), channel_id=1, source_target_pairs={{0,8},{4,12},{8,0},{12,4},{16,24},{20,28},{24,16},{28,20},{1,9},{5... | collective-permute-start | bytes 786440 | tf_op jit(solution)/shard_map/ppermute | solution.py:94
  58.5 15.2 %collective-permute-start.2 = (bf16[256,1024]{1,0:T(8,128)(2,1)}, bf16[256,1024]{1,0:T(8,128)(2,1)}, u32[]{:S(2)}, u32[]{:S(2)}) collective-permute-start(bf16[256,1024]{1,0:T(8,128)(2,1)} %copy-done.37), channel_id=1, source_target_pairs={{0,1},{1,0},{2,3},{3,2},{4,5},{5,4},{6,7},{7,6},{8,9},{9,8},{10,11... | collective-permute-start | bytes 1572872 | tf_op jit(solution)/shard_map/ppermute | solution.py:66
  73.7 29.1 %collective-permute-start.7 = (bf16[256,1024]{1,0:T(8,128)(2,1)S(1)}, bf16[256,1024]{1,0:T(8,128)(2,1)}, u32[]{:S(2)}, u32[]{:S(2)}) collective-permute-start(bf16[256,1024]{1,0:T(8,128)(2,1)S(1)} %copy-done.16), channel_id=1, source_target_pairs={{0,2},{1,3},{2,0},{3,1},{4,6},{5,7},{6,4},{7,5},{8,10},{9,11},{10,... | collective-permute-start | bytes 1572872 | tf_op jit(solution)/shard_map/ppermute | solution.py:66
  76.2 26.6 %collective-permute-start.6 = (bf16[256,1024]{1,0:T(8,128)(2,1)S(1)}, bf16[256,1024]{1,0:T(8,128)(2,1)S(1)}, u32[]{:S(2)}, u32[]{:S(2)}) collective-permute-start(bf16[256,1024]{1,0:T(8,128)(2,1)S(1)} %copy-done.16), channel_id=1, source_target_pairs={{0,1},{1,0},{2,3},{3,2},{4,5},{5,4},{6,7},{7,6},{8,9},{9,8},{10,11... | collective-permute-start | bytes 1572872 | tf_op jit(solution)/shard_map/ppermute | solution.py:66
  85.0 25.4 %collective-permute-start.16 = (bf16[2,4,256,128]{3,2,1,0:T(8,128)(2,1)S(1)}, bf16[2,4,256,128]{3,2,1,0:T(8,128)(2,1)S(1)}, u32[]{:S(2)}, u32[]{:S(2)}) collective-permute-start(bf16[2,4,256,128]{3,2,1,0:T(8,128)(2,1)S(1)} %pad_maximum_fusion.3), channel_id=1, source_target_pairs={{0,16},{4,20},{8,24},{12,28},{16,0},{20,4},{24,8},{28,12},{1,17},{... | collective-permute-start | bytes 1572872 | tf_op jit(solution)/shard_map/ppermute | solution.py:94
  102.8 12.5 %copy-start.12 = (bf16[1024,256]{1,0:T(8,128)(2,1)S(1)}, bf16[1024,256]{1,0:T(8,128)(2,1)}, u32[]{:S(2)}) copy-start(bf16[1024,256]{1,0:T(8,128)(2,1)} %get-tuple-element.87) | copy-start | bytes 1572868
  110.4 19.9 %collective-permute-start.17 = (bf16[4,4,256,128]{3,2,1,0:T(8,128)(2,1)S(1)}, bf16[4,4,256,128]{3,2,1,0:T(8,128)(2,1)S(1)}, u32[]{:S(2)}, u32[]{:S(2)}) collective-permute-start(bf16[4,4,256,128]{3,2,1,0:T(8,128)(2,1)S(1)} %pad_maximum_fusion.1), channel_id=1, source_target_pairs={{0,4},{4,0},{8,12},{12,8},{16,20},{20,16},{24,28},{28,24},{1,5},{5... | collective-permute-start | bytes 3145736 | tf_op jit(solution)/shard_map/ppermute | solution.py:94
  110.5 19.7 %collective-permute-start.8 = (bf16[256,1024]{1,0:T(8,128)(2,1)}, bf16[256,1024]{1,0:T(8,128)(2,1)S(1)}, u32[]{:S(2)}, u32[]{:S(2)}) collective-permute-start(bf16[256,1024]{1,0:T(8,128)(2,1)} %collective-permute-done.7.refs_6_.refs_9_), channel_id=1, source_target_pairs={{0,1},{1,0},{2,3},{3,2},{4,5},{5,4},{6,7},{7,6},{8,9},{9,8},{10,11... | collective-permute-start | bytes 1572872 | tf_op jit(solution)/shard_map/ppermute | solution.py:66
  116.0 15.1 %collective-permute-start.11 = (bf16[256,256]{1,0:T(8,128)(2,1)S(1)}, bf16[256,256]{1,0:T(8,128)(2,1)S(1)}, u32[]{:S(2)}, u32[]{:S(2)}) collective-permute-start(bf16[256,256]{1,0:T(8,128)(2,1)S(1)} %get-tuple-element.152), channel_id=1, source_target_pairs={{0,3},{1,2},{2,1},{3,0},{4,7},{5,6},{6,5},{7,4},{8,11},{9,10},{10,... | collective-permute-start | bytes 393224 | tf_op jit(solution)/shard_map/ppermute | solution.py:66
  116.0 15.1 %collective-permute-start.10 = (bf16[256,256]{1,0:T(8,128)(2,1)S(1)}, bf16[256,256]{1,0:T(8,128)(2,1)S(1)}, u32[]{:S(2)}, u32[]{:S(2)}) collective-permute-start(bf16[256,256]{1,0:T(8,128)(2,1)S(1)} %get-tuple-element.153), channel_id=1, source_target_pairs={{0,2},{1,3},{2,0},{3,1},{4,6},{5,7},{6,4},{7,5},{8,10},{9,11},{10,... | collective-permute-start | bytes 393224 | tf_op jit(solution)/shard_map/ppermute | solution.py:66
  118.9 14.6 %collective-permute-start.9 = (bf16[256,256]{1,0:T(8,128)(2,1)S(1)}, bf16[256,256]{1,0:T(8,128)(2,1)S(1)}, u32[]{:S(2)}, u32[]{:S(2)}) collective-permute-start(bf16[256,256]{1,0:T(8,128)(2,1)S(1)} %get-tuple-element.154), channel_id=1, source_target_pairs={{0,1},{1,0},{2,3},{3,2},{4,5},{5,4},{6,7},{7,6},{8,9},{9,8},{10,11... | collective-permute-start | bytes 393224 | tf_op jit(solution)/shard_map/ppermute | solution.py:66
  138.0 23.3 %collective-permute-start.19 = (bf16[256,1024]{1,0:T(8,128)(2,1)}, bf16[256,1024]{1,0:T(8,128)(2,1)S(1)}, u32[]{:S(2)}, u32[]{:S(2)}) collective-permute-start(bf16[256,1024]{1,0:T(8,128)(2,1)} %get-tuple-element.96.refs_0_.refs_3_), channel_id=1, source_target_pairs={{0,2},{1,3},{2,0},{3,1},{4,6},{5,7},{6,4},{7,5},{8,10},{9,11},{10,... | collective-permute-start | bytes 1572872 | tf_op jit(solution)/shard_map/ppermute | solution.py:66
  138.7 24.3 %collective-permute-start.18 = (bf16[256,1024]{1,0:T(8,128)(2,1)}, bf16[256,1024]{1,0:T(8,128)(2,1)S(1)}, u32[]{:S(2)}, u32[]{:S(2)}) collective-permute-start(bf16[256,1024]{1,0:T(8,128)(2,1)} %get-tuple-element.96.refs_0_.refs_3_), channel_id=1, source_target_pairs={{0,1},{1,0},{2,3},{3,2},{4,5},{5,4},{6,7},{7,6},{8,9},{9,8},{10,11... | collective-permute-start | bytes 1572872 | tf_op jit(solution)/shard_map/ppermute | solution.py:66
  161.3 16.2 %copy-start.42 = (bf16[256,1024]{1,0:T(8,128)(2,1)}, bf16[256,1024]{1,0:T(8,128)(2,1)S(1)}, u32[]{:S(2)}) copy-start(bf16[256,1024]{1,0:T(8,128)(2,1)S(1)} %collective-permute-done.19.refs_2_.refs_5_) | copy-start | bytes 1572868
  163.0 14.5 %copy-start.43 = (bf16[256,1024]{1,0:T(8,128)(2,1)}, bf16[256,1024]{1,0:T(8,128)(2,1)S(1)}, u32[]{:S(2)}) copy-start(bf16[256,1024]{1,0:T(8,128)(2,1)S(1)} %collective-permute-done.18.refs_1_.refs_4_) | copy-start | bytes 1572868
  163.0 14.5 %collective-permute-start.20 = (bf16[256,1024]{1,0:T(8,128)(2,1)S(1)}, bf16[256,1024]{1,0:T(8,128)(2,1)S(1)}, u32[]{:S(2)}, u32[]{:S(2)}) collective-permute-start(bf16[256,1024]{1,0:T(8,128)(2,1)S(1)} %collective-permute-done.19.refs_2_.refs_5_), channel_id=1, source_target_pairs={{0,1},{1,0},{2,3},{3,2},{4,5},{5,4},{6,7},{7,6},{8,9},{9,8},{10,11... | collective-permute-start | bytes 1572872 | tf_op jit(solution)/shard_map/ppermute | solution.py:66
  231.8 13.6 %copy-start.11 = (bf16[256,1024]{1,0:T(8,128)(2,1)S(1)}, bf16[256,1024]{1,0:T(8,128)(2,1)}, u32[]{:S(2)}) copy-start(bf16[256,1024]{1,0:T(8,128)(2,1)} %get-tuple-element.107) | copy-start | bytes 1572868
  231.8 13.9 %copy-start.45 = (bf16[256,1024]{1,0:T(8,128)(2,1)S(1)}, bf16[256,1024]{1,0:T(8,128)(2,1)}, u32[]{:S(2)}) copy-start(bf16[256,1024]{1,0:T(8,128)(2,1)} %get-tuple-element.115) | copy-start | bytes 1572868
  231.8 13.6 %collective-permute-start.21 = (bf16[256,1024]{1,0:T(8,128)(2,1)}, bf16[256,1024]{1,0:T(8,128)(2,1)S(1)}, u32[]{:S(2)}, u32[]{:S(2)}) collective-permute-start(bf16[256,1024]{1,0:T(8,128)(2,1)} %get-tuple-element.108), channel_id=1, source_target_pairs={{0,1},{1,0},{2,3},{3,2},{4,5},{5,4},{6,7},{7,6},{8,9},{9,8},{10,11... | collective-permute-start | bytes 1572872 | tf_op jit(solution)/shard_map/ppermute | solution.py:66
  245.6 26.6 %collective-permute-start.23 = (bf16[256,1024]{1,0:T(8,128)(2,1)S(1)}, bf16[256,1024]{1,0:T(8,128)(2,1)S(1)}, u32[]{:S(2)}, u32[]{:S(2)}) collective-permute-start(bf16[256,1024]{1,0:T(8,128)(2,1)S(1)} %add_convert_fusion.6), channel_id=1, source_target_pairs={{0,2},{1,3},{2,0},{3,1},{4,6},{5,7},{6,4},{7,5},{8,10},{9,11},{10,... | collective-permute-start | bytes 1572872 | tf_op jit(solution)/shard_map/ppermute | solution.py:66
  245.7 26.5 %collective-permute-start.22 = (bf16[256,1024]{1,0:T(8,128)(2,1)S(1)}, bf16[256,1024]{1,0:T(8,128)(2,1)S(1)}, u32[]{:S(2)}, u32[]{:S(2)}) collective-permute-start(bf16[256,1024]{1,0:T(8,128)(2,1)S(1)} %copy-done.45), channel_id=1, source_target_pairs={{0,1},{1,0},{2,3},{3,2},{4,5},{5,4},{6,7},{7,6},{8,9},{9,8},{10,11... | collective-permute-start | bytes 1572872 | tf_op jit(solution)/shard_map/ppermute | solution.py:66
  278.8 7.4 %collective-permute-start.24 = (bf16[256,256]{1,0:T(8,128)(2,1)S(1)}, bf16[256,256]{1,0:T(8,128)(2,1)S(1)}, u32[]{:S(2)}, u32[]{:S(2)}) collective-permute-start(bf16[256,256]{1,0:T(8,128)(2,1)S(1)} %copy-done.51), channel_id=1, source_target_pairs={{0,1},{1,0},{2,3},{3,2},{4,5},{5,4},{6,7},{7,6},{8,9},{9,8},{10,11... | collective-permute-start | bytes 393224 | tf_op jit(solution)/shard_map/ppermute | solution.py:66
  279.4 10.5 %collective-permute-start.25 = (bf16[256,256]{1,0:T(8,128)(2,1)S(1)}, bf16[256,256]{1,0:T(8,128)(2,1)S(1)}, u32[]{:S(2)}, u32[]{:S(2)}) collective-permute-start(bf16[256,256]{1,0:T(8,128)(2,1)S(1)} %copy-done.50), channel_id=1, source_target_pairs={{0,2},{1,3},{2,0},{3,1},{4,6},{5,7},{6,4},{7,5},{8,10},{9,11},{10,... | collective-permute-start | bytes 393224 | tf_op jit(solution)/shard_map/ppermute | solution.py:66
  282.2 9.8 %collective-permute-start.26 = (bf16[256,256]{1,0:T(8,128)(2,1)S(1)}, bf16[256,256]{1,0:T(8,128)(2,1)S(1)}, u32[]{:S(2)}, u32[]{:S(2)}) collective-permute-start(bf16[256,256]{1,0:T(8,128)(2,1)S(1)} %copy-done.49), channel_id=1, source_target_pairs={{0,3},{1,2},{2,1},{3,0},{4,7},{5,6},{6,5},{7,4},{8,11},{9,10},{10,... | collective-permute-start | bytes 393224 | tf_op jit(solution)/shard_map/ppermute | solution.py:66
  286.2 10.2 %copy-start.3 = (bf16[8,1024,128]{2,1,0:T(8,128)(2,1)S(1)}, bf16[8,1024,128]{2,1,0:T(8,128)(2,1)}, u32[]{:S(2)}) copy-start(bf16[8,1024,128]{2,1,0:T(8,128)(2,1)} %w_output_grad.1) | copy-start | bytes 6291460
  286.2 10.5 %copy-start.46 = (bf16[256,256]{1,0:T(8,128)(2,1)}, bf16[256,256]{1,0:T(8,128)(2,1)S(1)}, u32[]{:S(2)}) copy-start(bf16[256,256]{1,0:T(8,128)(2,1)S(1)} %collective-permute-done.24.refs_1_) | copy-start | bytes 393220
  293.6 2.8 collective-permute-start.29
  293.7 22.8 %collective-permute-start.27 = (bf16[256,1024]{1,0:T(8,128)(2,1)}, bf16[256,1024]{1,0:T(8,128)(2,1)}, u32[]{:S(2)}, u32[]{:S(2)}) collective-permute-start(bf16[256,1024]{1,0:T(8,128)(2,1)} %get-tuple-element.122), channel_id=1, source_target_pairs={{0,1},{1,0},{2,3},{3,2},{4,5},{5,4},{6,7},{7,6},{8,9},{9,8},{10,11... | collective-permute-start | bytes 1572872 | tf_op jit(solution)/shard_map/ppermute | solution.py:66
  293.8 25.8 %collective-permute-start.28 = (bf16[256,1024]{1,0:T(8,128)(2,1)}, bf16[256,1024]{1,0:T(8,128)(2,1)}, u32[]{:S(2)}, u32[]{:S(2)}) collective-permute-start(bf16[256,1024]{1,0:T(8,128)(2,1)} %get-tuple-element.123), channel_id=1, source_target_pairs={{0,1},{1,0},{2,3},{3,2},{4,5},{5,4},{6,7},{7,6},{8,9},{9,8},{10,11... | collective-permute-start | bytes 1572872 | tf_op jit(solution)/shard_map/ppermute | solution.py:66
  298.5 16.7 %collective-permute-start.30 = (bf16[2,1024,128]{2,1,0:T(8,128)(2,1)}, bf16[2,1024,128]{2,1,0:T(8,128)(2,1)}, u32[]{:S(2)}, u32[]{:S(2)}) collective-permute-start(bf16[2,1024,128]{2,1,0:T(8,128)(2,1)} %slice.207), channel_id=1, source_target_pairs={{0,8},{4,12},{8,0},{12,4},{16,24},{20,28},{24,16},{28,20},{1,9},{5... | collective-permute-start | bytes 1572872 | tf_op jit(solution)/shard_map/ppermute | solution.py:100
  299.1 16.2 %copy-start.5 = (bf16[4,1024,128]{2,1,0:T(8,128)(2,1)S(1)}, bf16[4,1024,128]{2,1,0:T(8,128)(2,1)}, u32[]{:S(2)}) copy-start(bf16[4,1024,128]{2,1,0:T(8,128)(2,1)} %copy-done.4) | copy-start | bytes 3145732
  299.1 20.5 %copy-start.9 = (bf16[256,1024]{1,0:T(8,128)(2,1)S(1)}, bf16[256,1024]{1,0:T(8,128)(2,1)}, u32[]{:S(2)}) copy-start(bf16[256,1024]{1,0:T(8,128)(2,1)} %get-tuple-element.110) | copy-start | bytes 1572868
  320.8 23.9 %collective-permute-start.31 = (bf16[256,1024]{1,0:T(8,128)(2,1)S(1)}, bf16[256,1024]{1,0:T(8,128)(2,1)S(1)}, u32[]{:S(2)}, u32[]{:S(2)}) collective-permute-start(bf16[256,1024]{1,0:T(8,128)(2,1)S(1)} %add_convert_fusion.4), channel_id=1, source_target_pairs={{0,2},{1,3},{2,0},{3,1},{4,6},{5,7},{6,4},{7,5},{8,10},{9,11},{10,... | collective-permute-start | bytes 1572872 | tf_op jit(solution)/shard_map/ppermute | solution.py:66
  328.1 22.8 %collective-permute-start.33 = (bf16[256,1024]{1,0:T(8,128)(2,1)}, bf16[256,1024]{1,0:T(8,128)(2,1)S(1)}, u32[]{:S(2)}, u32[]{:S(2)}) collective-permute-start(bf16[256,1024]{1,0:T(8,128)(2,1)} %get-tuple-element.137), channel_id=1, source_target_pairs={{0,1},{1,0},{2,3},{3,2},{4,5},{5,4},{6,7},{7,6},{8,9},{9,8},{10,11... | collective-permute-start | bytes 1572872 | tf_op jit(solution)/shard_map/ppermute | solution.py:66
  333.2 17.7 %copy-start.10 = (bf16[256,1024]{1,0:T(8,128)(2,1)S(1)}, bf16[256,1024]{1,0:T(8,128)(2,1)}, u32[]{:S(2)}) copy-start(bf16[256,1024]{1,0:T(8,128)(2,1)} %get-tuple-element.136) | copy-start | bytes 1572868
  338.6 15.5 %copy-start.41 = (bf16[256,1024]{1,0:T(8,128)(2,1)S(1)}, bf16[256,1024]{1,0:T(8,128)(2,1)}, u32[]{:S(2)}) copy-start(bf16[256,1024]{1,0:T(8,128)(2,1)} %get-tuple-element.135) | copy-start | bytes 1572868
  350.9 16.6 %copy-start.8 = (bf16[8,784,128]{2,1,0:T(8,128)(2,1)S(1)}, bf16[8,784,128]{2,1,0:T(8,128)(2,1)}, u32[]{:S(2)}) copy-start(bf16[8,784,128]{2,1,0:T(8,128)(2,1)} %attn_weight_grads.1) | copy-start | bytes 4816900
  352.7 14.8 %collective-permute-start.35 = (bf16[4,784,128]{2,1,0:T(8,128)(2,1)S(1)}, bf16[4,784,128]{2,1,0:T(8,128)(2,1)S(1)}, u32[]{:S(2)}, u32[]{:S(2)}) collective-permute-start(bf16[4,784,128]{2,1,0:T(8,128)(2,1)S(1)} %slice.175), channel_id=1, source_target_pairs={{0,4},{4,0},{8,12},{12,8},{16,20},{20,16},{24,28},{28,24},{1,5},{5... | collective-permute-start | bytes 2408456 | tf_op jit(solution)/shard_map/ppermute | solution.py:100
  352.8 14.7 %collective-permute-start.40 = (bf16[1,1024,128]{2,1,0:T(8,128)(2,1)S(1)}, bf16[1,1024,128]{2,1,0:T(8,128)(2,1)S(1)}, u32[]{:S(2)}, u32[]{:S(2)}) collective-permute-start(bf16[1,1024,128]{2,1,0:T(8,128)(2,1)S(1)} %slice.216), channel_id=1, source_target_pairs={{0,16},{4,20},{8,24},{12,28},{16,0},{20,4},{24,8},{28,12},{1,17},{... | collective-permute-start | bytes 786440 | tf_op jit(solution)/shard_map/ppermute | solution.py:100
  354.1 14.5 %collective-permute-start.32 = (bf16[256,1024]{1,0:T(8,128)(2,1)S(1)}, bf16[256,1024]{1,0:T(8,128)(2,1)}, u32[]{:S(2)}, u32[]{:S(2)}) collective-permute-start(bf16[256,1024]{1,0:T(8,128)(2,1)S(1)} %copy-done.41), channel_id=1, source_target_pairs={{0,1},{1,0},{2,3},{3,2},{4,5},{5,4},{6,7},{7,6},{8,9},{9,8},{10,11... | collective-permute-start | bytes 1572872 | tf_op jit(solution)/shard_map/ppermute | solution.py:66
  367.8 17.8 %copy-start.6 = (f32[256,1024]{1,0:T(8,128)S(1)}, f32[256,1024]{1,0:T(8,128)}, u32[]{:S(2)}) copy-start(f32[256,1024]{1,0:T(8,128)} %get-tuple-element.95.refs_3_) | copy-start | bytes 3145732
  367.8 17.8 %copy-start.13 = (bf16[256,1024]{1,0:T(8,128)(2,1)S(1)}, bf16[256,1024]{1,0:T(8,128)(2,1)}, u32[]{:S(2)}) copy-start(bf16[256,1024]{1,0:T(8,128)(2,1)} %get-tuple-element.105) | copy-start | bytes 1572868
  369.4 14.0 %collective-permute-start.36 = (bf16[2,784,128]{2,1,0:T(8,128)(2,1)}, bf16[2,784,128]{2,1,0:T(8,128)(2,1)}, u32[]{:S(2)}, u32[]{:S(2)}) collective-permute-start(bf16[2,784,128]{2,1,0:T(8,128)(2,1)} %slice.177), channel_id=1, source_target_pairs={{0,8},{4,12},{8,0},{12,4},{16,24},{20,28},{24,16},{28,20},{1,9},{5... | collective-permute-start | bytes 1204232 | tf_op jit(solution)/shard_map/ppermute | solution.py:100
  371.1 4.9 %collective-permute-start.41 = (bf16[256,128]{1,0:T(8,128)(2,1)}, bf16[256,128]{1,0:T(8,128)(2,1)S(1)}, u32[]{:S(2)}, u32[]{:S(2)}) collective-permute-start(bf16[256,128]{1,0:T(8,128)(2,1)} %get-tuple-element.159), channel_id=1, source_target_pairs={{0,1},{1,0},{2,3},{3,2},{4,5},{5,4},{6,7},{7,6},{8,9},{9,8},{10,11... | collective-permute-start | bytes 196616 | tf_op jit(solution)/shard_map/ppermute | solution.py:66
  372.8 6.6 %collective-permute-start.43 = (bf16[256,128]{1,0:T(8,128)(2,1)S(1)}, bf16[256,128]{1,0:T(8,128)(2,1)S(1)}, u32[]{:S(2)}, u32[]{:S(2)}) collective-permute-start(bf16[256,128]{1,0:T(8,128)(2,1)S(1)} %get-tuple-element.160), channel_id=1, source_target_pairs={{0,3},{1,2},{2,1},{3,0},{4,7},{5,6},{6,5},{7,4},{8,11},{9,10},{10,... | collective-permute-start | bytes 196616 | tf_op jit(solution)/shard_map/ppermute | solution.py:66
  373.3 6.2 %collective-permute-start.42 = (bf16[256,128]{1,0:T(8,128)(2,1)S(1)}, bf16[256,128]{1,0:T(8,128)(2,1)S(1)}, u32[]{:S(2)}, u32[]{:S(2)}) collective-permute-start(bf16[256,128]{1,0:T(8,128)(2,1)S(1)} %get-tuple-element.161), channel_id=1, source_target_pairs={{0,2},{1,3},{2,0},{3,1},{4,6},{5,7},{6,4},{7,5},{8,10},{9,11},{10,... | collective-permute-start | bytes 196616 | tf_op jit(solution)/shard_map/ppermute | solution.py:66
  380.2 23.3 %collective-permute-start.34 = (bf16[256,1024]{1,0:T(8,128)(2,1)S(1)}, bf16[256,1024]{1,0:T(8,128)(2,1)S(1)}, u32[]{:S(2)}, u32[]{:S(2)}) collective-permute-start(bf16[256,1024]{1,0:T(8,128)(2,1)S(1)} %add_convert_fusion.2), channel_id=1, source_target_pairs={{0,2},{1,3},{2,0},{3,1},{4,6},{5,7},{6,4},{7,5},{8,10},{9,11},{10,... | collective-permute-start | bytes 1572872 | tf_op jit(solution)/shard_map/ppermute | solution.py:66
  384.6 23.1 %collective-permute-start.37 = (bf16[1,784,128]{2,1,0:T(8,128)(2,1)S(1)}, bf16[1,784,128]{2,1,0:T(8,128)(2,1)S(1)}, u32[]{:S(2)}, u32[]{:S(2)}) collective-permute-start(bf16[1,784,128]{2,1,0:T(8,128)(2,1)S(1)} %slice.209), channel_id=1, source_target_pairs={{0,16},{4,20},{8,24},{12,28},{16,0},{20,4},{24,8},{28,12},{1,17},{... | collective-permute-start | bytes 602120 | tf_op jit(solution)/shard_map/ppermute | solution.py:100
  407.8 5.1 %collective-permute-start.38 = (f32[8,128]{1,0:T(8,128)S(1)}, f32[8,128]{1,0:T(8,128)S(1)}, u32[]{:S(2)}, u32[]{:S(2)}) collective-permute-start(f32[8,128]{1,0:T(8,128)S(1)} %slice_bitcast_fusion.4), channel_id=1, source_target_pairs={{0,1},{1,0},{2,3},{3,2},{4,5},{5,4},{6,7},{7,6},{8,9},{9,8},{10,11... | collective-permute-start | bytes 12296 | tf_op jit(solution)/shard_map/ppermute | solution.py:66
  412.9 4.9 %collective-permute-start.39 = (f32[8,128]{1,0:T(8,128)S(1)}, f32[8,128]{1,0:T(8,128)S(1)}, u32[]{:S(2)}, u32[]{:S(2)}) collective-permute-start(f32[8,128]{1,0:T(8,128)S(1)} %fusion.12), channel_id=1, source_target_pairs={{0,2},{1,3},{2,0},{3,1},{4,6},{5,7},{6,4},{7,5},{8,10},{9,11},{10,... | collective-permute-start | bytes 12296 | tf_op jit(solution)/shard_map/ppermute | solution.py:66
  (34 other events, 133.4 us)
Sparse Core Ops, SparseCore 0:
  10.6 107.9 all-gather.2
  278.0 129.7 reduce-scatter.1
